TPU v7x, 128 devices: a whole 4x4x4 slice. The times are simulated.
128 devices in a mesh: dp: 8 (over z_lo, y), chan: 16 (over x, z_hi, core).
Axes of the slice: x: 4, y: 4, z: 4 (z_hi: 2, z_lo: 2; z = z_hi * 2 + z_lo), core: 2. Of those that a mesh axis runs over, the one named last changes fastest.
Arguments:
- hidden_in: bfloat16 [8192, 8192], P('dp'), may hold values from -6 to 6
- proj_weight: bfloat16 [8192, 8192], P('dp', 'chan'), may hold values from -0.09375 to 0.09375
- embed: bfloat16 [8192, 8192], P('dp', 'chan')
- embed_grad: bfloat16 [8192, 8192], P('dp', 'chan')
- eigvec: float32 [8192, 512], P('chan'), as said below
- eigval: float32 [8192], P('chan'), as said below
Outputs:
- grad_weight: bfloat16 [8192, 8192], P('dp', 'chan')
- grad_hidden: bfloat16 [8192, 8192], P('dp', 'chan')
Inputs may be any that keep to these rules, and one draw needn't show every extreme that they name: `eigvec`: each group's block of 512 consecutive rows is an orthogonal matrix whose columns are that group's saved eigenvectors. `eigval`: each group's 512 saved eigenvalues are positive and any two of them differ by at least one percent of the larger.
All inputs are finite; a program needn't handle non-finite values.
Results may differ from a plain program's by a relative error of at most 0.005.
Values may be sent and summed in bfloat16 or wider, within the bound.
No kernel may reach another device: no remote copies, remote signals or barrier semaphores. Data moves between devices by JAX's collectives and lax.ppermute only.
A program may use at most 192 MiB of HBM per device.

v0:
```python
import jax
import jax.numpy as jnp
from jax import lax
from jax.sharding import PartitionSpec as P

HI = lax.Precision.HIGHEST


def local(hidden_in, proj_weight, embed, embed_grad, eigvec, eigval):
    rows = embed.shape[0] * lax.axis_size("dp")
    zlocal = embed.astype(jnp.float32)
    glocal = embed_grad.astype(jnp.float32)
    sums_z, sums_g = lax.psum((jnp.sum(zlocal, axis=0), jnp.sum(glocal, axis=0)), "dp")
    mean_z = sums_z / rows
    mean_g = sums_g / rows
    centered = zlocal - mean_z
    local_moment = jnp.dot(centered.T, glocal, precision=HI, preferred_element_type=jnp.float32)
    dmat = lax.psum(local_moment, "dp")
    sym = 0.5 * (dmat + dmat.T)
    root = jnp.sqrt(eigval)
    whiten = jnp.dot(
        eigvec / root[None, :], eigvec.T, precision=HI, preferred_element_type=jnp.float32
    )
    loewner = -1.0 / (root[:, None] * root[None, :] * (root[:, None] + root[None, :]))
    half_rot = jnp.dot(eigvec.T, sym, precision=HI, preferred_element_type=jnp.float32)
    rotated = jnp.dot(half_rot, eigvec, precision=HI, preferred_element_type=jnp.float32)
    half_back = jnp.dot(eigvec, loewner * rotated, precision=HI, preferred_element_type=jnp.float32)
    dsigma = jnp.dot(half_back, eigvec.T, precision=HI, preferred_element_type=jnp.float32)
    first = jnp.dot(glocal - mean_g, whiten, precision=HI, preferred_element_type=jnp.float32)
    second = jnp.dot(centered, dsigma, precision=HI, preferred_element_type=jnp.float32)
    grad_z = (first + 2.0 / rows * second).astype(jnp.bfloat16)
    grad_weight = lax.psum_scatter(
        lax.dot_general(
            hidden_in, grad_z, (((0,), (0,)), ((), ())), preferred_element_type=jnp.float32
        ),
        "dp",
        scatter_dimension=0,
        tiled=True,
    ).astype(jnp.bfloat16)
    partial_input = lax.dot_general(
        grad_z,
        lax.all_gather(proj_weight, "dp", axis=0, tiled=True),
        (((1,), (1,)), ((), ())),
        preferred_element_type=jnp.float32,
    )
    grad_hidden = lax.psum_scatter(partial_input, "chan", scatter_dimension=1, tiled=True).astype(
        jnp.bfloat16
    )
    return (grad_weight, grad_hidden)


def solution(mesh):
    in_specs = (
        P("dp", None),
        P("dp", "chan"),
        P("dp", "chan"),
        P("dp", "chan"),
        P("chan", None),
        P("chan"),
    )
    out_specs = (P("dp", "chan"), P("dp", "chan"))
    return jax.shard_map(local, mesh=mesh, in_specs=in_specs, out_specs=out_specs, check_vma=False)
```

profile of v0, /device:TPU:2, one launch (start us, length us, event | category | flops | bytes accessed | tf_op | source)
XLA Modules:
  0.0 632.4 jit_solution(18423183222383326655)
XLA Ops:
  7.2 0.0 copy-start.2
  7.2 0.0 copy-start.1
  7.2 0.0 all-reduce.3.cloned.1.call-start
  7.2 2.0 convert_reduce_fusion
  9.2 20.3 %all-reduce = (f32[512]{0:T(512)S(1)}, f32[512]{0:T(512)S(1)}) all-reduce(f32[512]{0:T(512)S(1)} %get-tuple-element.6, f32[512]{0:T(512)S(1)} %get-tuple-element.7), channel_id=1, replica_groups=mesh['dp'=8,'chan'=16] {'dp'}, use_global_device_ids=true, to_apply=%region_3.0 | all-reduce | flops 1024 | bytes 8192 | tf_op jit(solution)/shard_map/psum | solution.py:13
  29.6 2.8 fusion.1
  32.4 0.0 all-reduce.3.cloned.1.call-update
  32.4 0.0 all-gather.2.cloned.1.call-start
  32.5 0.7 all-gather.2.cloned.1.call-update
  33.2 0.2 reduce-scatter.3.cloned.1.call-start
  33.4 0.2 copy-done
  33.6 2.8 fusion.3
  36.5 72.6 %all-reduce.3.cloned.1.call-done = f32[512,512]{1,0:T(8,128)} async-done(((f32[512,512]{1,0:T(8,128)}), f32[512,512]{1,0:T(8,128)}) %all-reduce.3.cloned.1.call-update) | async-done | bytes 1048592 | tf_op jit(solution)/shard_map/psum | solution.py:18
  109.0 2.5 copy.8
  111.6 3.5 fusion.6
  115.0 2.0 convolution_multiply_fusion
  117.0 3.5 fusion.14
  120.5 3.7 fusion.15
  124.2 0.0 copy-start.3
  124.2 3.5 fusion
  127.7 3.6 add_convert_fusion
  131.3 15.8 %convolution_bitcast_fusion = f32[8192,512]{0,1:T(8,128)} fusion(bf16[1024,512]{1,0:T(8,128)(2,1)S(1)} %add_convert_fusion, bf16[1024,8192]{1,0:T(8,128)(2,1)} %param.6), kind=kOutput, calls=%fused_computation | convolution fusion | flops 8589934592 | bytes 34603008 | tf_op jit(solution)/shard_map/dot_general | solution.py:33
  147.1 0.0 reduce-scatter.3.cloned.1.call-update
  147.2 0.3 reduce-scatter.5.cloned.1.call-start
  147.5 54.7 %all-gather.2.cloned.1.call-done = bf16[8192,512]{1,0:T(8,128)(2,1)} async-done(((bf16[1024,512]{1,0:T(8,128)(2,1)}), bf16[8192,512]{1,0:T(8,128)(2,1)}) %all-gather.2.cloned.1.call-update) | async-done | bytes 8388624 | tf_op jit(solution)/shard_map/all_gather | solution.py:42
  202.2 18.1 %fusion.16 = f32[1024,8192]{1,0:T(8,128)} fusion(bf16[1024,512]{1,0:T(8,128)(2,1)S(1)} %add_convert_fusion, bf16[8192,512]{1,0:T(8,128)(2,1)} %all-gather.2.cloned.1.call-done), kind=kOutput, calls=%fused_computation.25 | convolution fusion | flops 8589934592 | bytes 42991616 | tf_op jit(solution)/shard_map/dot_general | solution.py:40
  220.3 0.0 reduce-scatter.5.cloned.1.call-update
  220.4 154.5 %reduce-scatter.3.cloned.1.call-done = f32[1024,512]{0,1:T(8,128)} async-done(((f32[8192,512]{0,1:T(8,128)}), f32[1024,512]{0,1:T(8,128)}) %reduce-scatter.3.cloned.1.call-update) | async-done | bytes 2097168 | tf_op jit(solution)/shard_map/reduce_scatter | solution.py:32
  374.8 1.7 convert_element_type.18
  376.6 1.3 copy.9
  377.9 245.3 %reduce-scatter.5.cloned.1.call-done = f32[1024,512]{1,0:T(8,128)} async-done(((f32[1024,8192]{1,0:T(8,128)}), f32[1024,512]{1,0:T(8,128)}) %reduce-scatter.5.cloned.1.call-update) | async-done | bytes 2097168 | tf_op jit(solution)/shard_map/reduce_scatter | solution.py:46
  623.2 2.7 convert_element_type.19
  (9 shorter events, 0.0 us)
Async XLA Ops:
  7.2 22.4 %copy-start.2 = (bf16[1024,512]{1,0:T(8,128)(2,1)S(1)}, bf16[1024,512]{1,0:T(8,128)(2,1)}, u32[]{:S(2)}) copy-start(bf16[1024,512]{1,0:T(8,128)(2,1)} %param.8) | copy-start | bytes 3145732
  7.2 22.4 %copy-start.1 = (bf16[1024,512]{1,0:T(8,128)(2,1)S(1)}, bf16[1024,512]{1,0:T(8,128)(2,1)}, u32[]{:S(2)}) copy-start(bf16[1024,512]{1,0:T(8,128)(2,1)} %param.9) | copy-start | bytes 3145732
  7.2 101.8 %all-reduce.3.cloned.1.call-start = ((), (), s32[]{:S(2)}) async-start(), calls=%async_computation.2 | async-start | bytes 2097152 | tf_op jit(solution)/shard_map/psum | solution.py:18
  32.4 1.0 copy-start.4
  32.4 1.2 copy-start
  32.4 169.8 %all-gather.2.cloned.1.call-start = ((), (), s32[]{:S(2)}) async-start(), calls=%async_computation.4 | async-start | bytes 9437184 | tf_op jit(solution)/shard_map/all_gather | solution.py:42
  33.2 341.7 %reduce-scatter.3.cloned.1.call-start = ((), (), s32[]{:S(2)}) async-start(), calls=%async_computation.3 | async-start | bytes 18874368 | tf_op jit(solution)/shard_map/reduce_scatter | solution.py:32
  124.2 3.5 copy-start.3
  147.2 476.0 %reduce-scatter.5.cloned.1.call-start = ((), (), s32[]{:S(2)}) async-start(), calls=%async_computation.5 | async-start | bytes 35651584 | tf_op jit(solution)/shard_map/reduce_scatter | solution.py:46
Sparse Core Ops, SparseCore 0:
  32.5 76.4 all-reduce.2
  110.7 91.5 all-gather.1
  204.7 170.0 reduce-scatter.2
  379.1 244.0 reduce-scatter.4
where the time goes:
time: 634 us; the launch traced here: 632 us
  waiting for transfers between devices  528 us (83%)
  matrix products  59.3 us (9%)
  blocking collectives  20.3 us (3%)
  between operations  13.9 us (2%)
  other arithmetic  6.47 us (1%)
    reduce_scatter x1, waiting for transfers between devices, local(): lax.psum_scatter(partial_input, 'chan', scatter_dimension=1, tiled=True)  245 us
    reduce_scatter x1, waiting for transfers between devices, local(): lax.psum_scatter(lax.dot_general(hidden_in, grad_z, (((0,), (0,)), ((), (...  154 us
    psum x1, waiting for transfers between devices, local(): dmat = lax.psum(local_moment, 'dp')  72.6 us
    all_gather x1, waiting for transfers between devices, local(): lax.all_gather(proj_weight, 'dp', axis=0, tiled=True)  54.7 us
    psum x1, blocking collectives, local(): lax.psum((jnp.sum(zlocal, axis=0), jnp.sum(glocal, axis=0)), 'dp')  20.3 us
    dot_general x1, matrix products, local(): lax.dot_general(grad_z, lax.all_gather(proj_weight, 'dp', axis=0, tiled=T...  18.1 us
    dot_general x1, matrix products, local(): lax.dot_general(hidden_in, grad_z, (((0,), (0,)), ((), ())), preferred_el...  15.8 us
  transfers between devices with their start and end apart: 4, of which 4 were waited for; matrix products, arithmetic and copies ran while one was open for 10% of the time, Pallas kernels for 0%

commit v1 on v0

v1 whole, which is shorter than its diff:
```python
import functools

import jax
import jax.numpy as jnp
from jax import lax
from jax.experimental import pallas as pl
from jax.experimental.pallas import tpu as pltpu
from jax.sharding import PartitionSpec as P

F32 = jnp.float32
BF16 = jnp.bfloat16
AXES = ("dp", "chan")


def place_of(index):
    dp, chan = divmod(index, 16)
    zlo, y = divmod(dp, 4)
    x, rest = divmod(chan, 4)
    zhi, core = divmod(rest, 2)
    return x, y, zhi * 2 + zlo, core


def index_of(x, y, z, core):
    zhi, zlo = divmod(z % 4, 2)
    return (zlo * 4 + y % 4) * 16 + ((x % 4) * 2 + zhi) * 2 + core


def mover(step):
    pairs = [(i, index_of(*step(*place_of(i)))) for i in range(128)]
    return lambda a: lax.ppermute(a, AXES, pairs)


x_up = mover(lambda x, y, z, k: (x + 1, y, z, k))
x_down = mover(lambda x, y, z, k: (x - 1, y, z, k))
y_up = mover(lambda x, y, z, k: (x, y + 1, z, k))
y_down = mover(lambda x, y, z, k: (x, y - 1, z, k))
z_up = mover(lambda x, y, z, k: (x, y, z + 1, k))
z_down = mover(lambda x, y, z, k: (x, y, z - 1, k))
z_flip = [None] + [mover(lambda x, y, z, k, j=j: (x, y, z ^ j, k)) for j in (1, 2, 3)]
swap = mover(lambda x, y, z, k: (x, y, z, 1 - k))


def bf(a):
    return a.astype(BF16)


def tie(*arrays):
    return lax.optimization_barrier(arrays)


def halves(a):
    head = bf(a)
    return head, bf(a - head.astype(F32))


def dot(a, b, ca, cb):
    return lax.dot_general(a, b, (((ca,), (cb,)), ((), ())), preferred_element_type=F32)


def dot3(a, b, ca, cb):
    (ah, al), (bh, bl) = halves(a), halves(b)
    return dot(ah, bh, ca, cb) + (dot(ah, bl, ca, cb) + dot(al, bh, ca, cb))


def hbm(*arrays):
    return [pltpu.with_memory_space_constraint(a, pltpu.HBM) for a in arrays]


def params(mib):
    return pltpu.CompilerParams(vmem_limit_bytes=mib * 2**20)


def cost(flops, nbytes):
    return pl.CostEstimate(flops=int(flops), bytes_accessed=int(nbytes), transcendentals=0)


def moments_kernel(z_ref, g_ref, u_ref, out_ref):
    n_loc, ch = z_ref.shape
    q = ch // 4
    z, g = z_ref[...], g_ref[...]
    sum_z = jnp.sum(z.astype(F32), axis=0, keepdims=True)
    sum_g = jnp.sum(g.astype(F32), axis=0, keepdims=True)
    zero = jnp.zeros((7, ch), F32)
    outer = dot3(jnp.concatenate([sum_z * (1.0 / n_loc), zero]), jnp.concatenate([sum_g, zero]), 0, 0)
    part = dot(z, g, 0, 0) - outer
    sym = 0.5 * (part + part.T)
    u = u_ref[...]
    rotated = dot3(dot3(u, sym, 0, 0), u, 1, 0)
    sums = jnp.concatenate([sum_z, sum_g])
    parts = []
    for _ in range(3):
        head = bf(sums).astype(F32)
        parts.append(head)
        sums = sums - head
    small = bf(jnp.concatenate(parts + [jnp.zeros((10, ch), F32)]))
    for r in range(4):
        out_ref[r, :q, :] = bf(rotated[r * q : (r + 1) * q])
        out_ref[r, q:, :] = small


def moments(embed, embed_grad, eigvec):
    n_loc, ch = embed.shape
    return pl.pallas_call(
        moments_kernel,
        out_shape=pltpu.HBM((4, ch // 4 + 16, ch), BF16),
        compiler_params=params(20),
        cost_estimate=cost(2 * n_loc * ch * ch + 12 * ch**3, 4 * n_loc * ch + 6 * ch * ch),
    )(*hbm(embed, embed_grad, eigvec))


def quarter_kernel(got_ref, quarter_ref, sent_ref):
    q = quarter_ref.shape[0]
    total = sum(got_ref[r, :q, :].astype(F32) for r in range(4))
    quarter_ref[...] = total
    sent_ref[:q, :] = bf(total)
    for r in range(4):
        sent_ref[q + 16 * r : q + 16 * (r + 1), :] = got_ref[r, q:, :]


def inner_kernel(y_ref, quarter_ref, sent_ref, other_ref, u_ref, uq_ref, root_ref, rootq_ref, inner_ref, mean_ref, *, n_loc):
    q, ch = quarter_ref.shape
    first, second = [], []
    for ref in (sent_ref, other_ref):
        small = ref[q:, :].astype(F32)
        for r in range(4):
            block = small[16 * r : 16 * r + 16]
            both = block[0:2] + block[2:4] + block[4:6]
            first.append(both[0:1])
            second.append(both[1:2])
    sum_z, sum_g = jnp.concatenate(first), jnp.concatenate(second)
    mean_z = jnp.sum(sum_z, axis=0, keepdims=True) * (1.0 / (8 * n_loc))
    mean_g = jnp.sum(sum_g, axis=0, keepdims=True) * (1.0 / (8 * n_loc))
    dev_z = sum_z - n_loc * mean_z
    dev_g = sum_g * (1.0 / n_loc)
    turned = dot3(jnp.concatenate([dev_g, dev_z]), u_ref[...], 1, 0)
    turned_q = dot3(jnp.concatenate([dev_z, dev_g]), uq_ref[...], 1, 0)
    total = quarter_ref[...] + other_ref[:q, :].astype(F32) + 0.5 * dot3(turned_q, turned, 0, 0)
    root, rootq = root_ref[...], rootq_ref[...]
    inner = bf(total * (-1.0 / (rootq * root * (rootq + root))))
    for r in range(4):
        inner_ref[r] = inner
    mean_ref[...] = jnp.concatenate([mean_z, mean_g, jnp.zeros((6, ch), F32)])


def quarter_terms(got):
    ch = got.shape[2]
    q = ch // 4
    return pl.pallas_call(
        quarter_kernel,
        out_shape=(pltpu.HBM((q, ch), F32), pltpu.HBM((q + 64, ch), BF16)),
        compiler_params=params(8),
    )(*hbm(got))


def inner_terms(quarter, sent, other, eigvec, root, y, n_loc):
    q, ch = quarter.shape
    full = lambda *shape: pl.BlockSpec(shape, lambda i, y: (0,) * len(shape))
    return pl.pallas_call(
        functools.partial(inner_kernel, n_loc=n_loc),
        out_shape=(pltpu.HBM((4, q, ch), BF16), pltpu.HBM((8, ch), F32)),
        grid_spec=pltpu.PrefetchScalarGridSpec(
            num_scalar_prefetch=1,
            grid=(1,),
            in_specs=[
                full(q, ch),
                full(q + 64, ch),
                full(q + 64, ch),
                full(ch, ch),
                pl.BlockSpec((ch, q), lambda i, y: (0, y[0])),
                full(1, ch),
                pl.BlockSpec((q, 1), lambda i, y: (y[0], 0)),
            ],
            out_specs=(full(4, q, ch), full(8, ch)),
        ),
        compiler_params=params(16),
    )(y.reshape(1), *hbm(quarter, sent, other, eigvec, eigvec), root[None, :], root[:, None])


def first_kernel(u_ref, root_ref, g_ref, wsum_ref, first_ref):
    u = u_ref[...]
    whiten = dot3(u / root_ref[...], u, 1, 1)
    wh, wl = halves(whiten)
    wsum_ref[...] = wh.astype(F32) + wl.astype(F32)
    g = g_ref[...]
    first_ref[...] = dot(g, wh, 1, 0) + dot(g, wl, 1, 0)


def first_terms(eigvec, root, embed_grad):
    n_loc, ch = embed_grad.shape
    return pl.pallas_call(
        first_kernel,
        out_shape=(pltpu.HBM((ch, ch), F32), pltpu.HBM((n_loc, ch), F32)),
        compiler_params=params(14),
        cost_estimate=cost(6 * ch**3 + 4 * n_loc * ch * ch, 6 * n_loc * ch + 8 * ch * ch),
    )(*hbm(eigvec), root[None, :], *hbm(embed_grad))


def grad_z_kernel(u_ref, inner_ref, z_ref, first_ref, wsum_ref, mean_ref, out_ref, turned_ref, *, scale):
    u, inner = u_ref[...], inner_ref[...]
    uh, ul = halves(u)
    back = dot(uh, inner, 1, 0) + dot(ul, inner, 1, 0)
    dsigma = dot3(back, u, 1, 1) * scale
    dh, dl = halves(dsigma)
    mean = mean_ref[...]
    bias = dot3(mean, wsum_ref[...], 1, 0)[1:2] + dot3(mean, dh.astype(F32) + dl.astype(F32), 1, 0)[0:1]
    z = z_ref[...]
    out = first_ref[...] + dot(z, dh, 1, 0) + dot(z, dl, 1, 0) - bias
    out_ref[...] = bf(out)
    turned_ref[...] = bf(out.T)


def grad_z_of(eigvec, inner, embed, first, wsum, means, rows):
    n_loc, ch = embed.shape
    return pl.pallas_call(
        functools.partial(grad_z_kernel, scale=2.0 / rows),
        out_shape=(pltpu.HBM((n_loc, ch), BF16), pltpu.HBM((ch, n_loc), BF16)),
        compiler_params=params(20),
        cost_estimate=cost(10 * ch**3 + 4 * n_loc * ch * ch, 8 * n_loc * ch + 10 * ch * ch),
    )(*hbm(eigvec, inner, embed, first, wsum), means)


def ring_shapes(rows, cols):
    half = rows // 2
    return (
        pltpu.HBM((rows, cols), BF16),
        pltpu.HBM((rows, cols), BF16),
        pltpu.HBM((rows, cols), F32),
        pltpu.HBM((half, cols), F32),
        pltpu.HBM((half, cols), F32),
    )


def ring_store(r, start, acc, up_ref, down_ref, b0_ref, b1_ref, b3_ref, cols=slice(None)):
    size, half = acc.shape[0], b1_ref.shape[0]
    lower = start < half
    at = pl.ds(start % half, size)
    later = pl.ds(half + start % half, size)

    @pl.when(r == 0)
    def _():
        b0_ref[pl.ds(start, size), cols] = acc

    @pl.when(r == 1)
    def _():
        if lower:
            b1_ref[at, cols] = acc
        else:
            up_ref[at, cols] = bf(acc)

    @pl.when(r == 2)
    def _():
        if lower:
            up_ref[later, cols] = bf(acc)
        else:
            down_ref[at, cols] = bf(acc)

    @pl.when(r == 3)
    def _():
        if lower:
            down_ref[later, cols] = bf(acc)
        else:
            b3_ref[at, cols] = acc


def order_kernel(idx_ref, own_ref, right_ref, two_a_ref, two_b_ref, left_ref, out_ref, sems):
    fs = own_ref.shape[2]
    for g in range(8):
        place, side = idx_ref[g] // 2, idx_ref[g] % 2
        to, sem = out_ref.at[:, g * fs : (g + 1) * fs], sems.at[g]
        for n, ref in ((0, own_ref), (1, right_ref), (3, left_ref)):

            @pl.when(place == n)
            def _():
                pltpu.make_async_copy(ref.at[side], to, sem).start()

        for n, ref in ((0, two_a_ref), (1, two_b_ref)):

            @pl.when((place == 2) & (side == n))
            def _():
                pltpu.make_async_copy(ref.at[0], to, sem).start()

    for g in range(8):
        to, sem = out_ref.at[:, g * fs : (g + 1) * fs], sems.at[g]
        pltpu.make_async_copy(own_ref.at[0], to, sem).wait()


def in_order(sources, order):
    _, depth, fs = sources[0].shape
    return pl.pallas_call(
        order_kernel,
        out_shape=jax.ShapeDtypeStruct((depth, 8 * fs), BF16),
        in_specs=[pl.BlockSpec(memory_space=pltpu.SMEM)] + [pl.BlockSpec(memory_space=pl.ANY)] * 5,
        out_specs=pl.BlockSpec(memory_space=pl.ANY),
        scratch_shapes=[pltpu.SemaphoreType.DMA((8,))],
        compiler_params=params(4),
    )(order, *sources)


def stack_kernel(*refs):
    *sources, out_ref = refs
    at = 0
    for ref in sources:
        out_ref[at : at + ref.shape[0], :] = ref[...]
        at += ref.shape[0]


def stacked(sources):
    rows = sum(a.shape[0] for a in sources)
    return pl.pallas_call(
        stack_kernel,
        out_shape=pltpu.HBM((rows, sources[0].shape[1]), BF16),
        compiler_params=params(12),
    )(*sources)


def halves_kernel(core_ref, keep_in, give_in, keep_ref, give_ref):
    keep_ref[...] = bf(keep_in[...].astype(F32).T)
    give_ref[...] = bf(give_in[...].astype(F32).T)


def turned_halves(weight, core):
    rows, ch = weight.shape
    half = rows // 2
    shape = jax.ShapeDtypeStruct((ch, half), BF16)
    return pl.pallas_call(
        halves_kernel,
        out_shape=(shape, shape),
        grid_spec=pltpu.PrefetchScalarGridSpec(
            num_scalar_prefetch=1,
            grid=(1,),
            in_specs=[
                pl.BlockSpec((half, ch), lambda i, c: (c[0], 0)),
                pl.BlockSpec((half, ch), lambda i, c: (1 - c[0], 0)),
            ],
            out_specs=tuple(pl.BlockSpec((ch, half), lambda i, c: (0, 0)) for _ in range(2)),
        ),
        compiler_params=params(12),
    )(core.reshape(1), weight, weight)


def hidden_kernel(*refs):
    *lhs, w_ref, out_ref = refs
    _, rows, wide = out_ref.shape
    tile = rows // 2
    for start in range(0, rows, tile):
        acc, k0 = None, 0
        for ref in lhs:
            depth = ref.shape[1]
            term = dot(ref[start : start + tile, :], w_ref[k0 : k0 + depth, :], 1, 0)
            acc = term if acc is None else acc + term
            k0 += depth
        for r in range(4):
            out_ref[r, start : start + tile, :] = bf(acc[:, r * wide : (r + 1) * wide])


def hidden_terms(pieces, w_all):
    rows = pieces[0].shape[0]
    depth, wide = w_all.shape
    return pl.pallas_call(
        hidden_kernel,
        out_shape=pltpu.HBM((4, rows, wide // 4), BF16),
        compiler_params=params(20),
        cost_estimate=cost(2 * rows * wide * depth, 2 * (rows + wide) * depth + 2 * rows * wide),
    )(*pieces, w_all)


def here_kernel(idx_ref, p_ref, own_ref, out_ref):
    out_ref[...] = dot(p_ref[...], own_ref[...], 1, 0)


def weight_here(turned, hidden, order):
    ch, n_loc = turned.shape
    feat = hidden.shape[1] // 8
    return pl.pallas_call(
        here_kernel,
        out_shape=pltpu.HBM((ch, 4 * feat), F32),
        grid_spec=pltpu.PrefetchScalarGridSpec(
            num_scalar_prefetch=1,
            grid=(4,),
            in_specs=[
                pl.BlockSpec((ch, n_loc), lambda r, idx: (0, 0)),
                pl.BlockSpec((n_loc, feat), lambda r, idx: (0, idx[r])),
            ],
            out_specs=pl.BlockSpec((ch, feat), lambda r, idx: (0, r)),
        ),
        compiler_params=params(14),
        cost_estimate=cost(8 * ch * n_loc * feat, 8 * feat * (n_loc + 2 * ch)),
    )(order, *hbm(turned, hidden))


def weight_kernel(idx_ref, q_ref, own_ref, hx_ref, hk_ref, up_ref, down_ref, b0_ref, b1_ref, b3_ref, turned_ref):
    r = pl.program_id(0)
    core, x = idx_ref[4], idx_ref[5]
    half = hx_ref.shape[0]
    h = b1_ref.shape[0]
    sub = half // 4

    @pl.when(r == 0)
    def _():
        for n in range(8):
            k = core if n < 4 else 1 - core
            row = pl.multiple_of((k * 4 + (x + n) % 4) * sub, sub)
            turned_ref[:, n * sub : (n + 1) * sub] = bf(q_ref[pl.ds(row, sub), :].astype(F32).T)

    acc = own_ref[...] + dot(turned_ref[:, :half], hx_ref[...], 1, 0) + dot(turned_ref[:, half:], hk_ref[...], 1, 0)
    for start in (0, h):
        ring_store(r, start, acc[start : start + h], up_ref, down_ref, b0_ref, b1_ref, b3_ref)


def weight_terms(q_own, w_here, h_x, h_k, order):
    n_loc, ch = q_own.shape
    feat = h_x.shape[1] // 4
    shapes = ring_shapes(ch, feat)
    whole = lambda a: pl.BlockSpec(a.shape, lambda r, idx: (0, 0))
    return pl.pallas_call(
        weight_kernel,
        out_shape=shapes,
        grid_spec=pltpu.PrefetchScalarGridSpec(
            num_scalar_prefetch=1,
            grid=(4,),
            in_specs=[
                whole(q_own),
                pl.BlockSpec((ch, feat), lambda r, idx: (0, r)),
                pl.BlockSpec((n_loc // 2, feat), lambda r, idx: (0, r)),
                pl.BlockSpec((n_loc // 2, feat), lambda r, idx: (0, r)),
            ],
            out_specs=tuple(whole(a) for a in shapes),
            scratch_shapes=[pltpu.VMEM((ch, n_loc), BF16)],
        ),
        compiler_params=params(30),
        cost_estimate=cost(8 * n_loc * feat * ch, 8 * n_loc * feat + 28 * ch * feat),
    )(order, q_own, *hbm(w_here, h_x, h_k))


def ring_finish(terms, first, up, down):
    _, _, b0, b1, b3 = terms
    from_down, from_up = first
    h = b1.shape[0]
    from_down2 = up(bf(b1 + from_down[h:].astype(F32)))
    from_up2 = down(bf(b3 + from_up[:h].astype(F32)))
    lower = b0[:h] + from_up[h:].astype(F32) + from_down2.astype(F32)
    upper = b0[h:] + from_down[:h].astype(F32) + from_up2.astype(F32)
    return jnp.concatenate([lower, upper])


def local(hidden, weight, embed, embed_grad, eigvec, eigval):
    dp, chan = lax.axis_index("dp"), lax.axis_index("chan")
    zlo, y = dp // 4, dp % 4
    x, zhi, core = chan // 4, (chan // 2) % 2, chan % 2
    z = zhi * 2 + zlo
    n_loc = embed.shape[0]
    rows = n_loc * 8
    ch = embed.shape[1]
    feat = hidden.shape[1] // 8
    sub = n_loc // 8

    groups = [[0, 1, 2, 3], [4, 5, 6, 7]]
    x_groups = [[(i * 2 + a) * 2 + b for i in range(4)] for a in range(2) for b in range(2)]
    message, hidden, weight = tie(moments(embed, embed_grad, eigvec), hidden, weight)
    got = lax.all_to_all(message, "dp", 0, 0, axis_index_groups=groups)

    def hidden_part(r, half, start, size):
        return lax.dynamic_slice(hidden, (start, (half * 4 + (y + r) % 4) * feat), (size, feat))

    mine = jnp.concatenate([hidden_part(r, 1 - zlo, (core * 4 + x) * sub, sub) for r in range(4)], axis=1)
    h0 = stacked([z_up(mine[: sub // 2]), z_down(mine[sub // 2 :])])

    half_rows = weight.shape[0] // 2
    fs = half_rows // 4
    w_keep, w_give = turned_halves(weight, core)
    w1 = jnp.concatenate([w_keep, swap(w_give)])
    got, h0, w1 = tie(got, h0, w1)
    h_left, h_right = x_up(h0), x_down(h0)
    quarter, sent = quarter_terms(got)
    other = z_flip[1](sent)
    root = jnp.sqrt(eigval)
    root, _ = tie(root, quarter)
    wsum, first = first_terms(eigvec, root, embed_grad)
    other, first, wsum = tie(other, first, wsum)
    inner4, means = inner_terms(quarter, sent, other, eigvec, root, y, n_loc)
    inner4, w1 = tie(inner4, w1)
    inner = lax.all_to_all(inner4, "dp", 0, 0, axis_index_groups=groups).reshape(ch, ch)
    wz = [lax.dynamic_slice(w1, (0, (z ^ j) * fs), (2 * ch, fs)) for j in range(4)]
    wz = [wz[0]] + [z_flip[j](wz[j]) for j in (1, 2, 3)]
    inner, h_left, h_right, *wz = tie(inner, h_left, h_right, *wz)
    w_own = jnp.stack([jnp.concatenate([wz[0], wz[2]]), jnp.concatenate([wz[1], wz[3]])])
    w_left, w_right = y_up(w_own), y_down(w_own)
    h_two = x_up(h_left[: sub // 2]), x_down(h_right[sub // 2 :])
    grad_z, turned = grad_z_of(eigvec, inner, embed, first, wsum, means, rows)

    w_order = []
    for r in range(4):
        for f in range(2):
            y_s = 2 * (r % 2) + (zhi ^ f)
            w_order.append(((y_s - y) % 4) * 2 + ((r // 2) ^ zlo))
    w_order = jnp.stack(w_order).astype(jnp.int32)
    h_order = jnp.stack([zlo * 4 + (y + r) % 4 for r in range(4)] + [core, x]).astype(jnp.int32)

    ht = n_loc // 2
    r_own = z_flip[1](grad_z)
    r_oth = z_flip[3](grad_z)
    own2 = swap(grad_z)
    w_here = weight_here(turned, hidden, h_order)
    w_two = y_up(w_left[:1]), y_down(w_right[1:])
    r_own, r_oth, w_here, *two = tie(r_own, r_oth, w_here, *w_two, *h_two)
    w_two, h_two = two[:2], two[2:]
    h_x = stacked([h0, h_right, *h_two, h_left])
    h_k = swap(h_x)
    w_all = in_order([w_own, w_right, *w_two, w_left], w_order)

    far = z_flip[1](r_oth[:ht]), z_flip[3](r_own[ht:])
    par = hidden_terms([r_own, swap(r_own), r_oth, swap(r_oth)], w_all)
    par, *far = tie(par, *far)
    par_got = lax.all_to_all(par, "chan", 0, 0, axis_index_groups=x_groups)

    r_own, _ = tie(r_own, par)
    w_terms = weight_terms(r_own, w_here, h_x, h_k, h_order)
    w_first = y_up(w_terms[0]), y_down(w_terms[1])

    far = jnp.concatenate(far)
    far2 = swap(far)
    grad_z, _ = tie(grad_z, w_terms[0])
    own = hidden_terms([grad_z, own2, far, far2], w_all)
    own, par_got = tie(own, par_got)
    own_got = lax.all_to_all(own, "chan", 0, 0, axis_index_groups=x_groups)
    s_par = bf(jnp.sum(par_got.astype(F32), axis=0))
    p1 = z_flip[1](s_par[:, :fs])
    p3 = z_flip[3](s_par[:, fs:])
    w_sum = ring_finish(w_terms, w_first, y_up, y_down)
    s_own = bf(jnp.sum(own_got.astype(F32), axis=0))
    p0 = s_own[:, :fs]
    p2 = z_flip[2](s_own[:, fs:])
    grad_weight = bf(w_sum.T)
    odd = zlo == 1
    u0, u1 = jnp.where(odd, p1, p0), jnp.where(odd, p0, p1)
    u2, u3 = jnp.where(odd, p3, p2), jnp.where(odd, p2, p3)
    low = jnp.concatenate([u0, u1], axis=1)
    high = jnp.concatenate([u2, u3], axis=1)
    up = zhi == 1
    grad_hidden = jnp.concatenate([jnp.where(up, high, low), jnp.where(up, low, high)], axis=1)
    return grad_weight, grad_hidden


def solution(mesh):
    in_specs = (
        P("dp", None),
        P("dp", "chan"),
        P("dp", "chan"),
        P("dp", "chan"),
        P("chan", None),
        P("chan"),
    )
    out_specs = (P("dp", "chan"), P("dp", "chan"))
    return jax.shard_map(local, mesh=mesh, in_specs=in_specs, out_specs=out_specs, check_vma=False)
```

time: 634 us -> 207 us (0.33)
  waiting for transfers between devices: 528 us -> 48 us
  Pallas kernels: 0 us -> 68.7 us
  matrix products: 59.3 us -> 0 us
  starting transfers between devices: 0.6 us -> 54.5 us
  blocking collectives: 20.3 us -> 0 us
  between operations: 13.9 us -> 1.09 us
  local copies, waits for them, and re-layouts: 4.08 us -> 16.2 us
  other arithmetic: 6.47 us -> 17.1 us
    reduce_scatter x2 -> x0, waiting for transfers between devices: 400 us -> none  [the longest x1 245 us: local(): lax.psum_scatter(partial_input, 'chan', scatter_dimension=1, tiled=True)]
    psum x1 -> x0, waiting for transfers between devices: 72.6 us -> none  [local(): dmat = lax.psum(local_moment, 'dp')]
    pallas_call x0 -> x13, Pallas kernels: none -> 68.7 us  [the longest x2 14.8 us: hidden_terms(): pl.pallas_call(hidden_kernel, out_shape=pltpu.HBM((4, rows, wide // 4), B...]
    dot_general x10 -> x0, matrix products: 59.3 us -> none  [the longest x1 18.1 us: local(): lax.dot_general(grad_z, lax.all_gather(proj_weight, 'dp', axis=0, tiled=T...]
    all_gather x1 -> x0, waiting for transfers between devices: 54.7 us -> none  [local(): lax.all_gather(proj_weight, 'dp', axis=0, tiled=True)]
    ppermute x0 -> x31, waiting for transfers between devices: none -> 44.6 us  [mover(): return lambda a: lax.ppermute(a, AXES, pairs)]
    ppermute x0 -> x31, starting transfers between devices: none -> 35.1 us  [mover(): return lambda a: lax.ppermute(a, AXES, pairs)]
    psum x1 -> x0, blocking collectives: 20.3 us -> none  [local(): lax.psum((jnp.sum(zlocal, axis=0), jnp.sum(glocal, axis=0)), 'dp')]
  transfers between devices with their start and end apart: 4 -> 35, of which waited for: 4 -> 15; matrix products, arithmetic and copies ran while one was open for 10% -> 12% of each run, Pallas kernels for 0% -> 29%
where the time goes in v1:
time: 207 us; the launch traced here: 206 us
  Pallas kernels  68.7 us (33%)
  starting transfers between devices  54.5 us (26%)
  waiting for transfers between devices  48 us (23%)
  other arithmetic  17.1 us (8%)
  local copies, waits for them, and re-layouts  16.2 us (8%)
    ppermute x31, waiting for transfers between devices, mover(): return lambda a: lax.ppermute(a, AXES, pairs)  44.6 us
    ppermute x31, starting transfers between devices, mover(): return lambda a: lax.ppermute(a, AXES, pairs)  35.1 us
    pallas_call x2, Pallas kernels, hidden_terms(): pl.pallas_call(hidden_kernel, out_shape=pltpu.HBM((4, rows, wide // 4), B...  14.8 us
    pallas_call x1, Pallas kernels, weight_terms(): pl.pallas_call(weight_kernel, out_shape=shapes, grid_spec=pltpu.PrefetchS...  12.8 us
    pallas_call x1, Pallas kernels, weight_here(): pl.pallas_call(here_kernel, out_shape=pltpu.HBM((ch, 4 * feat), F32), gri...  10.4 us
    pallas_call x1, Pallas kernels, grad_z_of(): pl.pallas_call(functools.partial(grad_z_kernel, scale=2.0 / rows), out_sh...  7.38 us
    unnamed x44, local copies, waits for them, and re-layouts  6.15 us
    pallas_call x1, Pallas kernels, moments(): pl.pallas_call(moments_kernel, out_shape=pltpu.HBM((4, ch // 4 + 16, ch),...  6.04 us
  transfers between devices with their start and end apart: 35, of which 15 were waited for; matrix products, arithmetic and copies ran while one was open for 12% of the time, Pallas kernels for 29%

profile of v1, /device:TPU:2, one launch (start us, length us, event | category | flops | bytes accessed | tf_op | source)
XLA Modules:
  0.0 205.6 jit_solution(12594095321358466757)
XLA Ops:
  0.8 6.0 %shard_map.77 = bf16[4,144,512]{2,1,0:T(8,128)(2,1)} custom-call(bf16[1024,512]{1,0:T(8,128)(2,1)} %z_ref.3, bf16[1024,512]{1,0:T(8,128)(2,1)} %g_ref.3, f32[512,512]{1,0:T(8,128)} %u_ref.7), custom_call_target="tpu_custom_call" | custom-call | flops 2147483648 | bytes 3670016 | tf_op jit(solution)/shard_map/pallas_call | solution.py:103
  8.3 2.0 collective-permute-start
  10.3 2.2 %collective-permute-start.1 = (bf16[64,4096]{1,0:T(8,128)(2,1)S(1)}, bf16[64,4096]{1,0:T(8,128)(2,1)S(1)}, u32[]{:S(2)}, u32[]{:S(2)}) collective-permute-start(bf16[64,4096]{1,0:T(8,128)(2,1)S(1)} %get-tuple-element.114), channel_id=1, source_target_pairs={{0,66},{1,67},{2,64},{3,65},{4,70},{5,71},{6,68},{7,69},{8,74},{9,... | collective-permute-start | bytes 1572872 | tf_op jit(solution)/shard_map/ppermute | solution.py:30
  12.9 4.5 %all-to-all-start = ((bf16[4,144,512]{2,1,0:T(8,128)(2,1)}), bf16[4,144,512]{2,1,0:T(8,128)(2,1)}, u32[]{:S(2)}, u32[]{:S(2)}) async-start(bf16[4,144,512]{2,1,0:T(8,128)(2,1)} %shard_map.77), calls=%async_computation | async-start | bytes 1179648 | tf_op jit(solution)/shard_map/all_to_all | solution.py:460
  17.4 6.9 %collective-permute-done.refs_0_ = bf16[64,4096]{1,0:T(8,128)(2,1)S(1)} collective-permute-done((bf16[64,4096]{1,0:T(8,128)(2,1)S(1)}, bf16[64,4096]{1,0:T(8,128)(2,1)S(1)}, u32[]{:S(2)}, u32[]{:S(2)}) %collective-permute-start) | collective-permute-done | bytes 524320 | tf_op jit(solution)/shard_map/ppermute | solution.py:30
  25.4 2.2 %pad_maximum_fusion.1 = bf16[1024,512]{1,0:T(8,128)(2,1)} fusion(bf16[512,512]{1,0:T(8,128)(2,1)} %collective-permute-done.2, bf16[512,512]{1,0:T(8,128)(2,1)S(1)} %get-tuple-element.53), kind=kLoop, calls=%fused_computation.1 | loop fusion | flops 2097152 | bytes 2097152 | tf_op jit(solution)/shard_map/concatenate | solution.py:471
  32.9 5.1 %shard_map.81 = (f32[512,512]{1,0:T(8,128)}, f32[1024,512]{1,0:T(8,128)}) custom-call(f32[512,512]{1,0:T(8,128)} %u_ref.7, f32[1,512]{1,0:T(1,128)S(1)} %bitcast.25, bf16[1024,512]{1,0:T(8,128)(2,1)} %g_ref.3), custom_call_target="tpu_custom_call" | custom-call | flops 1879048192 | bytes 5242880 | tf_op jit(solution)/shard_map/pallas_call | solution.py:190
  38.2 3.0 %shard_map.82 = (bf16[4,128,512]{2,1,0:T(8,128)(2,1)}, f32[8,512]{1,0:T(8,128)}) custom-call(s32[1]{0:T(128)} %bitcast.6.y_ref, f32[128,512]{1,0:T(8,128)} %get-tuple-element.56.quarter_ref, bf16[192,512]{1,0:T(8,128)(2,1)} %get-tuple-element.57.sent_ref, bf16[192,512]{1,0:T(8,128)(2,1)} %collective-permute-done.3.other_ref, f32[512,512]{1,0:T(8,128)} %u_ref.7, ...), custom_call_target="tpu_custom_call" | custom-call | tf_op jit(solution)/shard_map/pallas_call | solution.py:158
  41.2 4.2 %all-to-all-start.1 = ((bf16[4,128,512]{2,1,0:T(8,128)(2,1)}), bf16[4,128,512]{2,1,0:T(8,128)(2,1)}, u32[]{:S(2)}, u32[]{:S(2)}) async-start(bf16[4,128,512]{2,1,0:T(8,128)(2,1)} %get-tuple-element.64), calls=%async_computation.1 | async-start | bytes 1048576 | tf_op jit(solution)/shard_map/all_to_all | solution.py:482
  48.1 2.7 %collective-permute-start.7 = (bf16[1024,128]{1,0:T(8,128)(2,1)S(1)}, bf16[1024,128]{1,0:T(8,128)(2,1)S(1)}, u32[]{:S(2)}, u32[]{:S(2)}) collective-permute-start(bf16[1024,128]{1,0:T(8,128)(2,1)S(1)} %get-tuple-element.111), channel_id=1, source_target_pairs={{0,2},{1,3},{2,0},{3,1},{4,6},{5,7},{6,4},{7,5},{8,10},{9,11},{10,... | collective-permute-start | bytes 786440 | tf_op jit(solution)/shard_map/ppermute | solution.py:30
  51.5 4.4 %collective-permute-done.6 = bf16[1024,128]{1,0:T(8,128)(2,1)S(1)} collective-permute-done((bf16[1024,128]{1,0:T(8,128)(2,1)S(1)}, bf16[1024,128]{1,0:T(8,128)(2,1)S(1)}, u32[]{:S(2)}, u32[]{:S(2)}) %collective-permute-start.6) | collective-permute-done | bytes 262176 | tf_op jit(solution)/shard_map/ppermute | solution.py:30
  55.9 4.3 %collective-permute-done.7 = bf16[1024,128]{1,0:T(8,128)(2,1)S(1)} collective-permute-done((bf16[1024,128]{1,0:T(8,128)(2,1)S(1)}, bf16[1024,128]{1,0:T(8,128)(2,1)S(1)}, u32[]{:S(2)}, u32[]{:S(2)}) %collective-permute-start.7) | collective-permute-done | bytes 262176 | tf_op jit(solution)/shard_map/ppermute | solution.py:30
  60.9 2.0 collective-permute-done.8
  68.3 7.4 %shard_map.83 = (bf16[1024,512]{1,0:T(8,128)(2,1)}, bf16[512,1024]{1,0:T(8,128)(2,1)}) custom-call(f32[512,512]{1,0:T(8,128)} %u_ref.7, bf16[512,512]{1,0:T(8,128)(2,1)} %bitcast.9.inner_ref, bf16[1024,512]{1,0:T(8,128)(2,1)} %z_ref.3, f32[1024,512]{1,0:T(8,128)} %get-tuple-element.68.first_ref, f32[512,512]{1,0:T(8,128)} %get-tuple-element.69.wsum_ref, ...), custom_call_target="tpu_custom_call" | custom-call | flops 2415919104 | bytes 6815744 | tf_op jit(solution)/shard_map/pallas_call | solution.py:214
  79.4 10.3 %collective-permute-done.11.left_ref = bf16[2,2048,128]{2,1,0:T(8,128)(2,1)S(1)} collective-permute-done((bf16[2,2048,128]{2,1,0:T(8,128)(2,1)S(1)}, bf16[2,2048,128]{2,1,0:T(8,128)(2,1)S(1)}, u32[]{:S(2)}, u32[]{:S(2)}) %collective-permute-start.11) | collective-permute-done | bytes 1048608 | tf_op jit(solution)/shard_map/ppermute | solution.py:30
  95.3 2.8 %collective-permute-start.14 = (bf16[1,2048,128]{2,1,0:T(8,128)(2,1)}, bf16[1,2048,128]{2,1,0:T(8,128)(2,1)}, u32[]{:S(2)}, u32[]{:S(2)}) collective-permute-start(bf16[1,2048,128]{2,1,0:T(8,128)(2,1)} %slice.75), channel_id=1, source_target_pairs={{0,48},{1,49},{2,50},{3,51},{4,52},{5,53},{6,54},{7,55},{8,56},{9,... | collective-permute-start | bytes 1572872 | tf_op jit(solution)/shard_map/ppermute | solution.py:30
  98.2 10.4 %shard_map.84.own_ref = f32[512,4096]{1,0:T(8,128)} custom-call(s32[6]{0:T(128)S(1)} %stack.63.idx_ref, bf16[512,1024]{1,0:T(8,128)(2,1)} %get-tuple-element.72.p_ref, bf16[1024,8192]{1,0:T(8,128)(2,1)} %own_ref), custom_call_target="tpu_custom_call" | custom-call | flops 4294967296 | bytes 16777216 | tf_op jit(solution)/shard_map/pallas_call | solution.py:374
  108.7 3.4 %shard_map.87.hx_ref = bf16[512,4096]{1,0:T(8,128)(2,1)} custom-call(bf16[128,4096]{1,0:T(8,128)(2,1)S(1)} %copy-done.3, bf16[128,4096]{1,0:T(8,128)(2,1)S(1)} %copy-done.13, bf16[64,4096]{1,0:T(8,128)(2,1)S(1)} %copy-done.15, bf16[64,4096]{1,0:T(8,128)(2,1)} %collective-permute-done.16.refs_3_, bf16[128,4096]{1,0:T(8,128)(2,1)S(1)} %copy-done.10), custom_call_target="tpu_custom_call" | custom-call | tf_op jit(solution)/shard_map/pallas_call | solution.py:309
  117.9 2.6 %shard_map.85.refs_4_ = bf16[2048,1024]{1,0:T(8,128)(2,1)S(1)} custom-call(s32[8]{0:T(128)S(1)} %stack.75.idx_ref, bf16[2,2048,128]{2,1,0:T(8,128)(2,1)S(1)} %pad_maximum_fusion.2.own_ref, bf16[2,2048,128]{2,1,0:T(8,128)(2,1)S(1)} %copy-done.7, bf16[1,2048,128]{2,1,0:T(8,128)(2,1)} %collective-permute-done.12.two_a_ref, ...), custom_call_target="tpu_custom_call" | custom-call | tf_op jit(solution)/shard_map/pallas_call | solution.py:289
  122.5 7.7 %shard_map.86 = bf16[4,1024,256]{2,1,0:T(8,128)(2,1)} custom-call(bf16[1024,512]{1,0:T(8,128)(2,1)S(1)} %collective-permute-done.9.refs_0_.q_ref, bf16[1024,512]{1,0:T(8,128)(2,1)} %collective-permute-done.17.refs_1_, bf16[1024,512]{1,0:T(8,128)(2,1)} %collective-permute-done.10.refs_2_, bf16[1024,512]{1,0:T(8,128)(2,1)} %collective-permute-done.18.refs_3_, ...), custom_call_target="tpu_custom_call" | custom-call | flops 4294967296 | bytes 10485760 | tf_op jit(solution)/shard_map/pallas_call | solution.py:359
  131.1 5.9 %all-to-all-start.2 = ((bf16[4,1024,256]{2,1,0:T(8,128)(2,1)}), bf16[4,1024,256]{2,1,0:T(8,128)(2,1)}, u32[]{:S(2)}, u32[]{:S(2)}) async-start(bf16[4,1024,256]{2,1,0:T(8,128)(2,1)} %shard_map.86), calls=%async_computation.2 | async-start | bytes 4194304 | tf_op jit(solution)/shard_map/all_to_all | solution.py:514
  139.3 12.8 %shard_map.88 = (bf16[512,1024]{1,0:T(8,128)(2,1)}, bf16[512,1024]{1,0:T(8,128)(2,1)}, f32[512,1024]{1,0:T(8,128)}, f32[256,1024]{1,0:T(8,128)}, f32[256,1024]{1,0:T(8,128)}) custom-call(s32[6]{0:T(128)S(1)} %stack.63.idx_ref, bf16[1024,512]{1,0:T(8,128)(2,1)S(1)} %collective-permute-done.9.refs_0_.q_ref, f32[512,4096]{1,0:T(8,128)} %shard_map.84.own_ref, ...), custom_call_target="tpu_custom_call" | custom-call | flops 4294967296 | bytes 23068672 | tf_op jit(solution)/shard_map/pallas_call | solution.py:415
  152.1 3.2 %collective-permute-start.22 = (bf16[512,1024]{1,0:T(8,128)(2,1)}, bf16[512,1024]{1,0:T(8,128)(2,1)}, u32[]{:S(2)}, u32[]{:S(2)}) collective-permute-start(bf16[512,1024]{1,0:T(8,128)(2,1)} %get-tuple-element.89), channel_id=1, source_target_pairs={{0,48},{1,49},{2,50},{3,51},{4,52},{5,53},{6,54},{7,55},{8,56},{9,... | collective-permute-start | bytes 3145736 | tf_op jit(solution)/shard_map/ppermute | solution.py:30
  155.3 7.1 %shard_map.89 = bf16[4,1024,256]{2,1,0:T(8,128)(2,1)} custom-call(bf16[1024,512]{1,0:T(8,128)(2,1)} %get-tuple-element.93.refs_0_, bf16[1024,512]{1,0:T(8,128)(2,1)S(1)} %collective-permute-done.26.refs_1_, bf16[1024,512]{1,0:T(8,128)(2,1)S(1)} %constant_dynamic-update-slice_fusion.refs_2_, bf16[1024,512]{1,0:T(8,128)(2,1)S(1)} %collective-permute-done.27.refs_3_, ...), custom_call_target="tpu_custom_call" | custom-call | flops 4294967296 | bytes 10485760 | tf_op jit(solution)/shard_map/pallas_call | solution.py:359
  162.4 4.8 %all-to-all-start.3 = ((bf16[4,1024,256]{2,1,0:T(8,128)(2,1)}), bf16[4,1024,256]{2,1,0:T(8,128)(2,1)S(1)}, u32[]{:S(2)}, u32[]{:S(2)}) async-start(bf16[4,1024,256]{2,1,0:T(8,128)(2,1)} %shard_map.89), calls=%async_computation.3 | async-start | bytes 4194304 | tf_op jit(solution)/shard_map/all_to_all | solution.py:525
  167.2 2.2 %reduce_sum.24 = bf16[1024,256]{1,0:T(8,128)(2,1)S(1)} reduce(bf16[4,1024,256]{2,1,0:T(8,128)(2,1)} %all-to-all-done.2, bf16[]{:T(256)} %constant.124.clone.1), dimensions={0}, to_apply=%region_0.1 | reduce | flops 786432 | bytes 2621442 | tf_op jit(solution)/shard_map/reduce_sum | solution.py:526
  169.4 9.4 %collective-permute-done.23 = bf16[512,1024]{1,0:T(8,128)(2,1)} collective-permute-done((bf16[512,1024]{1,0:T(8,128)(2,1)}, bf16[512,1024]{1,0:T(8,128)(2,1)}, u32[]{:S(2)}, u32[]{:S(2)}) %collective-permute-start.23) | collective-permute-done | bytes 1048608 | tf_op jit(solution)/shard_map/ppermute | solution.py:30
  178.8 2.3 %add_convert_fusion.3 = bf16[256,1024]{1,0:T(8,128)(2,1)} fusion(f32[256,1024]{1,0:T(8,128)} %get-tuple-element.90, bf16[512,1024]{1,0:T(8,128)(2,1)} %collective-permute-done.23), kind=kLoop, calls=%fused_computation.8 | loop fusion | flops 786432 | bytes 2097152 | tf_op jit(solution)/shard_map/convert_element_type | solution.py:44
  183.1 3.2 %collective-permute-start.25 = (bf16[256,1024]{1,0:T(8,128)(2,1)}, bf16[256,1024]{1,0:T(8,128)(2,1)}, u32[]{:S(2)}, u32[]{:S(2)}) collective-permute-start(bf16[256,1024]{1,0:T(8,128)(2,1)} %add_convert_fusion.1), channel_id=1, source_target_pairs={{0,48},{1,49},{2,50},{3,51},{4,52},{5,53},{6,54},{7,55},{8,56},{9,... | collective-permute-start | bytes 1572872 | tf_op jit(solution)/shard_map/ppermute | solution.py:30
  189.2 2.6 %all-to-all-done.3 = bf16[4,1024,256]{2,1,0:T(8,128)(2,1)S(1)} async-done(((bf16[4,1024,256]{2,1,0:T(8,128)(2,1)}), bf16[4,1024,256]{2,1,0:T(8,128)(2,1)S(1)}, u32[]{:S(2)}, u32[]{:S(2)}) %all-to-all-start.3) | async-done | bytes 2097184 | tf_op jit(solution)/shard_map/all_to_all | solution.py:525
  197.0 2.5 %add_convert_fusion.2 = (bf16[256,1024]{1,0:T(8,128)(2,1)S(1)}, bf16[256,1024]{1,0:T(8,128)(2,1)S(1)}) fusion(bf16[256,1024]{1,0:T(8,128)(2,1)S(1)} %collective-permute-done.24, f32[512,1024]{1,0:T(8,128)} %get-tuple-element.88, bf16[512,1024]{1,0:T(8,128)(2,1)} %collective-permute-done.22, bf16[256,1024]{1,0:T(8,128)(2,1)} %collective-permute-done.25, ...), kind=kLoop, calls=%fused_computation.7 | loop fusion | flops 2621440 | bytes 5242880 | tf_op jit(solution)/shard_map/convert.2
  200.9 2.4 %collective-permute-done.29 = bf16[1024,128]{1,0:T(8,128)(2,1)S(1)} collective-permute-done((bf16[1024,128]{1,0:T(8,128)(2,1)S(1)}, bf16[1024,128]{1,0:T(8,128)(2,1)S(1)}, u32[]{:S(2)}, u32[]{:S(2)}) %collective-permute-start.29) | collective-permute-done | bytes 262176 | tf_op jit(solution)/shard_map/ppermute | solution.py:30
  (124 shorter events, 52.0 us)
Async XLA Ops:
  8.3 16.0 %collective-permute-start = (bf16[64,4096]{1,0:T(8,128)(2,1)S(1)}, bf16[64,4096]{1,0:T(8,128)(2,1)S(1)}, u32[]{:S(2)}, u32[]{:S(2)}) collective-permute-start(bf16[64,4096]{1,0:T(8,128)(2,1)S(1)} %get-tuple-element.115), channel_id=1, source_target_pairs={{0,64},{1,65},{2,66},{3,67},{4,68},{5,69},{6,70},{7,71},{8,72},{9,... | collective-permute-start | bytes 1572872 | tf_op jit(solution)/shard_map/ppermute | solution.py:30
  10.3 14.0 %collective-permute-start.1 = (bf16[64,4096]{1,0:T(8,128)(2,1)S(1)}, bf16[64,4096]{1,0:T(8,128)(2,1)S(1)}, u32[]{:S(2)}, u32[]{:S(2)}) collective-permute-start(bf16[64,4096]{1,0:T(8,128)(2,1)S(1)} %get-tuple-element.114), channel_id=1, source_target_pairs={{0,66},{1,67},{2,64},{3,65},{4,70},{5,71},{6,68},{7,69},{8,74},{9,... | collective-permute-start | bytes 1572872 | tf_op jit(solution)/shard_map/ppermute | solution.py:30
  12.8 12.5 %collective-permute-start.2 = (bf16[512,512]{1,0:T(8,128)(2,1)S(1)}, bf16[512,512]{1,0:T(8,128)(2,1)}, u32[]{:S(2)}, u32[]{:S(2)}) collective-permute-start(bf16[512,512]{1,0:T(8,128)(2,1)S(1)} %get-tuple-element.54), channel_id=1, source_target_pairs={{0,1},{1,0},{2,3},{3,2},{4,5},{5,4},{6,7},{7,6},{8,9},{9,8},{10,11... | collective-permute-start | bytes 1572872 | tf_op jit(solution)/shard_map/ppermute | solution.py:30
  12.9 15.4 %all-to-all-start = ((bf16[4,144,512]{2,1,0:T(8,128)(2,1)}), bf16[4,144,512]{2,1,0:T(8,128)(2,1)}, u32[]{:S(2)}, u32[]{:S(2)}) async-start(bf16[4,144,512]{2,1,0:T(8,128)(2,1)} %shard_map.77), calls=%async_computation | async-start | bytes 1179648 | tf_op jit(solution)/shard_map/all_to_all | solution.py:460
  28.3 34.7 %collective-permute-start.4 = (bf16[128,4096]{1,0:T(8,128)(2,1)S(1)}, bf16[128,4096]{1,0:T(8,128)(2,1)S(1)}, u32[]{:S(2)}, u32[]{:S(2)}) collective-permute-start(bf16[128,4096]{1,0:T(8,128)(2,1)S(1)} %copy-done.3), channel_id=1, source_target_pairs={{0,4},{1,5},{2,6},{3,7},{4,8},{5,9},{6,10},{7,11},{8,12},{9,13},{1... | collective-permute-start | bytes 3145736 | tf_op jit(solution)/shard_map/ppermute | solution.py:30
  29.8 33.2 %collective-permute-start.5 = (bf16[128,4096]{1,0:T(8,128)(2,1)S(1)}, bf16[128,4096]{1,0:T(8,128)(2,1)S(1)}, u32[]{:S(2)}, u32[]{:S(2)}) collective-permute-start(bf16[128,4096]{1,0:T(8,128)(2,1)S(1)} %copy-done.3), channel_id=1, source_target_pairs={{0,12},{1,13},{2,14},{3,15},{4,0},{5,1},{6,2},{7,3},{8,4},{9,5},{1... | collective-permute-start | bytes 3145736 | tf_op jit(solution)/shard_map/ppermute | solution.py:30
  41.2 21.7 %all-to-all-start.1 = ((bf16[4,128,512]{2,1,0:T(8,128)(2,1)}), bf16[4,128,512]{2,1,0:T(8,128)(2,1)}, u32[]{:S(2)}, u32[]{:S(2)}) async-start(bf16[4,128,512]{2,1,0:T(8,128)(2,1)} %get-tuple-element.64), calls=%async_computation.1 | async-start | bytes 1048576 | tf_op jit(solution)/shard_map/all_to_all | solution.py:482
  46.7 9.2 %collective-permute-start.6 = (bf16[1024,128]{1,0:T(8,128)(2,1)S(1)}, bf16[1024,128]{1,0:T(8,128)(2,1)S(1)}, u32[]{:S(2)}, u32[]{:S(2)}) collective-permute-start(bf16[1024,128]{1,0:T(8,128)(2,1)S(1)} %get-tuple-element.112), channel_id=1, source_target_pairs={{0,64},{1,65},{2,66},{3,67},{4,68},{5,69},{6,70},{7,71},{8,72},{9,... | collective-permute-start | bytes 786440 | tf_op jit(solution)/shard_map/ppermute | solution.py:30
  48.1 12.2 %collective-permute-start.7 = (bf16[1024,128]{1,0:T(8,128)(2,1)S(1)}, bf16[1024,128]{1,0:T(8,128)(2,1)S(1)}, u32[]{:S(2)}, u32[]{:S(2)}) collective-permute-start(bf16[1024,128]{1,0:T(8,128)(2,1)S(1)} %get-tuple-element.111), channel_id=1, source_target_pairs={{0,2},{1,3},{2,0},{3,1},{4,6},{5,7},{6,4},{7,5},{8,10},{9,11},{10,... | collective-permute-start | bytes 786440 | tf_op jit(solution)/shard_map/ppermute | solution.py:30
  50.8 12.2 %collective-permute-start.8 = (bf16[1024,128]{1,0:T(8,128)(2,1)S(1)}, bf16[1024,128]{1,0:T(8,128)(2,1)}, u32[]{:S(2)}, u32[]{:S(2)}) collective-permute-start(bf16[1024,128]{1,0:T(8,128)(2,1)S(1)} %get-tuple-element.110), channel_id=1, source_target_pairs={{0,66},{1,67},{2,64},{3,65},{4,70},{5,71},{6,68},{7,69},{8,74},{9,... | collective-permute-start | bytes 786440 | tf_op jit(solution)/shard_map/ppermute | solution.py:30
  65.0 24.7 %collective-permute-start.11 = (bf16[2,2048,128]{2,1,0:T(8,128)(2,1)S(1)}, bf16[2,2048,128]{2,1,0:T(8,128)(2,1)S(1)}, u32[]{:S(2)}, u32[]{:S(2)}) collective-permute-start(bf16[2,2048,128]{2,1,0:T(8,128)(2,1)S(1)} %pad_maximum_fusion.2.own_ref), channel_id=1, source_target_pairs={{0,16},{1,17},{2,18},{3,19},{4,20},{5,21},{6,22},{7,23},{8,24},{9,... | collective-permute-start | bytes 3145736 | tf_op jit(solution)/shard_map/ppermute | solution.py:30
  66.7 25.5 %collective-permute-start.13 = (bf16[2,2048,128]{2,1,0:T(8,128)(2,1)S(1)}, bf16[2,2048,128]{2,1,0:T(8,128)(2,1)S(1)}, u32[]{:S(2)}, u32[]{:S(2)}) collective-permute-start(bf16[2,2048,128]{2,1,0:T(8,128)(2,1)S(1)} %pad_maximum_fusion.2.own_ref), channel_id=1, source_target_pairs={{0,48},{1,49},{2,50},{3,51},{4,52},{5,53},{6,54},{7,55},{8,56},{9,... | collective-permute-start | bytes 3145736 | tf_op jit(solution)/shard_map/ppermute | solution.py:30
  75.7 32.9 %collective-permute-start.9 = (bf16[1024,512]{1,0:T(8,128)(2,1)}, bf16[1024,512]{1,0:T(8,128)(2,1)S(1)}, u32[]{:S(2)}, u32[]{:S(2)}) collective-permute-start(bf16[1024,512]{1,0:T(8,128)(2,1)} %get-tuple-element.93.refs_0_), channel_id=1, source_target_pairs={{0,64},{1,65},{2,66},{3,67},{4,68},{5,69},{6,70},{7,71},{8,72},{9,... | collective-permute-start | bytes 3145736 | tf_op jit(solution)/shard_map/ppermute | solution.py:30
  75.7 32.9 %collective-permute-start.10 = (bf16[1024,512]{1,0:T(8,128)(2,1)}, bf16[1024,512]{1,0:T(8,128)(2,1)}, u32[]{:S(2)}, u32[]{:S(2)}) collective-permute-start(bf16[1024,512]{1,0:T(8,128)(2,1)} %get-tuple-element.93.refs_0_), channel_id=1, source_target_pairs={{0,66},{1,67},{2,64},{3,65},{4,70},{5,71},{6,68},{7,69},{8,74},{9,... | collective-permute-start | bytes 3145736 | tf_op jit(solution)/shard_map/ppermute | solution.py:30
  77.0 17.5 %collective-permute-start.15 = (bf16[64,4096]{1,0:T(8,128)(2,1)S(1)}, bf16[64,4096]{1,0:T(8,128)(2,1)S(1)}, u32[]{:S(2)}, u32[]{:S(2)}) collective-permute-start(bf16[64,4096]{1,0:T(8,128)(2,1)S(1)} %slice.58), channel_id=1, source_target_pairs={{0,4},{1,5},{2,6},{3,7},{4,8},{5,9},{6,10},{7,11},{8,12},{9,13},{1... | collective-permute-start | bytes 1572872 | tf_op jit(solution)/shard_map/ppermute | solution.py:30
  89.7 18.9 %collective-permute-start.16 = (bf16[64,4096]{1,0:T(8,128)(2,1)}, bf16[64,4096]{1,0:T(8,128)(2,1)}, u32[]{:S(2)}, u32[]{:S(2)}) collective-permute-start(bf16[64,4096]{1,0:T(8,128)(2,1)} %slice.59), channel_id=1, source_target_pairs={{0,12},{1,13},{2,14},{3,15},{4,0},{5,1},{6,2},{7,3},{8,4},{9,5},{1... | collective-permute-start | bytes 1572872 | tf_op jit(solution)/shard_map/ppermute | solution.py:30
  92.2 16.4 %collective-permute-start.12 = (bf16[1,2048,128]{2,1,0:T(8,128)(2,1)}, bf16[1,2048,128]{2,1,0:T(8,128)(2,1)}, u32[]{:S(2)}, u32[]{:S(2)}) collective-permute-start(bf16[1,2048,128]{2,1,0:T(8,128)(2,1)} %slice.74), channel_id=1, source_target_pairs={{0,16},{1,17},{2,18},{3,19},{4,20},{5,21},{6,22},{7,23},{8,24},{9,... | collective-permute-start | bytes 1572872 | tf_op jit(solution)/shard_map/ppermute | solution.py:30
  95.3 13.3 %collective-permute-start.14 = (bf16[1,2048,128]{2,1,0:T(8,128)(2,1)}, bf16[1,2048,128]{2,1,0:T(8,128)(2,1)}, u32[]{:S(2)}, u32[]{:S(2)}) collective-permute-start(bf16[1,2048,128]{2,1,0:T(8,128)(2,1)} %slice.75), channel_id=1, source_target_pairs={{0,48},{1,49},{2,50},{3,51},{4,52},{5,53},{6,54},{7,55},{8,56},{9,... | collective-permute-start | bytes 1572872 | tf_op jit(solution)/shard_map/ppermute | solution.py:30
  112.0 27.3 %collective-permute-start.21 = (bf16[512,4096]{1,0:T(8,128)(2,1)}, bf16[512,4096]{1,0:T(8,128)(2,1)}, u32[]{:S(2)}, u32[]{:S(2)}) collective-permute-start(bf16[512,4096]{1,0:T(8,128)(2,1)} %shard_map.87.hx_ref), channel_id=1, source_target_pairs={{0,1},{1,0},{2,3},{3,2},{4,5},{5,4},{6,7},{7,6},{8,9},{9,8},{10,11... | collective-permute-start | bytes 12582920 | tf_op jit(solution)/shard_map/ppermute | solution.py:30
  112.0 9.0 %collective-permute-start.17 = (bf16[1024,512]{1,0:T(8,128)(2,1)S(1)}, bf16[1024,512]{1,0:T(8,128)(2,1)}, u32[]{:S(2)}, u32[]{:S(2)}) collective-permute-start(bf16[1024,512]{1,0:T(8,128)(2,1)S(1)} %collective-permute-done.9.refs_0_.q_ref), channel_id=1, source_target_pairs={{0,1},{1,0},{2,3},{3,2},{4,5},{5,4},{6,7},{7,6},{8,9},{9,8},{10,11... | collective-permute-start | bytes 3145736 | tf_op jit(solution)/shard_map/ppermute | solution.py:30
  112.5 10.0 %collective-permute-start.18 = (bf16[1024,512]{1,0:T(8,128)(2,1)}, bf16[1024,512]{1,0:T(8,128)(2,1)}, u32[]{:S(2)}, u32[]{:S(2)}) collective-permute-start(bf16[1024,512]{1,0:T(8,128)(2,1)} %collective-permute-done.10.refs_2_), channel_id=1, source_target_pairs={{0,1},{1,0},{2,3},{3,2},{4,5},{5,4},{6,7},{7,6},{8,9},{9,8},{10,11... | collective-permute-start | bytes 3145736 | tf_op jit(solution)/shard_map/ppermute | solution.py:30
  115.3 15.0 %collective-permute-start.19 = (bf16[512,512]{1,0:T(8,128)(2,1)}, bf16[512,512]{1,0:T(8,128)(2,1)}, u32[]{:S(2)}, u32[]{:S(2)}) collective-permute-start(bf16[512,512]{1,0:T(8,128)(2,1)} %slice.60), channel_id=1, source_target_pairs={{0,64},{1,65},{2,66},{3,67},{4,68},{5,69},{6,70},{7,71},{8,72},{9,... | collective-permute-start | bytes 1572872 | tf_op jit(solution)/shard_map/ppermute | solution.py:30
  115.3 15.9 %collective-permute-start.20 = (bf16[512,512]{1,0:T(8,128)(2,1)}, bf16[512,512]{1,0:T(8,128)(2,1)}, u32[]{:S(2)}, u32[]{:S(2)}) collective-permute-start(bf16[512,512]{1,0:T(8,128)(2,1)} %slice.61), channel_id=1, source_target_pairs={{0,66},{1,67},{2,64},{3,65},{4,70},{5,71},{6,68},{7,69},{8,74},{9,... | collective-permute-start | bytes 1572872 | tf_op jit(solution)/shard_map/ppermute | solution.py:30
  121.0 34.3 %collective-permute-start.26 = (bf16[1024,512]{1,0:T(8,128)(2,1)}, bf16[1024,512]{1,0:T(8,128)(2,1)S(1)}, u32[]{:S(2)}, u32[]{:S(2)}) collective-permute-start(bf16[1024,512]{1,0:T(8,128)(2,1)} %get-tuple-element.93.refs_0_), channel_id=1, source_target_pairs={{0,1},{1,0},{2,3},{3,2},{4,5},{5,4},{6,7},{7,6},{8,9},{9,8},{10,11... | collective-permute-start | bytes 3145736 | tf_op jit(solution)/shard_map/ppermute | solution.py:30
  131.1 31.2 %all-to-all-start.2 = ((bf16[4,1024,256]{2,1,0:T(8,128)(2,1)}), bf16[4,1024,256]{2,1,0:T(8,128)(2,1)}, u32[]{:S(2)}, u32[]{:S(2)}) async-start(bf16[4,1024,256]{2,1,0:T(8,128)(2,1)} %shard_map.86), calls=%async_computation.2 | async-start | bytes 4194304 | tf_op jit(solution)/shard_map/all_to_all | solution.py:514
  139.2 16.1 %collective-permute-start.27 = (bf16[1024,512]{1,0:T(8,128)(2,1)S(1)}, bf16[1024,512]{1,0:T(8,128)(2,1)S(1)}, u32[]{:S(2)}, u32[]{:S(2)}) collective-permute-start(bf16[1024,512]{1,0:T(8,128)(2,1)S(1)} %constant_dynamic-update-slice_fusion.refs_2_), channel_id=1, source_target_pairs={{0,1},{1,0},{2,3},{3,2},{4,5},{5,4},{6,7},{7,6},{8,9},{9,8},{10,11... | collective-permute-start | bytes 3145736 | tf_op jit(solution)/shard_map/ppermute | solution.py:30
  152.1 26.7 %collective-permute-start.23 = (bf16[512,1024]{1,0:T(8,128)(2,1)}, bf16[512,1024]{1,0:T(8,128)(2,1)}, u32[]{:S(2)}, u32[]{:S(2)}) collective-permute-start(bf16[512,1024]{1,0:T(8,128)(2,1)} %get-tuple-element.91), channel_id=1, source_target_pairs={{0,16},{1,17},{2,18},{3,19},{4,20},{5,21},{6,22},{7,23},{8,24},{9,... | collective-permute-start | bytes 3145736 | tf_op jit(solution)/shard_map/ppermute | solution.py:30
  152.1 29.0 %collective-permute-start.22 = (bf16[512,1024]{1,0:T(8,128)(2,1)}, bf16[512,1024]{1,0:T(8,128)(2,1)}, u32[]{:S(2)}, u32[]{:S(2)}) collective-permute-start(bf16[512,1024]{1,0:T(8,128)(2,1)} %get-tuple-element.89), channel_id=1, source_target_pairs={{0,48},{1,49},{2,50},{3,51},{4,52},{5,53},{6,54},{7,55},{8,56},{9,... | collective-permute-start | bytes 3145736 | tf_op jit(solution)/shard_map/ppermute | solution.py:30
  162.4 29.4 %all-to-all-start.3 = ((bf16[4,1024,256]{2,1,0:T(8,128)(2,1)}), bf16[4,1024,256]{2,1,0:T(8,128)(2,1)S(1)}, u32[]{:S(2)}, u32[]{:S(2)}) async-start(bf16[4,1024,256]{2,1,0:T(8,128)(2,1)} %shard_map.89), calls=%async_computation.3 | async-start | bytes 4194304 | tf_op jit(solution)/shard_map/all_to_all | solution.py:525
  181.1 15.9 %collective-permute-start.24 = (bf16[256,1024]{1,0:T(8,128)(2,1)}, bf16[256,1024]{1,0:T(8,128)(2,1)S(1)}, u32[]{:S(2)}, u32[]{:S(2)}) collective-permute-start(bf16[256,1024]{1,0:T(8,128)(2,1)} %add_convert_fusion.3), channel_id=1, source_target_pairs={{0,16},{1,17},{2,18},{3,19},{4,20},{5,21},{6,22},{7,23},{8,24},{9,... | collective-permute-start | bytes 1572872 | tf_op jit(solution)/shard_map/ppermute | solution.py:30
  183.1 13.9 %collective-permute-start.25 = (bf16[256,1024]{1,0:T(8,128)(2,1)}, bf16[256,1024]{1,0:T(8,128)(2,1)}, u32[]{:S(2)}, u32[]{:S(2)}) collective-permute-start(bf16[256,1024]{1,0:T(8,128)(2,1)} %add_convert_fusion.1), channel_id=1, source_target_pairs={{0,48},{1,49},{2,50},{3,51},{4,52},{5,53},{6,54},{7,55},{8,56},{9,... | collective-permute-start | bytes 1572872 | tf_op jit(solution)/shard_map/ppermute | solution.py:30
  187.6 13.4 %collective-permute-start.28 = (bf16[1024,128]{1,0:T(8,128)(2,1)S(1)}, bf16[1024,128]{1,0:T(8,128)(2,1)}, u32[]{:S(2)}, u32[]{:S(2)}) collective-permute-start(bf16[1024,128]{1,0:T(8,128)(2,1)S(1)} %get-tuple-element.120), channel_id=1, source_target_pairs={{0,66},{1,67},{2,64},{3,65},{4,70},{5,71},{6,68},{7,69},{8,74},{9,... | collective-permute-start | bytes 786440 | tf_op jit(solution)/shard_map/ppermute | solution.py:30
  (24 other events, 156.1 us)

commit v2 on v1

--- a/solution.py
+++ b/solution.py
@@ -343,12 +343,15 @@
     _, rows, wide = out_ref.shape
     tile = rows // 2
     for start in range(0, rows, tile):
-        acc, k0 = None, 0
+        acc, k0, seen = None, 0, 0
         for ref in lhs:
             depth = ref.shape[1]
-            term = dot(ref[start : start + tile, :], w_ref[k0 : k0 + depth, :], 1, 0)
-            acc = term if acc is None else acc + term
-            k0 += depth
+            if seen <= start < seen + ref.shape[0]:
+                term = dot(ref[start - seen : start - seen + tile, :], w_ref[k0 : k0 + depth, :], 1, 0)
+                acc = term if acc is None else acc + term
+            seen += ref.shape[0]
+            if seen == rows:
+                seen, k0 = 0, k0 + depth
         for r in range(4):
             out_ref[r, start : start + tile, :] = bf(acc[:, r * wide : (r + 1) * wide])
 
@@ -456,7 +459,13 @@
 
     groups = [[0, 1, 2, 3], [4, 5, 6, 7]]
     x_groups = [[(i * 2 + a) * 2 + b for i in range(4)] for a in range(2) for b in range(2)]
-    message, hidden, weight = tie(moments(embed, embed_grad, eigvec), hidden, weight)
+    fs = weight.shape[0] // 8
+    w_keep, w_give = turned_halves(weight, core)
+    w_got = swap(w_give)
+    wz = [
+        jnp.concatenate([lax.dynamic_slice(a, (0, (z ^ j) * fs), (ch, fs)) for a in (w_keep, w_got)]) for j in range(4)
+    ]
+    message, hidden, *wz = tie(moments(embed, embed_grad, eigvec), hidden, *wz)
     got = lax.all_to_all(message, "dp", 0, 0, axis_index_groups=groups)
 
     def hidden_part(r, half, start, size):
@@ -464,28 +473,20 @@
 
     mine = jnp.concatenate([hidden_part(r, 1 - zlo, (core * 4 + x) * sub, sub) for r in range(4)], axis=1)
     h0 = stacked([z_up(mine[: sub // 2]), z_down(mine[sub // 2 :])])
-
-    half_rows = weight.shape[0] // 2
-    fs = half_rows // 4
-    w_keep, w_give = turned_halves(weight, core)
-    w1 = jnp.concatenate([w_keep, swap(w_give)])
-    got, h0, w1 = tie(got, h0, w1)
     h_left, h_right = x_up(h0), x_down(h0)
+    wz = [wz[0]] + [z_flip[j](wz[j]) for j in (1, 2, 3)]
     quarter, sent = quarter_terms(got)
     other = z_flip[1](sent)
     root = jnp.sqrt(eigval)
     root, _ = tie(root, quarter)
     wsum, first = first_terms(eigvec, root, embed_grad)
-    other, first, wsum = tie(other, first, wsum)
-    inner4, means = inner_terms(quarter, sent, other, eigvec, root, y, n_loc)
-    inner4, w1 = tie(inner4, w1)
-    inner = lax.all_to_all(inner4, "dp", 0, 0, axis_index_groups=groups).reshape(ch, ch)
-    wz = [lax.dynamic_slice(w1, (0, (z ^ j) * fs), (2 * ch, fs)) for j in range(4)]
-    wz = [wz[0]] + [z_flip[j](wz[j]) for j in (1, 2, 3)]
-    inner, h_left, h_right, *wz = tie(inner, h_left, h_right, *wz)
+    other, first, wsum, *wz = tie(other, first, wsum, *wz)
     w_own = jnp.stack([jnp.concatenate([wz[0], wz[2]]), jnp.concatenate([wz[1], wz[3]])])
     w_left, w_right = y_up(w_own), y_down(w_own)
-    h_two = x_up(h_left[: sub // 2]), x_down(h_right[sub // 2 :])
+    inner4, means = inner_terms(quarter, sent, other, eigvec, root, y, n_loc)
+    inner = lax.all_to_all(inner4, "dp", 0, 0, axis_index_groups=groups).reshape(ch, ch)
+    inner, h_left, h_right = tie(inner, h_left, h_right)
+    h_two = x_up(h_left)
     grad_z, turned = grad_z_of(eigvec, inner, embed, first, wsum, means, rows)
 
     w_order = []
@@ -500,27 +501,26 @@
     r_own = z_flip[1](grad_z)
     r_oth = z_flip[3](grad_z)
     own2 = swap(grad_z)
+    turned, w_left, w_right = tie(turned, w_left, w_right)
     w_here = weight_here(turned, hidden, h_order)
     w_two = y_up(w_left[:1]), y_down(w_right[1:])
-    r_own, r_oth, w_here, *two = tie(r_own, r_oth, w_here, *w_two, *h_two)
-    w_two, h_two = two[:2], two[2:]
-    h_x = stacked([h0, h_right, *h_two, h_left])
-    h_k = swap(h_x)
     w_all = in_order([w_own, w_right, *w_two, w_left], w_order)
+    h_x = stacked([h0, h_right, h_two, h_left])
+    r_own, r_oth, w_here, w_all, h_x = tie(r_own, r_oth, w_here, w_all, h_x)
 
     far = z_flip[1](r_oth[:ht]), z_flip[3](r_own[ht:])
     par = hidden_terms([r_own, swap(r_own), r_oth, swap(r_oth)], w_all)
-    par, *far = tie(par, *far)
+    _, h_x = tie(par, h_x)
+    h_k = swap(h_x)
     par_got = lax.all_to_all(par, "chan", 0, 0, axis_index_groups=x_groups)
 
     r_own, _ = tie(r_own, par)
     w_terms = weight_terms(r_own, w_here, h_x, h_k, h_order)
     w_first = y_up(w_terms[0]), y_down(w_terms[1])
 
-    far = jnp.concatenate(far)
-    far2 = swap(far)
-    grad_z, _ = tie(grad_z, w_terms[0])
-    own = hidden_terms([grad_z, own2, far, far2], w_all)
+    grad_z, _, *far = tie(grad_z, w_terms[0], *far)
+    far2 = [swap(a) for a in far]
+    own = hidden_terms([grad_z, own2, *far, *far2], w_all)
     own, par_got = tie(own, par_got)
     own_got = lax.all_to_all(own, "chan", 0, 0, axis_index_groups=x_groups)
     s_par = bf(jnp.sum(par_got.astype(F32), axis=0))

time: 207 us -> 198 us (0.957)
  local copies, waits for them, and re-layouts: 16.2 us -> 10.6 us
  waiting for transfers between devices: 48 us -> 44.7 us
    ppermute x31, waiting for transfers between devices: 44.6 us -> 31.4 us  [mover(): return lambda a: lax.ppermute(a, AXES, pairs)]
    all_to_all x1, waiting for transfers between devices: 0.01 us -> 5.49 us  [local(): lax.all_to_all(inner4, 'dp', 0, 0, axis_index_groups=groups).reshape(ch, ch)]
    all_to_all x1, waiting for transfers between devices: 0.79 us -> 5.68 us  [local(): got = lax.all_to_all(message, 'dp', 0, 0, axis_index_groups=groups)]
    ppermute x31, starting transfers between devices: 35.1 us -> 37.5 us  [mover(): return lambda a: lax.ppermute(a, AXES, pairs)]
    unnamed x44 -> x25, local copies, waits for them, and re-layouts: 6.15 us -> 4.07 us
  transfers between devices with their start and end apart: 35 -> 35, of which waited for: 15 -> 10; matrix products, arithmetic and copies ran while one was open for 12% -> 10% of each run, Pallas kernels for 29% -> 31%
where the time goes in v2:
time: 198 us; the launch traced here: 197 us
  Pallas kernels  68.1 us (34%)
  starting transfers between devices  56.2 us (28%)
  waiting for transfers between devices  44.7 us (23%)
  other arithmetic  16 us (8%)
  local copies, waits for them, and re-layouts  10.6 us (5%)
    ppermute x31, starting transfers between devices, mover(): return lambda a: lax.ppermute(a, AXES, pairs)  37.5 us
    ppermute x31, waiting for transfers between devices, mover(): return lambda a: lax.ppermute(a, AXES, pairs)  31.4 us
    pallas_call x2, Pallas kernels, hidden_terms(): pl.pallas_call(hidden_kernel, out_shape=pltpu.HBM((4, rows, wide // 4), B...  13 us
    pallas_call x1, Pallas kernels, weight_terms(): pl.pallas_call(weight_kernel, out_shape=shapes, grid_spec=pltpu.PrefetchS...  12.5 us
    pallas_call x1, Pallas kernels, weight_here(): pl.pallas_call(here_kernel, out_shape=pltpu.HBM((ch, 4 * feat), F32), gri...  10.3 us
    pallas_call x1, Pallas kernels, grad_z_of(): pl.pallas_call(functools.partial(grad_z_kernel, scale=2.0 / rows), out_sh...  7.26 us
    pallas_call x2, Pallas kernels, stacked(): pl.pallas_call(stack_kernel, out_shape=pltpu.HBM((rows, sources[0].shape[...  6.28 us
    pallas_call x1, Pallas kernels, moments(): pl.pallas_call(moments_kernel, out_shape=pltpu.HBM((4, ch // 4 + 16, ch),...  6.03 us
  transfers between devices with their start and end apart: 35, of which 10 were waited for; matrix products, arithmetic and copies ran while one was open for 10% of the time, Pallas kernels for 31%

profile of v2, /device:TPU:2, one launch (start us, length us, event | category | flops | bytes accessed | tf_op | source)
XLA Modules:
  0.0 196.7 jit_solution(8345331864506549353)
XLA Ops:
  2.6 6.0 %shard_map.77 = bf16[4,144,512]{2,1,0:T(8,128)(2,1)} custom-call(bf16[1024,512]{1,0:T(8,128)(2,1)} %z_ref.3, bf16[1024,512]{1,0:T(8,128)(2,1)} %g_ref.3, f32[512,512]{1,0:T(8,128)} %u_ref.7), custom_call_target="tpu_custom_call" | custom-call | flops 2147483648 | bytes 3670016 | tf_op jit(solution)/shard_map/pallas_call | solution.py:103
  13.0 2.2 %collective-permute-start.6 = (bf16[64,4096]{1,0:T(8,128)(2,1)S(1)}, bf16[64,4096]{1,0:T(8,128)(2,1)S(1)}, u32[]{:S(2)}, u32[]{:S(2)}) collective-permute-start(bf16[64,4096]{1,0:T(8,128)(2,1)S(1)} %get-tuple-element.108), channel_id=1, source_target_pairs={{0,66},{1,67},{2,64},{3,65},{4,70},{5,71},{6,68},{7,69},{8,74},{9,... | collective-permute-start | bytes 1572872 | tf_op jit(solution)/shard_map/ppermute | solution.py:30
  15.2 4.5 %all-to-all-start = ((bf16[4,144,512]{2,1,0:T(8,128)(2,1)}), bf16[4,144,512]{2,1,0:T(8,128)(2,1)S(1)}, u32[]{:S(2)}, u32[]{:S(2)}) async-start(bf16[4,144,512]{2,1,0:T(8,128)(2,1)} %shard_map.77), calls=%async_computation | async-start | bytes 1179648 | tf_op jit(solution)/shard_map/all_to_all | solution.py:469
  19.6 3.4 %collective-permute-start.3 = (bf16[1024,128]{1,0:T(8,128)(2,1)S(1)}, bf16[1024,128]{1,0:T(8,128)(2,1)}, u32[]{:S(2)}, u32[]{:S(2)}) collective-permute-start(bf16[1024,128]{1,0:T(8,128)(2,1)S(1)} %get-tuple-element.59), channel_id=1, source_target_pairs={{0,2},{1,3},{2,0},{3,1},{4,6},{5,7},{6,4},{7,5},{8,10},{9,11},{10,... | collective-permute-start | bytes 786440 | tf_op jit(solution)/shard_map/ppermute | solution.py:30
  24.3 5.7 %all-to-all-done.got_ref = bf16[4,144,512]{2,1,0:T(8,128)(2,1)S(1)} async-done(((bf16[4,144,512]{2,1,0:T(8,128)(2,1)}), bf16[4,144,512]{2,1,0:T(8,128)(2,1)S(1)}, u32[]{:S(2)}, u32[]{:S(2)}) %all-to-all-start) | async-done | bytes 589856 | tf_op jit(solution)/shard_map/all_to_all | solution.py:469
  35.8 5.1 %shard_map.80 = (f32[512,512]{1,0:T(8,128)}, f32[1024,512]{1,0:T(8,128)}) custom-call(f32[512,512]{1,0:T(8,128)} %u_ref.7, f32[1,512]{1,0:T(1,128)S(1)} %bitcast.24, bf16[1024,512]{1,0:T(8,128)(2,1)} %g_ref.3), custom_call_target="tpu_custom_call" | custom-call | flops 1879048192 | bytes 5242880 | tf_op jit(solution)/shard_map/pallas_call | solution.py:190
  43.2 3.0 %shard_map.81 = (bf16[4,128,512]{2,1,0:T(8,128)(2,1)}, f32[8,512]{1,0:T(8,128)}) custom-call(s32[1]{0:T(128)} %bitcast.6.y_ref, f32[128,512]{1,0:T(8,128)} %get-tuple-element.52.quarter_ref, bf16[192,512]{1,0:T(8,128)(2,1)} %get-tuple-element.53.sent_ref, bf16[192,512]{1,0:T(8,128)(2,1)} %copy-done.10, f32[512,512]{1,0:T(8,128)} %u_ref.7, f32[512,512]{1,0:T(8,128)} %u_ref.7, ...), custom_call_target="tpu_custom_call" | custom-call | tf_op jit(solution)/shard_map/pallas_call | solution.py:158
  46.2 4.5 %all-to-all-start.1 = ((bf16[4,128,512]{2,1,0:T(8,128)(2,1)}), bf16[4,128,512]{2,1,0:T(8,128)(2,1)}, u32[]{:S(2)}, u32[]{:S(2)}) async-start(bf16[4,128,512]{2,1,0:T(8,128)(2,1)} %get-tuple-element.62), calls=%async_computation.1 | async-start | bytes 1048576 | tf_op jit(solution)/shard_map/all_to_all | solution.py:487
  52.8 2.1 %collective-permute-start.11 = (bf16[2,2048,128]{2,1,0:T(8,128)(2,1)S(1)}, bf16[2,2048,128]{2,1,0:T(8,128)(2,1)S(1)}, u32[]{:S(2)}, u32[]{:S(2)}) collective-permute-start(bf16[2,2048,128]{2,1,0:T(8,128)(2,1)S(1)} %pad_maximum_fusion.1.own_ref), channel_id=1, source_target_pairs={{0,16},{1,17},{2,18},{3,19},{4,20},{5,21},{6,22},{7,23},{8,24},{9,... | collective-permute-start | bytes 3145736 | tf_op jit(solution)/shard_map/ppermute | solution.py:30
  56.2 5.5 %all-to-all-done.1 = bf16[4,128,512]{2,1,0:T(8,128)(2,1)} async-done(((bf16[4,128,512]{2,1,0:T(8,128)(2,1)}), bf16[4,128,512]{2,1,0:T(8,128)(2,1)}, u32[]{:S(2)}, u32[]{:S(2)}) %all-to-all-start.1) | async-done | bytes 524320 | tf_op jit(solution)/shard_map/all_to_all | solution.py:487
  63.5 7.3 %shard_map.83 = (bf16[1024,512]{1,0:T(8,128)(2,1)}, bf16[512,1024]{1,0:T(8,128)(2,1)}) custom-call(f32[512,512]{1,0:T(8,128)} %u_ref.7, bf16[512,512]{1,0:T(8,128)(2,1)} %bitcast.9.inner_ref, bf16[1024,512]{1,0:T(8,128)(2,1)} %z_ref.3, f32[1024,512]{1,0:T(8,128)} %get-tuple-element.65.first_ref, f32[512,512]{1,0:T(8,128)} %get-tuple-element.66.wsum_ref, ...), custom_call_target="tpu_custom_call" | custom-call | flops 2415919104 | bytes 6815744 | tf_op jit(solution)/shard_map/pallas_call | solution.py:214
  70.7 2.2 %collective-permute-start.10 = (bf16[1024,512]{1,0:T(8,128)(2,1)}, bf16[1024,512]{1,0:T(8,128)(2,1)}, u32[]{:S(2)}, u32[]{:S(2)}) collective-permute-start(bf16[1024,512]{1,0:T(8,128)(2,1)} %get-tuple-element.91.refs_0_), channel_id=1, source_target_pairs={{0,66},{1,67},{2,64},{3,65},{4,70},{5,71},{6,68},{7,69},{8,74},{9,... | collective-permute-start | bytes 3145736 | tf_op jit(solution)/shard_map/ppermute | solution.py:30
  74.0 8.2 %collective-permute-done.11.left_ref = bf16[2,2048,128]{2,1,0:T(8,128)(2,1)S(1)} collective-permute-done((bf16[2,2048,128]{2,1,0:T(8,128)(2,1)S(1)}, bf16[2,2048,128]{2,1,0:T(8,128)(2,1)S(1)}, u32[]{:S(2)}, u32[]{:S(2)}) %collective-permute-start.11) | collective-permute-done | bytes 1048608 | tf_op jit(solution)/shard_map/ppermute | solution.py:30
  85.4 2.8 %collective-permute-start.14 = (bf16[1,2048,128]{2,1,0:T(8,128)(2,1)}, bf16[1,2048,128]{2,1,0:T(8,128)(2,1)}, u32[]{:S(2)}, u32[]{:S(2)}) collective-permute-start(bf16[1,2048,128]{2,1,0:T(8,128)(2,1)} %slice.51), channel_id=1, source_target_pairs={{0,48},{1,49},{2,50},{3,51},{4,52},{5,53},{6,54},{7,55},{8,56},{9,... | collective-permute-start | bytes 1572872 | tf_op jit(solution)/shard_map/ppermute | solution.py:30
  88.4 10.3 %shard_map.84.own_ref = f32[512,4096]{1,0:T(8,128)} custom-call(s32[6]{0:T(128)S(1)} %stack.63.idx_ref, bf16[512,1024]{1,0:T(8,128)(2,1)} %get-tuple-element.74.p_ref, bf16[1024,8192]{1,0:T(8,128)(2,1)} %own_ref), custom_call_target="tpu_custom_call" | custom-call | flops 4294967296 | bytes 16777216 | tf_op jit(solution)/shard_map/pallas_call | solution.py:377
  98.7 2.4 %shard_map.85.refs_4_.refs_6_ = bf16[2048,1024]{1,0:T(8,128)(2,1)S(1)} custom-call(s32[8]{0:T(128)S(1)} %stack.75.idx_ref, bf16[2,2048,128]{2,1,0:T(8,128)(2,1)S(1)} %pad_maximum_fusion.1.own_ref, bf16[2,2048,128]{2,1,0:T(8,128)(2,1)} %collective-permute-done.12.right_ref, bf16[1,2048,128]{2,1,0:T(8,128)(2,1)} %collective-permute-done.13.two_a_ref, ...), custom_call_target="tpu_custom_call" | custom-call | tf_op jit(solution)/shard_map/pallas_call | solution.py:289
  101.1 5.2 %shard_map.86.hx_ref = bf16[512,4096]{1,0:T(8,128)(2,1)} custom-call(bf16[128,4096]{1,0:T(8,128)(2,1)S(1)} %copy-done.3, bf16[128,4096]{1,0:T(8,128)(2,1)S(1)} %copy-done.5, bf16[128,4096]{1,0:T(8,128)(2,1)} %collective-permute-done.15.refs_2_, bf16[128,4096]{1,0:T(8,128)(2,1)} %collective-permute-done.7.refs_3_), custom_call_target="tpu_custom_call" | custom-call | tf_op jit(solution)/shard_map/pallas_call | solution.py:309
  106.9 2.8 %collective-permute-done.16.refs_1_ = bf16[1024,512]{1,0:T(8,128)(2,1)S(1)} collective-permute-done((bf16[1024,512]{1,0:T(8,128)(2,1)S(1)}, bf16[1024,512]{1,0:T(8,128)(2,1)S(1)}, u32[]{:S(2)}, u32[]{:S(2)}) %collective-permute-start.16) | collective-permute-done | bytes 1048608 | tf_op jit(solution)/shard_map/ppermute | solution.py:30
  110.8 7.1 %shard_map.87 = bf16[4,1024,256]{2,1,0:T(8,128)(2,1)} custom-call(bf16[1024,512]{1,0:T(8,128)(2,1)S(1)} %collective-permute-done.9.refs_0_.q_ref, bf16[1024,512]{1,0:T(8,128)(2,1)S(1)} %collective-permute-done.16.refs_1_, bf16[1024,512]{1,0:T(8,128)(2,1)} %collective-permute-done.10.refs_2_, bf16[1024,512]{1,0:T(8,128)(2,1)S(1)} %collective-permute-done.17.refs_3_, ...), custom_call_target="tpu_custom_call" | custom-call | flops 4294967296 | bytes 10485760 | tf_op jit(solution)/shard_map/pallas_call | solution.py:362
  118.0 5.0 %all-to-all-start.2 = ((bf16[4,1024,256]{2,1,0:T(8,128)(2,1)}), bf16[4,1024,256]{2,1,0:T(8,128)(2,1)}, u32[]{:S(2)}, u32[]{:S(2)}) async-start(bf16[4,1024,256]{2,1,0:T(8,128)(2,1)} %shard_map.87), calls=%async_computation.2 | async-start | bytes 4194304 | tf_op jit(solution)/shard_map/all_to_all | solution.py:515
  124.6 3.5 %collective-permute-start.24 = (bf16[512,512]{1,0:T(8,128)(2,1)S(1)}, bf16[512,512]{1,0:T(8,128)(2,1)S(1)}, u32[]{:S(2)}, u32[]{:S(2)}) collective-permute-start(bf16[512,512]{1,0:T(8,128)(2,1)S(1)} %slice.59), channel_id=1, source_target_pairs={{0,66},{1,67},{2,64},{3,65},{4,70},{5,71},{6,68},{7,69},{8,74},{9,... | collective-permute-start | bytes 1572872 | tf_op jit(solution)/shard_map/ppermute | solution.py:30
  128.1 12.5 %shard_map.88 = (bf16[512,1024]{1,0:T(8,128)(2,1)}, bf16[512,1024]{1,0:T(8,128)(2,1)}, f32[512,1024]{1,0:T(8,128)}, f32[256,1024]{1,0:T(8,128)}, f32[256,1024]{1,0:T(8,128)}) custom-call(s32[6]{0:T(128)S(1)} %stack.63.idx_ref, bf16[1024,512]{1,0:T(8,128)(2,1)S(1)} %collective-permute-done.9.refs_0_.q_ref, f32[512,4096]{1,0:T(8,128)} %shard_map.84.own_ref, ...), custom_call_target="tpu_custom_call" | custom-call | flops 4294967296 | bytes 23068672 | tf_op jit(solution)/shard_map/pallas_call | solution.py:418
  141.3 3.2 %collective-permute-start.19 = (bf16[512,1024]{1,0:T(8,128)(2,1)}, bf16[512,1024]{1,0:T(8,128)(2,1)}, u32[]{:S(2)}, u32[]{:S(2)}) collective-permute-start(bf16[512,1024]{1,0:T(8,128)(2,1)} %get-tuple-element.87), channel_id=1, source_target_pairs={{0,48},{1,49},{2,50},{3,51},{4,52},{5,53},{6,54},{7,55},{8,56},{9,... | collective-permute-start | bytes 3145736 | tf_op jit(solution)/shard_map/ppermute | solution.py:30
  144.5 5.9 %shard_map.89 = bf16[4,1024,256]{2,1,0:T(8,128)(2,1)} custom-call(bf16[1024,512]{1,0:T(8,128)(2,1)S(1)} %copy-done.6, bf16[1024,512]{1,0:T(8,128)(2,1)S(1)} %collective-permute-done.25.refs_1_, bf16[512,512]{1,0:T(8,128)(2,1)S(1)} %collective-permute-done.23.refs_2_, bf16[512,512]{1,0:T(8,128)(2,1)S(1)} %collective-permute-done.24.refs_3_, ...), custom_call_target="tpu_custom_call" | custom-call | flops 4294967296 | bytes 10485760 | tf_op jit(solution)/shard_map/pallas_call | solution.py:362
  150.4 4.8 %all-to-all-start.3 = ((bf16[4,1024,256]{2,1,0:T(8,128)(2,1)}), bf16[4,1024,256]{2,1,0:T(8,128)(2,1)S(1)}, u32[]{:S(2)}, u32[]{:S(2)}) async-start(bf16[4,1024,256]{2,1,0:T(8,128)(2,1)} %shard_map.89), calls=%async_computation.3 | async-start | bytes 4194304 | tf_op jit(solution)/shard_map/all_to_all | solution.py:525
  155.2 2.2 %reduce_sum.24 = bf16[1024,256]{1,0:T(8,128)(2,1)S(1)} reduce(bf16[4,1024,256]{2,1,0:T(8,128)(2,1)} %all-to-all-done.2, bf16[]{:T(256)} %constant.124.clone.1), dimensions={0}, to_apply=%region_0.1 | reduce | flops 786432 | bytes 2621442 | tf_op jit(solution)/shard_map/reduce_sum | solution.py:526
  157.3 10.4 %collective-permute-done.19 = bf16[512,1024]{1,0:T(8,128)(2,1)} collective-permute-done((bf16[512,1024]{1,0:T(8,128)(2,1)}, bf16[512,1024]{1,0:T(8,128)(2,1)}, u32[]{:S(2)}, u32[]{:S(2)}) %collective-permute-start.19) | collective-permute-done | bytes 1048608 | tf_op jit(solution)/shard_map/ppermute | solution.py:30
  167.8 2.3 %add_convert_fusion.1 = bf16[256,1024]{1,0:T(8,128)(2,1)} fusion(f32[256,1024]{1,0:T(8,128)} %get-tuple-element.90, bf16[512,1024]{1,0:T(8,128)(2,1)} %collective-permute-done.19), kind=kLoop, calls=%fused_computation.5 | loop fusion | flops 786432 | bytes 2097152 | tf_op jit(solution)/shard_map/convert_element_type | solution.py:44
  170.1 3.7 %collective-permute-start.22 = (bf16[256,1024]{1,0:T(8,128)(2,1)}, bf16[256,1024]{1,0:T(8,128)(2,1)S(1)}, u32[]{:S(2)}, u32[]{:S(2)}) collective-permute-start(bf16[256,1024]{1,0:T(8,128)(2,1)} %add_convert_fusion.1), channel_id=1, source_target_pairs={{0,48},{1,49},{2,50},{3,51},{4,52},{5,53},{6,54},{7,55},{8,56},{9,... | collective-permute-start | bytes 1572872 | tf_op jit(solution)/shard_map/ppermute | solution.py:30
  181.0 3.4 %collective-permute-done.30 = bf16[1024,128]{1,0:T(8,128)(2,1)} collective-permute-done((bf16[1024,128]{1,0:T(8,128)(2,1)}, bf16[1024,128]{1,0:T(8,128)(2,1)}, u32[]{:S(2)}, u32[]{:S(2)}) %collective-permute-start.30) | collective-permute-done | bytes 262176 | tf_op jit(solution)/shard_map/ppermute | solution.py:30
  186.5 4.0 %collective-permute-done.21 = bf16[256,1024]{1,0:T(8,128)(2,1)} collective-permute-done((bf16[256,1024]{1,0:T(8,128)(2,1)}, bf16[256,1024]{1,0:T(8,128)(2,1)}, u32[]{:S(2)}, u32[]{:S(2)}) %collective-permute-start.21) | collective-permute-done | bytes 524320 | tf_op jit(solution)/shard_map/ppermute | solution.py:30
  190.5 2.5 %add_convert_fusion.2 = (bf16[256,1024]{1,0:T(8,128)(2,1)S(1)}, bf16[256,1024]{1,0:T(8,128)(2,1)S(1)}) fusion(bf16[256,1024]{1,0:T(8,128)(2,1)} %collective-permute-done.21, f32[512,1024]{1,0:T(8,128)} %get-tuple-element.86, bf16[512,1024]{1,0:T(8,128)(2,1)} %collective-permute-done.19, bf16[256,1024]{1,0:T(8,128)(2,1)S(1)} %collective-permute-done.22, ...), kind=kLoop, calls=%fused_computation.6 | loop fusion | flops 2621440 | bytes 5242880 | tf_op jit(solution)/shard_map/convert.2
  (105 shorter events, 42.0 us)
Async XLA Ops:
  2.2 6.4 %collective-permute-start = (bf16[512,512]{1,0:T(8,128)(2,1)S(1)}, bf16[512,512]{1,0:T(8,128)(2,1)S(1)}, u32[]{:S(2)}, u32[]{:S(2)}) collective-permute-start(bf16[512,512]{1,0:T(8,128)(2,1)S(1)} %get-tuple-element.50), channel_id=1, source_target_pairs={{0,1},{1,0},{2,3},{3,2},{4,5},{5,4},{6,7},{7,6},{8,9},{9,8},{10,11... | collective-permute-start | bytes 1572872 | tf_op jit(solution)/shard_map/ppermute | solution.py:30
  11.0 21.8 %collective-permute-start.5 = (bf16[64,4096]{1,0:T(8,128)(2,1)S(1)}, bf16[64,4096]{1,0:T(8,128)(2,1)S(1)}, u32[]{:S(2)}, u32[]{:S(2)}) collective-permute-start(bf16[64,4096]{1,0:T(8,128)(2,1)S(1)} %get-tuple-element.109), channel_id=1, source_target_pairs={{0,64},{1,65},{2,66},{3,67},{4,68},{5,69},{6,70},{7,71},{8,72},{9,... | collective-permute-start | bytes 1572872 | tf_op jit(solution)/shard_map/ppermute | solution.py:30
  13.0 19.8 %collective-permute-start.6 = (bf16[64,4096]{1,0:T(8,128)(2,1)S(1)}, bf16[64,4096]{1,0:T(8,128)(2,1)S(1)}, u32[]{:S(2)}, u32[]{:S(2)}) collective-permute-start(bf16[64,4096]{1,0:T(8,128)(2,1)S(1)} %get-tuple-element.108), channel_id=1, source_target_pairs={{0,66},{1,67},{2,64},{3,65},{4,70},{5,71},{6,68},{7,69},{8,74},{9,... | collective-permute-start | bytes 1572872 | tf_op jit(solution)/shard_map/ppermute | solution.py:30
  15.2 14.8 %all-to-all-start = ((bf16[4,144,512]{2,1,0:T(8,128)(2,1)}), bf16[4,144,512]{2,1,0:T(8,128)(2,1)S(1)}, u32[]{:S(2)}, u32[]{:S(2)}) async-start(bf16[4,144,512]{2,1,0:T(8,128)(2,1)} %shard_map.77), calls=%async_computation | async-start | bytes 1179648 | tf_op jit(solution)/shard_map/all_to_all | solution.py:469
  19.6 15.7 %collective-permute-start.2 = (bf16[1024,128]{1,0:T(8,128)(2,1)}, bf16[1024,128]{1,0:T(8,128)(2,1)}, u32[]{:S(2)}, u32[]{:S(2)}) collective-permute-start(bf16[1024,128]{1,0:T(8,128)(2,1)} %get-tuple-element.58), channel_id=1, source_target_pairs={{0,64},{1,65},{2,66},{3,67},{4,68},{5,69},{6,70},{7,71},{8,72},{9,... | collective-permute-start | bytes 786440 | tf_op jit(solution)/shard_map/ppermute | solution.py:30
  19.6 21.4 %collective-permute-start.3 = (bf16[1024,128]{1,0:T(8,128)(2,1)S(1)}, bf16[1024,128]{1,0:T(8,128)(2,1)}, u32[]{:S(2)}, u32[]{:S(2)}) collective-permute-start(bf16[1024,128]{1,0:T(8,128)(2,1)S(1)} %get-tuple-element.59), channel_id=1, source_target_pairs={{0,2},{1,3},{2,0},{3,1},{4,6},{5,7},{6,4},{7,5},{8,10},{9,11},{10,... | collective-permute-start | bytes 786440 | tf_op jit(solution)/shard_map/ppermute | solution.py:30
  23.0 18.1 %collective-permute-start.4 = (bf16[1024,128]{1,0:T(8,128)(2,1)S(1)}, bf16[1024,128]{1,0:T(8,128)(2,1)}, u32[]{:S(2)}, u32[]{:S(2)}) collective-permute-start(bf16[1024,128]{1,0:T(8,128)(2,1)S(1)} %get-tuple-element.60), channel_id=1, source_target_pairs={{0,66},{1,67},{2,64},{3,65},{4,70},{5,71},{6,68},{7,69},{8,74},{9,... | collective-permute-start | bytes 786440 | tf_op jit(solution)/shard_map/ppermute | solution.py:30
  32.7 9.8 %collective-permute-start.1 = (bf16[192,512]{1,0:T(8,128)(2,1)}, bf16[192,512]{1,0:T(8,128)(2,1)S(1)}, u32[]{:S(2)}, u32[]{:S(2)}) collective-permute-start(bf16[192,512]{1,0:T(8,128)(2,1)} %get-tuple-element.53.sent_ref), channel_id=1, source_target_pairs={{0,64},{1,65},{2,66},{3,67},{4,68},{5,69},{6,70},{7,71},{8,72},{9,... | collective-permute-start | bytes 589832 | tf_op jit(solution)/shard_map/ppermute | solution.py:30
  33.8 27.9 %collective-permute-start.7 = (bf16[128,4096]{1,0:T(8,128)(2,1)}, bf16[128,4096]{1,0:T(8,128)(2,1)}, u32[]{:S(2)}, u32[]{:S(2)}) collective-permute-start(bf16[128,4096]{1,0:T(8,128)(2,1)} %shard_map.82.refs_0_), channel_id=1, source_target_pairs={{0,4},{1,5},{2,6},{3,7},{4,8},{5,9},{6,10},{7,11},{8,12},{9,13},{1... | collective-permute-start | bytes 3145736 | tf_op jit(solution)/shard_map/ppermute | solution.py:30
  35.3 26.4 %collective-permute-start.8 = (bf16[128,4096]{1,0:T(8,128)(2,1)}, bf16[128,4096]{1,0:T(8,128)(2,1)S(1)}, u32[]{:S(2)}, u32[]{:S(2)}) collective-permute-start(bf16[128,4096]{1,0:T(8,128)(2,1)} %shard_map.82.refs_0_), channel_id=1, source_target_pairs={{0,12},{1,13},{2,14},{3,15},{4,0},{5,1},{6,2},{7,3},{8,4},{9,5},{1... | collective-permute-start | bytes 3145736 | tf_op jit(solution)/shard_map/ppermute | solution.py:30
  46.2 15.5 %all-to-all-start.1 = ((bf16[4,128,512]{2,1,0:T(8,128)(2,1)}), bf16[4,128,512]{2,1,0:T(8,128)(2,1)}, u32[]{:S(2)}, u32[]{:S(2)}) async-start(bf16[4,128,512]{2,1,0:T(8,128)(2,1)} %get-tuple-element.62), calls=%async_computation.1 | async-start | bytes 1048576 | tf_op jit(solution)/shard_map/all_to_all | solution.py:487
  52.8 29.4 %collective-permute-start.11 = (bf16[2,2048,128]{2,1,0:T(8,128)(2,1)S(1)}, bf16[2,2048,128]{2,1,0:T(8,128)(2,1)S(1)}, u32[]{:S(2)}, u32[]{:S(2)}) collective-permute-start(bf16[2,2048,128]{2,1,0:T(8,128)(2,1)S(1)} %pad_maximum_fusion.1.own_ref), channel_id=1, source_target_pairs={{0,16},{1,17},{2,18},{3,19},{4,20},{5,21},{6,22},{7,23},{8,24},{9,... | collective-permute-start | bytes 3145736 | tf_op jit(solution)/shard_map/ppermute | solution.py:30
  54.9 27.3 %collective-permute-start.12 = (bf16[2,2048,128]{2,1,0:T(8,128)(2,1)S(1)}, bf16[2,2048,128]{2,1,0:T(8,128)(2,1)}, u32[]{:S(2)}, u32[]{:S(2)}) collective-permute-start(bf16[2,2048,128]{2,1,0:T(8,128)(2,1)S(1)} %pad_maximum_fusion.1.own_ref), channel_id=1, source_target_pairs={{0,48},{1,49},{2,50},{3,51},{4,52},{5,53},{6,54},{7,55},{8,56},{9,... | collective-permute-start | bytes 3145736 | tf_op jit(solution)/shard_map/ppermute | solution.py:30
  61.7 39.4 %collective-permute-start.15 = (bf16[128,4096]{1,0:T(8,128)(2,1)}, bf16[128,4096]{1,0:T(8,128)(2,1)}, u32[]{:S(2)}, u32[]{:S(2)}) collective-permute-start(bf16[128,4096]{1,0:T(8,128)(2,1)} %collective-permute-done.7.refs_3_), channel_id=1, source_target_pairs={{0,4},{1,5},{2,6},{3,7},{4,8},{5,9},{6,10},{7,11},{8,12},{9,13},{1... | collective-permute-start | bytes 3145736 | tf_op jit(solution)/shard_map/ppermute | solution.py:30
  70.7 35.6 %collective-permute-start.10 = (bf16[1024,512]{1,0:T(8,128)(2,1)}, bf16[1024,512]{1,0:T(8,128)(2,1)}, u32[]{:S(2)}, u32[]{:S(2)}) collective-permute-start(bf16[1024,512]{1,0:T(8,128)(2,1)} %get-tuple-element.91.refs_0_), channel_id=1, source_target_pairs={{0,66},{1,67},{2,64},{3,65},{4,70},{5,71},{6,68},{7,69},{8,74},{9,... | collective-permute-start | bytes 3145736 | tf_op jit(solution)/shard_map/ppermute | solution.py:30
  72.9 33.5 %collective-permute-start.9 = (bf16[1024,512]{1,0:T(8,128)(2,1)}, bf16[1024,512]{1,0:T(8,128)(2,1)S(1)}, u32[]{:S(2)}, u32[]{:S(2)}) collective-permute-start(bf16[1024,512]{1,0:T(8,128)(2,1)} %get-tuple-element.91.refs_0_), channel_id=1, source_target_pairs={{0,64},{1,65},{2,66},{3,67},{4,68},{5,69},{6,70},{7,71},{8,72},{9,... | collective-permute-start | bytes 3145736 | tf_op jit(solution)/shard_map/ppermute | solution.py:30
  83.1 15.6 %collective-permute-start.13 = (bf16[1,2048,128]{2,1,0:T(8,128)(2,1)}, bf16[1,2048,128]{2,1,0:T(8,128)(2,1)}, u32[]{:S(2)}, u32[]{:S(2)}) collective-permute-start(bf16[1,2048,128]{2,1,0:T(8,128)(2,1)} %slice.50), channel_id=1, source_target_pairs={{0,16},{1,17},{2,18},{3,19},{4,20},{5,21},{6,22},{7,23},{8,24},{9,... | collective-permute-start | bytes 1572872 | tf_op jit(solution)/shard_map/ppermute | solution.py:30
  85.4 13.3 %collective-permute-start.14 = (bf16[1,2048,128]{2,1,0:T(8,128)(2,1)}, bf16[1,2048,128]{2,1,0:T(8,128)(2,1)}, u32[]{:S(2)}, u32[]{:S(2)}) collective-permute-start(bf16[1,2048,128]{2,1,0:T(8,128)(2,1)} %slice.51), channel_id=1, source_target_pairs={{0,48},{1,49},{2,50},{3,51},{4,52},{5,53},{6,54},{7,55},{8,56},{9,... | collective-permute-start | bytes 1572872 | tf_op jit(solution)/shard_map/ppermute | solution.py:30
  106.4 4.4 %collective-permute-start.17 = (bf16[1024,512]{1,0:T(8,128)(2,1)}, bf16[1024,512]{1,0:T(8,128)(2,1)S(1)}, u32[]{:S(2)}, u32[]{:S(2)}) collective-permute-start(bf16[1024,512]{1,0:T(8,128)(2,1)} %collective-permute-done.10.refs_2_), channel_id=1, source_target_pairs={{0,1},{1,0},{2,3},{3,2},{4,5},{5,4},{6,7},{7,6},{8,9},{9,8},{10,11... | collective-permute-start | bytes 3145736 | tf_op jit(solution)/shard_map/ppermute | solution.py:30
  117.9 10.2 %collective-permute-start.18 = (bf16[512,4096]{1,0:T(8,128)(2,1)}, bf16[512,4096]{1,0:T(8,128)(2,1)}, u32[]{:S(2)}, u32[]{:S(2)}) collective-permute-start(bf16[512,4096]{1,0:T(8,128)(2,1)} %shard_map.86.hx_ref), channel_id=1, source_target_pairs={{0,1},{1,0},{2,3},{3,2},{4,5},{5,4},{6,7},{7,6},{8,9},{9,8},{10,11... | collective-permute-start | bytes 12582920 | tf_op jit(solution)/shard_map/ppermute | solution.py:30
  118.0 32.4 %all-to-all-start.2 = ((bf16[4,1024,256]{2,1,0:T(8,128)(2,1)}), bf16[4,1024,256]{2,1,0:T(8,128)(2,1)}, u32[]{:S(2)}, u32[]{:S(2)}) async-start(bf16[4,1024,256]{2,1,0:T(8,128)(2,1)} %shard_map.87), calls=%async_computation.2 | async-start | bytes 4194304 | tf_op jit(solution)/shard_map/all_to_all | solution.py:515
  124.2 16.4 %collective-permute-start.23 = (bf16[512,512]{1,0:T(8,128)(2,1)S(1)}, bf16[512,512]{1,0:T(8,128)(2,1)S(1)}, u32[]{:S(2)}, u32[]{:S(2)}) collective-permute-start(bf16[512,512]{1,0:T(8,128)(2,1)S(1)} %slice.58), channel_id=1, source_target_pairs={{0,64},{1,65},{2,66},{3,67},{4,68},{5,69},{6,70},{7,71},{8,72},{9,... | collective-permute-start | bytes 1572872 | tf_op jit(solution)/shard_map/ppermute | solution.py:30
  124.6 16.0 %collective-permute-start.24 = (bf16[512,512]{1,0:T(8,128)(2,1)S(1)}, bf16[512,512]{1,0:T(8,128)(2,1)S(1)}, u32[]{:S(2)}, u32[]{:S(2)}) collective-permute-start(bf16[512,512]{1,0:T(8,128)(2,1)S(1)} %slice.59), channel_id=1, source_target_pairs={{0,66},{1,67},{2,64},{3,65},{4,70},{5,71},{6,68},{7,69},{8,74},{9,... | collective-permute-start | bytes 1572872 | tf_op jit(solution)/shard_map/ppermute | solution.py:30
  128.1 16.4 %collective-permute-start.25 = (bf16[1024,512]{1,0:T(8,128)(2,1)S(1)}, bf16[1024,512]{1,0:T(8,128)(2,1)S(1)}, u32[]{:S(2)}, u32[]{:S(2)}) collective-permute-start(bf16[1024,512]{1,0:T(8,128)(2,1)S(1)} %copy-done.6), channel_id=1, source_target_pairs={{0,1},{1,0},{2,3},{3,2},{4,5},{5,4},{6,7},{7,6},{8,9},{9,8},{10,11... | collective-permute-start | bytes 3145736 | tf_op jit(solution)/shard_map/ppermute | solution.py:30
  141.3 26.5 %collective-permute-start.19 = (bf16[512,1024]{1,0:T(8,128)(2,1)}, bf16[512,1024]{1,0:T(8,128)(2,1)}, u32[]{:S(2)}, u32[]{:S(2)}) collective-permute-start(bf16[512,1024]{1,0:T(8,128)(2,1)} %get-tuple-element.87), channel_id=1, source_target_pairs={{0,48},{1,49},{2,50},{3,51},{4,52},{5,53},{6,54},{7,55},{8,56},{9,... | collective-permute-start | bytes 3145736 | tf_op jit(solution)/shard_map/ppermute | solution.py:30
  144.5 29.3 %collective-permute-start.20 = (bf16[512,1024]{1,0:T(8,128)(2,1)}, bf16[512,1024]{1,0:T(8,128)(2,1)}, u32[]{:S(2)}, u32[]{:S(2)}) collective-permute-start(bf16[512,1024]{1,0:T(8,128)(2,1)} %get-tuple-element.89), channel_id=1, source_target_pairs={{0,16},{1,17},{2,18},{3,19},{4,20},{5,21},{6,22},{7,23},{8,24},{9,... | collective-permute-start | bytes 3145736 | tf_op jit(solution)/shard_map/ppermute | solution.py:30
  150.4 30.0 %all-to-all-start.3 = ((bf16[4,1024,256]{2,1,0:T(8,128)(2,1)}), bf16[4,1024,256]{2,1,0:T(8,128)(2,1)S(1)}, u32[]{:S(2)}, u32[]{:S(2)}) async-start(bf16[4,1024,256]{2,1,0:T(8,128)(2,1)} %shard_map.89), calls=%async_computation.3 | async-start | bytes 4194304 | tf_op jit(solution)/shard_map/all_to_all | solution.py:525
  170.1 16.4 %collective-permute-start.22 = (bf16[256,1024]{1,0:T(8,128)(2,1)}, bf16[256,1024]{1,0:T(8,128)(2,1)S(1)}, u32[]{:S(2)}, u32[]{:S(2)}) collective-permute-start(bf16[256,1024]{1,0:T(8,128)(2,1)} %add_convert_fusion.1), channel_id=1, source_target_pairs={{0,48},{1,49},{2,50},{3,51},{4,52},{5,53},{6,54},{7,55},{8,56},{9,... | collective-permute-start | bytes 1572872 | tf_op jit(solution)/shard_map/ppermute | solution.py:30
  175.8 14.7 %collective-permute-start.21 = (bf16[256,1024]{1,0:T(8,128)(2,1)}, bf16[256,1024]{1,0:T(8,128)(2,1)}, u32[]{:S(2)}, u32[]{:S(2)}) collective-permute-start(bf16[256,1024]{1,0:T(8,128)(2,1)} %add_convert_fusion.3), channel_id=1, source_target_pairs={{0,16},{1,17},{2,18},{3,19},{4,20},{5,21},{6,22},{7,23},{8,24},{9,... | collective-permute-start | bytes 1572872 | tf_op jit(solution)/shard_map/ppermute | solution.py:30
  176.5 7.9 %collective-permute-start.30 = (bf16[1024,128]{1,0:T(8,128)(2,1)}, bf16[1024,128]{1,0:T(8,128)(2,1)}, u32[]{:S(2)}, u32[]{:S(2)}) collective-permute-start(bf16[1024,128]{1,0:T(8,128)(2,1)} %get-tuple-element.115), channel_id=1, source_target_pairs={{0,64},{1,65},{2,66},{3,67},{4,68},{5,69},{6,70},{7,71},{8,72},{9,... | collective-permute-start | bytes 786440 | tf_op jit(solution)/shard_map/ppermute | solution.py:30
  176.6 17.8 %collective-permute-start.28 = (bf16[1024,128]{1,0:T(8,128)(2,1)S(1)}, bf16[1024,128]{1,0:T(8,128)(2,1)}, u32[]{:S(2)}, u32[]{:S(2)}) collective-permute-start(bf16[1024,128]{1,0:T(8,128)(2,1)S(1)} %get-tuple-element.114), channel_id=1, source_target_pairs={{0,66},{1,67},{2,64},{3,65},{4,70},{5,71},{6,68},{7,69},{8,74},{9,... | collective-permute-start | bytes 786440 | tf_op jit(solution)/shard_map/ppermute | solution.py:30
  185.4 9.0 %collective-permute-start.29 = (bf16[1024,128]{1,0:T(8,128)(2,1)S(1)}, bf16[1024,128]{1,0:T(8,128)(2,1)S(1)}, u32[]{:S(2)}, u32[]{:S(2)}) collective-permute-start(bf16[1024,128]{1,0:T(8,128)(2,1)S(1)} %get-tuple-element.116), channel_id=1, source_target_pairs={{0,2},{1,3},{2,0},{3,1},{4,6},{5,7},{6,4},{7,5},{8,10},{9,11},{10,... | collective-permute-start | bytes 786440 | tf_op jit(solution)/shard_map/ppermute | solution.py:30
  (15 other events, 113.4 us)

commit v3 on v2

--- a/solution.py
+++ b/solution.py
@@ -435,15 +435,42 @@
     )(order, q_own, *hbm(w_here, h_x, h_k))
 
 
+def finish_kernel(b0_ref, down_ref, up_ref, down2_ref, up2_ref, out_ref):
+    h = down2_ref.shape[0]
+    lower = b0_ref[:h, :] + up_ref[h:, :].astype(F32) + down2_ref[...].astype(F32)
+    upper = b0_ref[h:, :] + down_ref[:h, :].astype(F32) + up2_ref[...].astype(F32)
+    out_ref[:, :h] = bf(lower.T)
+    out_ref[:, h:] = bf(upper.T)
+
+
 def ring_finish(terms, first, up, down):
     _, _, b0, b1, b3 = terms
     from_down, from_up = first
     h = b1.shape[0]
     from_down2 = up(bf(b1 + from_down[h:].astype(F32)))
     from_up2 = down(bf(b3 + from_up[:h].astype(F32)))
-    lower = b0[:h] + from_up[h:].astype(F32) + from_down2.astype(F32)
-    upper = b0[h:] + from_down[:h].astype(F32) + from_up2.astype(F32)
-    return jnp.concatenate([lower, upper])
+    return pl.pallas_call(
+        finish_kernel,
+        out_shape=jax.ShapeDtypeStruct(b0.shape[::-1], BF16),
+        compiler_params=params(16),
+    )(*hbm(b0, from_down, from_up), from_down2, from_up2)
+
+
+def placed_kernel(z_ref, *refs):
+    *pieces, out_ref = refs
+    for j, ref in enumerate(pieces):
+        wide = ref.shape[1]
+        out_ref[:, pl.ds(pl.multiple_of((z_ref[0] ^ j) * wide, wide), wide)] = ref[...]
+
+
+def placed(pieces, z):
+    rows, wide = pieces[0].shape
+    return pl.pallas_call(
+        placed_kernel,
+        out_shape=jax.ShapeDtypeStruct((rows, 4 * wide), BF16),
+        in_specs=[pl.BlockSpec(memory_space=pltpu.SMEM)] + [pl.BlockSpec(memory_space=pltpu.VMEM)] * 4,
+        compiler_params=params(8),
+    )(z.reshape(1), *pieces)
 
 
 def local(hidden, weight, embed, embed_grad, eigvec, eigval):
@@ -526,18 +553,11 @@
     s_par = bf(jnp.sum(par_got.astype(F32), axis=0))
     p1 = z_flip[1](s_par[:, :fs])
     p3 = z_flip[3](s_par[:, fs:])
-    w_sum = ring_finish(w_terms, w_first, y_up, y_down)
+    grad_weight = ring_finish(w_terms, w_first, y_up, y_down)
     s_own = bf(jnp.sum(own_got.astype(F32), axis=0))
     p0 = s_own[:, :fs]
     p2 = z_flip[2](s_own[:, fs:])
-    grad_weight = bf(w_sum.T)
-    odd = zlo == 1
-    u0, u1 = jnp.where(odd, p1, p0), jnp.where(odd, p0, p1)
-    u2, u3 = jnp.where(odd, p3, p2), jnp.where(odd, p2, p3)
-    low = jnp.concatenate([u0, u1], axis=1)
-    high = jnp.concatenate([u2, u3], axis=1)
-    up = zhi == 1
-    grad_hidden = jnp.concatenate([jnp.where(up, high, low), jnp.where(up, low, high)], axis=1)
+    grad_hidden = placed([p0, p1, p2, p3], z)
     return grad_weight, grad_hidden
 
 

time: 198 us -> 203 us (1.025)
  other arithmetic: 16 us -> 11.4 us
  Pallas kernels: 68.1 us -> 72.6 us
  waiting for transfers between devices: 44.7 us -> 49.1 us
    ppermute x31, waiting for transfers between devices: 31.4 us -> 38 us  [mover(): return lambda a: lax.ppermute(a, AXES, pairs)]
    pallas_call x0 -> x2, Pallas kernels: none -> 4.73 us  [the longest x1 3.57 us: ring_finish(): pl.pallas_call(finish_kernel, out_shape=jax.ShapeDtypeStruct(b0.shape[::-...]
    another operation x1 -> x0, other arithmetic: 2.5 us -> none
    select_n x3 -> x0, other arithmetic: 2.23 us -> none  [the longest x1 1 us: local(): u0, u1 = (jnp.where(odd, p1, p0), jnp.where(odd, p0, p1))]
    all_to_all x1, waiting for transfers between devices: 2.09 us -> 0.01 us  [local(): own_got = lax.all_to_all(own, 'chan', 0, 0, axis_index_groups=x_groups)]
    convert_element_type x3 -> x2, other arithmetic: 4.35 us -> 3.31 us  [bf(): return a.astype(BF16)]
    unnamed x25 -> x28, local copies, waits for them, and re-layouts: 4.07 us -> 3.71 us
  transfers between devices with their start and end apart: 35 -> 35, of which waited for: 10 -> 9; matrix products, arithmetic and copies ran while one was open for 10% -> 7% of each run, Pallas kernels for 31% -> 32%
where the time goes in v3:
time: 203 us; the launch traced here: 202 us
  Pallas kernels  72.6 us (36%)
  starting transfers between devices  57.6 us (28%)
  waiting for transfers between devices  49.1 us (24%)
  other arithmetic  11.4 us (6%)
  local copies, waits for them, and re-layouts  10.3 us (5%)
    ppermute x31, starting transfers between devices, mover(): return lambda a: lax.ppermute(a, AXES, pairs)  38.9 us
    ppermute x31, waiting for transfers between devices, mover(): return lambda a: lax.ppermute(a, AXES, pairs)  38 us
    pallas_call x2, Pallas kernels, hidden_terms(): pl.pallas_call(hidden_kernel, out_shape=pltpu.HBM((4, rows, wide // 4), B...  12.9 us
    pallas_call x1, Pallas kernels, weight_terms(): pl.pallas_call(weight_kernel, out_shape=shapes, grid_spec=pltpu.PrefetchS...  12.5 us
    pallas_call x1, Pallas kernels, weight_here(): pl.pallas_call(here_kernel, out_shape=pltpu.HBM((ch, 4 * feat), F32), gri...  10.2 us
    pallas_call x1, Pallas kernels, grad_z_of(): pl.pallas_call(functools.partial(grad_z_kernel, scale=2.0 / rows), out_sh...  7.23 us
    pallas_call x2, Pallas kernels, stacked(): pl.pallas_call(stack_kernel, out_shape=pltpu.HBM((rows, sources[0].shape[...  6.27 us
    pallas_call x1, Pallas kernels, moments(): pl.pallas_call(moments_kernel, out_shape=pltpu.HBM((4, ch // 4 + 16, ch),...  6.03 us
  transfers between devices with their start and end apart: 35, of which 9 were waited for; matrix products, arithmetic and copies ran while one was open for 7% of the time, Pallas kernels for 32%

profile of v3, /device:TPU:2, one launch (start us, length us, event | category | flops | bytes accessed | tf_op | source)
XLA Modules:
  0.0 202.2 jit_solution(4463238950834412007)
XLA Ops:
  2.6 6.0 %shard_map.77 = bf16[4,144,512]{2,1,0:T(8,128)(2,1)} custom-call(bf16[1024,512]{1,0:T(8,128)(2,1)} %z_ref.3, bf16[1024,512]{1,0:T(8,128)(2,1)} %g_ref.3, f32[512,512]{1,0:T(8,128)} %u_ref.7), custom_call_target="tpu_custom_call" | custom-call | flops 2147483648 | bytes 3670016 | tf_op jit(solution)/shard_map/pallas_call | solution.py:103
  13.7 2.2 %collective-permute-start.6 = (bf16[64,4096]{1,0:T(8,128)(2,1)S(1)}, bf16[64,4096]{1,0:T(8,128)(2,1)S(1)}, u32[]{:S(2)}, u32[]{:S(2)}) collective-permute-start(bf16[64,4096]{1,0:T(8,128)(2,1)S(1)} %get-tuple-element.100), channel_id=1, source_target_pairs={{0,66},{1,67},{2,64},{3,65},{4,70},{5,71},{6,68},{7,69},{8,74},{9,... | collective-permute-start | bytes 1572872 | tf_op jit(solution)/shard_map/ppermute | solution.py:30
  15.9 4.5 %all-to-all-start = ((bf16[4,144,512]{2,1,0:T(8,128)(2,1)}), bf16[4,144,512]{2,1,0:T(8,128)(2,1)S(1)}, u32[]{:S(2)}, u32[]{:S(2)}) async-start(bf16[4,144,512]{2,1,0:T(8,128)(2,1)} %shard_map.77), calls=%async_computation | async-start | bytes 1179648 | tf_op jit(solution)/shard_map/all_to_all | solution.py:496
  20.3 3.4 %collective-permute-start.3 = (bf16[1024,128]{1,0:T(8,128)(2,1)}, bf16[1024,128]{1,0:T(8,128)(2,1)}, u32[]{:S(2)}, u32[]{:S(2)}) collective-permute-start(bf16[1024,128]{1,0:T(8,128)(2,1)} %get-tuple-element.59), channel_id=1, source_target_pairs={{0,2},{1,3},{2,0},{3,1},{4,6},{5,7},{6,4},{7,5},{8,10},{9,11},{10,... | collective-permute-start | bytes 786440 | tf_op jit(solution)/shard_map/ppermute | solution.py:30
  25.0 5.7 %all-to-all-done.got_ref = bf16[4,144,512]{2,1,0:T(8,128)(2,1)S(1)} async-done(((bf16[4,144,512]{2,1,0:T(8,128)(2,1)}), bf16[4,144,512]{2,1,0:T(8,128)(2,1)S(1)}, u32[]{:S(2)}, u32[]{:S(2)}) %all-to-all-start) | async-done | bytes 589856 | tf_op jit(solution)/shard_map/all_to_all | solution.py:496
  36.5 5.1 %shard_map.80 = (f32[512,512]{1,0:T(8,128)}, f32[1024,512]{1,0:T(8,128)}) custom-call(f32[512,512]{1,0:T(8,128)} %u_ref.7, f32[1,512]{1,0:T(1,128)S(1)} %bitcast.23, bf16[1024,512]{1,0:T(8,128)(2,1)} %g_ref.3), custom_call_target="tpu_custom_call" | custom-call | flops 1879048192 | bytes 5242880 | tf_op jit(solution)/shard_map/pallas_call | solution.py:190
  43.9 3.0 %shard_map.81 = (bf16[4,128,512]{2,1,0:T(8,128)(2,1)}, f32[8,512]{1,0:T(8,128)}) custom-call(s32[1]{0:T(128)} %bitcast.6.y_ref, f32[128,512]{1,0:T(8,128)} %get-tuple-element.52.quarter_ref, bf16[192,512]{1,0:T(8,128)(2,1)} %get-tuple-element.53.sent_ref, bf16[192,512]{1,0:T(8,128)(2,1)} %copy-done.12, f32[512,512]{1,0:T(8,128)} %u_ref.7, f32[512,512]{1,0:T(8,128)} %u_ref.7, ...), custom_call_target="tpu_custom_call" | custom-call | tf_op jit(solution)/shard_map/pallas_call | solution.py:158
  46.9 4.5 %all-to-all-start.1 = ((bf16[4,128,512]{2,1,0:T(8,128)(2,1)}), bf16[4,128,512]{2,1,0:T(8,128)(2,1)}, u32[]{:S(2)}, u32[]{:S(2)}) async-start(bf16[4,128,512]{2,1,0:T(8,128)(2,1)} %get-tuple-element.62), calls=%async_computation.1 | async-start | bytes 1048576 | tf_op jit(solution)/shard_map/all_to_all | solution.py:514
  56.9 5.5 %all-to-all-done.1 = bf16[4,128,512]{2,1,0:T(8,128)(2,1)} async-done(((bf16[4,128,512]{2,1,0:T(8,128)(2,1)}), bf16[4,128,512]{2,1,0:T(8,128)(2,1)}, u32[]{:S(2)}, u32[]{:S(2)}) %all-to-all-start.1) | async-done | bytes 524320 | tf_op jit(solution)/shard_map/all_to_all | solution.py:514
  64.2 7.2 %shard_map.83 = (bf16[1024,512]{1,0:T(8,128)(2,1)}, bf16[512,1024]{1,0:T(8,128)(2,1)}) custom-call(f32[512,512]{1,0:T(8,128)} %u_ref.7, bf16[512,512]{1,0:T(8,128)(2,1)} %bitcast.9.inner_ref, bf16[1024,512]{1,0:T(8,128)(2,1)} %z_ref.3, f32[1024,512]{1,0:T(8,128)} %get-tuple-element.65.first_ref, f32[512,512]{1,0:T(8,128)} %get-tuple-element.66.wsum_ref, ...), custom_call_target="tpu_custom_call" | custom-call | flops 2415919104 | bytes 6815744 | tf_op jit(solution)/shard_map/pallas_call | solution.py:214
  71.4 2.2 %collective-permute-start.10 = (bf16[1024,512]{1,0:T(8,128)(2,1)}, bf16[1024,512]{1,0:T(8,128)(2,1)}, u32[]{:S(2)}, u32[]{:S(2)}) collective-permute-start(bf16[1024,512]{1,0:T(8,128)(2,1)} %get-tuple-element.91.refs_0_), channel_id=1, source_target_pairs={{0,66},{1,67},{2,64},{3,65},{4,70},{5,71},{6,68},{7,69},{8,74},{9,... | collective-permute-start | bytes 3145736 | tf_op jit(solution)/shard_map/ppermute | solution.py:30
  74.7 8.2 %collective-permute-done.11.left_ref = bf16[2,2048,128]{2,1,0:T(8,128)(2,1)S(1)} collective-permute-done((bf16[2,2048,128]{2,1,0:T(8,128)(2,1)S(1)}, bf16[2,2048,128]{2,1,0:T(8,128)(2,1)S(1)}, u32[]{:S(2)}, u32[]{:S(2)}) %collective-permute-start.11) | collective-permute-done | bytes 1048608 | tf_op jit(solution)/shard_map/ppermute | solution.py:30
  86.0 2.8 %collective-permute-start.14 = (bf16[1,2048,128]{2,1,0:T(8,128)(2,1)}, bf16[1,2048,128]{2,1,0:T(8,128)(2,1)}, u32[]{:S(2)}, u32[]{:S(2)}) collective-permute-start(bf16[1,2048,128]{2,1,0:T(8,128)(2,1)} %slice.39), channel_id=1, source_target_pairs={{0,48},{1,49},{2,50},{3,51},{4,52},{5,53},{6,54},{7,55},{8,56},{9,... | collective-permute-start | bytes 1572872 | tf_op jit(solution)/shard_map/ppermute | solution.py:30
  89.0 10.2 %shard_map.84.own_ref = f32[512,4096]{1,0:T(8,128)} custom-call(s32[6]{0:T(128)S(1)} %stack.63.idx_ref, bf16[512,1024]{1,0:T(8,128)(2,1)} %get-tuple-element.74.p_ref, bf16[1024,8192]{1,0:T(8,128)(2,1)} %own_ref), custom_call_target="tpu_custom_call" | custom-call | flops 4294967296 | bytes 16777216 | tf_op jit(solution)/shard_map/pallas_call | solution.py:377
  99.2 2.4 %shard_map.85.refs_4_.refs_6_ = bf16[2048,1024]{1,0:T(8,128)(2,1)S(1)} custom-call(s32[8]{0:T(128)S(1)} %stack.75.idx_ref, bf16[2,2048,128]{2,1,0:T(8,128)(2,1)S(1)} %pad_maximum_fusion.1.own_ref, bf16[2,2048,128]{2,1,0:T(8,128)(2,1)} %collective-permute-done.12.right_ref, bf16[1,2048,128]{2,1,0:T(8,128)(2,1)} %collective-permute-done.13.two_a_ref, ...), custom_call_target="tpu_custom_call" | custom-call | tf_op jit(solution)/shard_map/pallas_call | solution.py:289
  101.7 5.2 %shard_map.86.hx_ref = bf16[512,4096]{1,0:T(8,128)(2,1)} custom-call(bf16[128,4096]{1,0:T(8,128)(2,1)S(1)} %copy-done.3, bf16[128,4096]{1,0:T(8,128)(2,1)S(1)} %copy-done.5, bf16[128,4096]{1,0:T(8,128)(2,1)} %collective-permute-done.15.refs_2_, bf16[128,4096]{1,0:T(8,128)(2,1)} %collective-permute-done.7.refs_3_), custom_call_target="tpu_custom_call" | custom-call | tf_op jit(solution)/shard_map/pallas_call | solution.py:309
  107.5 2.8 %collective-permute-done.16.refs_1_ = bf16[1024,512]{1,0:T(8,128)(2,1)S(1)} collective-permute-done((bf16[1024,512]{1,0:T(8,128)(2,1)S(1)}, bf16[1024,512]{1,0:T(8,128)(2,1)S(1)}, u32[]{:S(2)}, u32[]{:S(2)}) %collective-permute-start.16) | collective-permute-done | bytes 1048608 | tf_op jit(solution)/shard_map/ppermute | solution.py:30
  111.3 7.0 %shard_map.87 = bf16[4,1024,256]{2,1,0:T(8,128)(2,1)} custom-call(bf16[1024,512]{1,0:T(8,128)(2,1)S(1)} %collective-permute-done.9.refs_0_.q_ref, bf16[1024,512]{1,0:T(8,128)(2,1)S(1)} %collective-permute-done.16.refs_1_, bf16[1024,512]{1,0:T(8,128)(2,1)} %collective-permute-done.10.refs_2_, bf16[1024,512]{1,0:T(8,128)(2,1)S(1)} %collective-permute-done.17.refs_3_, ...), custom_call_target="tpu_custom_call" | custom-call | flops 4294967296 | bytes 10485760 | tf_op jit(solution)/shard_map/pallas_call | solution.py:362
  118.5 5.0 %all-to-all-start.2 = ((bf16[4,1024,256]{2,1,0:T(8,128)(2,1)}), bf16[4,1024,256]{2,1,0:T(8,128)(2,1)}, u32[]{:S(2)}, u32[]{:S(2)}) async-start(bf16[4,1024,256]{2,1,0:T(8,128)(2,1)} %shard_map.87), calls=%async_computation.2 | async-start | bytes 4194304 | tf_op jit(solution)/shard_map/all_to_all | solution.py:542
  125.1 3.5 %collective-permute-start.24 = (bf16[512,512]{1,0:T(8,128)(2,1)S(1)}, bf16[512,512]{1,0:T(8,128)(2,1)S(1)}, u32[]{:S(2)}, u32[]{:S(2)}) collective-permute-start(bf16[512,512]{1,0:T(8,128)(2,1)S(1)} %slice.43), channel_id=1, source_target_pairs={{0,66},{1,67},{2,64},{3,65},{4,70},{5,71},{6,68},{7,69},{8,74},{9,... | collective-permute-start | bytes 1572872 | tf_op jit(solution)/shard_map/ppermute | solution.py:30
  128.6 12.5 %shard_map.88 = (bf16[512,1024]{1,0:T(8,128)(2,1)}, bf16[512,1024]{1,0:T(8,128)(2,1)}, f32[512,1024]{1,0:T(8,128)}, f32[256,1024]{1,0:T(8,128)}, f32[256,1024]{1,0:T(8,128)}) custom-call(s32[6]{0:T(128)S(1)} %stack.63.idx_ref, bf16[1024,512]{1,0:T(8,128)(2,1)S(1)} %collective-permute-done.9.refs_0_.q_ref, f32[512,4096]{1,0:T(8,128)} %shard_map.84.own_ref, ...), custom_call_target="tpu_custom_call" | custom-call | flops 4294967296 | bytes 23068672 | tf_op jit(solution)/shard_map/pallas_call | solution.py:418
  141.7 3.3 %collective-permute-start.20 = (bf16[512,1024]{1,0:T(8,128)(2,1)}, bf16[512,1024]{1,0:T(8,128)(2,1)S(1)}, u32[]{:S(2)}, u32[]{:S(2)}) collective-permute-start(bf16[512,1024]{1,0:T(8,128)(2,1)} %get-tuple-element.88), channel_id=1, source_target_pairs={{0,48},{1,49},{2,50},{3,51},{4,52},{5,53},{6,54},{7,55},{8,56},{9,... | collective-permute-start | bytes 3145736 | tf_op jit(solution)/shard_map/ppermute | solution.py:30
  145.0 5.9 %shard_map.90 = bf16[4,1024,256]{2,1,0:T(8,128)(2,1)} custom-call(bf16[1024,512]{1,0:T(8,128)(2,1)S(1)} %copy-done.6, bf16[1024,512]{1,0:T(8,128)(2,1)S(1)} %collective-permute-done.25.refs_1_, bf16[512,512]{1,0:T(8,128)(2,1)S(1)} %collective-permute-done.23.refs_2_, bf16[512,512]{1,0:T(8,128)(2,1)S(1)} %collective-permute-done.24.refs_3_, ...), custom_call_target="tpu_custom_call" | custom-call | flops 4294967296 | bytes 10485760 | tf_op jit(solution)/shard_map/pallas_call | solution.py:362
  150.9 4.8 %all-to-all-start.3 = ((bf16[4,1024,256]{2,1,0:T(8,128)(2,1)}), bf16[4,1024,256]{2,1,0:T(8,128)(2,1)}, u32[]{:S(2)}, u32[]{:S(2)}) async-start(bf16[4,1024,256]{2,1,0:T(8,128)(2,1)} %shard_map.90), calls=%async_computation.3 | async-start | bytes 4194304 | tf_op jit(solution)/shard_map/all_to_all | solution.py:552
  157.9 10.5 %collective-permute-done.20.up_ref = bf16[512,1024]{1,0:T(8,128)(2,1)S(1)} collective-permute-done((bf16[512,1024]{1,0:T(8,128)(2,1)}, bf16[512,1024]{1,0:T(8,128)(2,1)S(1)}, u32[]{:S(2)}, u32[]{:S(2)}) %collective-permute-start.20) | collective-permute-done | bytes 1048608 | tf_op jit(solution)/shard_map/ppermute | solution.py:30
  169.3 2.2 %add_convert_fusion = bf16[256,1024]{1,0:T(8,128)(2,1)} fusion(f32[256,1024]{1,0:T(8,128)} %get-tuple-element.90, bf16[512,1024]{1,0:T(8,128)(2,1)S(1)} %collective-permute-done.20.up_ref), kind=kLoop, calls=%fused_computation.2 | loop fusion | flops 786432 | bytes 2097152 | tf_op jit(solution)/shard_map/convert_element_type | solution.py:44
  171.6 3.6 %collective-permute-start.22 = (bf16[256,1024]{1,0:T(8,128)(2,1)}, bf16[256,1024]{1,0:T(8,128)(2,1)S(1)}, u32[]{:S(2)}, u32[]{:S(2)}) collective-permute-start(bf16[256,1024]{1,0:T(8,128)(2,1)} %add_convert_fusion), channel_id=1, source_target_pairs={{0,48},{1,49},{2,50},{3,51},{4,52},{5,53},{6,54},{7,55},{8,56},{9,... | collective-permute-start | bytes 1572872 | tf_op jit(solution)/shard_map/ppermute | solution.py:30
  175.1 6.9 %collective-permute-done.19.down_ref = bf16[512,1024]{1,0:T(8,128)(2,1)S(1)} collective-permute-done((bf16[512,1024]{1,0:T(8,128)(2,1)}, bf16[512,1024]{1,0:T(8,128)(2,1)S(1)}, u32[]{:S(2)}, u32[]{:S(2)}) %collective-permute-start.19) | collective-permute-done | bytes 1048608 | tf_op jit(solution)/shard_map/ppermute | solution.py:30
  184.0 2.8 %collective-permute-start.30 = (bf16[1024,128]{1,0:T(8,128)(2,1)S(1)}, bf16[1024,128]{1,0:T(8,128)(2,1)S(1)}, u32[]{:S(2)}, u32[]{:S(2)}) collective-permute-start(bf16[1024,128]{1,0:T(8,128)(2,1)S(1)} %get-tuple-element.102), channel_id=1, source_target_pairs={{0,66},{1,67},{2,64},{3,65},{4,70},{5,71},{6,68},{7,69},{8,74},{9,... | collective-permute-start | bytes 786440 | tf_op jit(solution)/shard_map/ppermute | solution.py:30
  186.8 2.2 %reduce_sum.24 = bf16[1024,256]{1,0:T(8,128)(2,1)S(1)} reduce(bf16[4,1024,256]{2,1,0:T(8,128)(2,1)} %all-to-all-done.3, bf16[]{:T(256)} %constant.124.clone.1), dimensions={0}, to_apply=%region_0.1 | reduce | flops 786432 | bytes 2621442 | tf_op jit(solution)/shard_map/reduce_sum | solution.py:557
  190.3 7.1 %collective-permute-done.21.down2_ref = bf16[256,1024]{1,0:T(8,128)(2,1)S(1)} collective-permute-done((bf16[256,1024]{1,0:T(8,128)(2,1)}, bf16[256,1024]{1,0:T(8,128)(2,1)S(1)}, u32[]{:S(2)}, u32[]{:S(2)}) %collective-permute-start.21) | collective-permute-done | bytes 524320 | tf_op jit(solution)/shard_map/ppermute | solution.py:30
  197.4 3.6 %shard_map.89 = bf16[1024,512]{1,0:T(8,128)(2,1)} custom-call(f32[512,1024]{1,0:T(8,128)} %get-tuple-element.86.b0_ref, bf16[512,1024]{1,0:T(8,128)(2,1)} %copy-done.10, bf16[512,1024]{1,0:T(8,128)(2,1)} %copy-done.9, bf16[256,1024]{1,0:T(8,128)(2,1)S(1)} %collective-permute-done.21.down2_ref, bf16[256,1024]{1,0:T(8,128)(2,1)S(1)} %collective-permute-done.22.up2_ref), custom_call_target="tpu_custom_call" | custom-call | tf_op jit(solution)/shard_map/pallas_call | solution.py:452
  (105 shorter events, 39.3 us)
Async XLA Ops:
  2.2 6.4 %collective-permute-start = (bf16[512,512]{1,0:T(8,128)(2,1)S(1)}, bf16[512,512]{1,0:T(8,128)(2,1)S(1)}, u32[]{:S(2)}, u32[]{:S(2)}) collective-permute-start(bf16[512,512]{1,0:T(8,128)(2,1)S(1)} %get-tuple-element.50), channel_id=1, source_target_pairs={{0,1},{1,0},{2,3},{3,2},{4,5},{5,4},{6,7},{7,6},{8,9},{9,8},{10,11... | collective-permute-start | bytes 1572872 | tf_op jit(solution)/shard_map/ppermute | solution.py:30
  11.7 21.8 %collective-permute-start.5 = (bf16[64,4096]{1,0:T(8,128)(2,1)S(1)}, bf16[64,4096]{1,0:T(8,128)(2,1)S(1)}, u32[]{:S(2)}, u32[]{:S(2)}) collective-permute-start(bf16[64,4096]{1,0:T(8,128)(2,1)S(1)} %get-tuple-element.101), channel_id=1, source_target_pairs={{0,64},{1,65},{2,66},{3,67},{4,68},{5,69},{6,70},{7,71},{8,72},{9,... | collective-permute-start | bytes 1572872 | tf_op jit(solution)/shard_map/ppermute | solution.py:30
  13.7 19.8 %collective-permute-start.6 = (bf16[64,4096]{1,0:T(8,128)(2,1)S(1)}, bf16[64,4096]{1,0:T(8,128)(2,1)S(1)}, u32[]{:S(2)}, u32[]{:S(2)}) collective-permute-start(bf16[64,4096]{1,0:T(8,128)(2,1)S(1)} %get-tuple-element.100), channel_id=1, source_target_pairs={{0,66},{1,67},{2,64},{3,65},{4,70},{5,71},{6,68},{7,69},{8,74},{9,... | collective-permute-start | bytes 1572872 | tf_op jit(solution)/shard_map/ppermute | solution.py:30
  15.9 14.8 %all-to-all-start = ((bf16[4,144,512]{2,1,0:T(8,128)(2,1)}), bf16[4,144,512]{2,1,0:T(8,128)(2,1)S(1)}, u32[]{:S(2)}, u32[]{:S(2)}) async-start(bf16[4,144,512]{2,1,0:T(8,128)(2,1)} %shard_map.77), calls=%async_computation | async-start | bytes 1179648 | tf_op jit(solution)/shard_map/all_to_all | solution.py:496
  20.3 15.7 %collective-permute-start.2 = (bf16[1024,128]{1,0:T(8,128)(2,1)}, bf16[1024,128]{1,0:T(8,128)(2,1)}, u32[]{:S(2)}, u32[]{:S(2)}) collective-permute-start(bf16[1024,128]{1,0:T(8,128)(2,1)} %get-tuple-element.58), channel_id=1, source_target_pairs={{0,64},{1,65},{2,66},{3,67},{4,68},{5,69},{6,70},{7,71},{8,72},{9,... | collective-permute-start | bytes 786440 | tf_op jit(solution)/shard_map/ppermute | solution.py:30
  20.3 21.5 %collective-permute-start.3 = (bf16[1024,128]{1,0:T(8,128)(2,1)}, bf16[1024,128]{1,0:T(8,128)(2,1)}, u32[]{:S(2)}, u32[]{:S(2)}) collective-permute-start(bf16[1024,128]{1,0:T(8,128)(2,1)} %get-tuple-element.59), channel_id=1, source_target_pairs={{0,2},{1,3},{2,0},{3,1},{4,6},{5,7},{6,4},{7,5},{8,10},{9,11},{10,... | collective-permute-start | bytes 786440 | tf_op jit(solution)/shard_map/ppermute | solution.py:30
  23.7 18.1 %collective-permute-start.4 = (bf16[1024,128]{1,0:T(8,128)(2,1)S(1)}, bf16[1024,128]{1,0:T(8,128)(2,1)}, u32[]{:S(2)}, u32[]{:S(2)}) collective-permute-start(bf16[1024,128]{1,0:T(8,128)(2,1)S(1)} %get-tuple-element.60), channel_id=1, source_target_pairs={{0,66},{1,67},{2,64},{3,65},{4,70},{5,71},{6,68},{7,69},{8,74},{9,... | collective-permute-start | bytes 786440 | tf_op jit(solution)/shard_map/ppermute | solution.py:30
  33.4 9.7 %collective-permute-start.1 = (bf16[192,512]{1,0:T(8,128)(2,1)}, bf16[192,512]{1,0:T(8,128)(2,1)S(1)}, u32[]{:S(2)}, u32[]{:S(2)}) collective-permute-start(bf16[192,512]{1,0:T(8,128)(2,1)} %get-tuple-element.53.sent_ref), channel_id=1, source_target_pairs={{0,64},{1,65},{2,66},{3,67},{4,68},{5,69},{6,70},{7,71},{8,72},{9,... | collective-permute-start | bytes 589832 | tf_op jit(solution)/shard_map/ppermute | solution.py:30
  34.5 27.9 %collective-permute-start.7 = (bf16[128,4096]{1,0:T(8,128)(2,1)}, bf16[128,4096]{1,0:T(8,128)(2,1)}, u32[]{:S(2)}, u32[]{:S(2)}) collective-permute-start(bf16[128,4096]{1,0:T(8,128)(2,1)} %shard_map.82.refs_0_), channel_id=1, source_target_pairs={{0,4},{1,5},{2,6},{3,7},{4,8},{5,9},{6,10},{7,11},{8,12},{9,13},{1... | collective-permute-start | bytes 3145736 | tf_op jit(solution)/shard_map/ppermute | solution.py:30
  36.0 26.4 %collective-permute-start.8 = (bf16[128,4096]{1,0:T(8,128)(2,1)}, bf16[128,4096]{1,0:T(8,128)(2,1)S(1)}, u32[]{:S(2)}, u32[]{:S(2)}) collective-permute-start(bf16[128,4096]{1,0:T(8,128)(2,1)} %shard_map.82.refs_0_), channel_id=1, source_target_pairs={{0,12},{1,13},{2,14},{3,15},{4,0},{5,1},{6,2},{7,3},{8,4},{9,5},{1... | collective-permute-start | bytes 3145736 | tf_op jit(solution)/shard_map/ppermute | solution.py:30
  46.9 15.5 %all-to-all-start.1 = ((bf16[4,128,512]{2,1,0:T(8,128)(2,1)}), bf16[4,128,512]{2,1,0:T(8,128)(2,1)}, u32[]{:S(2)}, u32[]{:S(2)}) async-start(bf16[4,128,512]{2,1,0:T(8,128)(2,1)} %get-tuple-element.62), calls=%async_computation.1 | async-start | bytes 1048576 | tf_op jit(solution)/shard_map/all_to_all | solution.py:514
  53.5 29.4 %collective-permute-start.11 = (bf16[2,2048,128]{2,1,0:T(8,128)(2,1)S(1)}, bf16[2,2048,128]{2,1,0:T(8,128)(2,1)S(1)}, u32[]{:S(2)}, u32[]{:S(2)}) collective-permute-start(bf16[2,2048,128]{2,1,0:T(8,128)(2,1)S(1)} %pad_maximum_fusion.1.own_ref), channel_id=1, source_target_pairs={{0,16},{1,17},{2,18},{3,19},{4,20},{5,21},{6,22},{7,23},{8,24},{9,... | collective-permute-start | bytes 3145736 | tf_op jit(solution)/shard_map/ppermute | solution.py:30
  55.6 27.3 %collective-permute-start.12 = (bf16[2,2048,128]{2,1,0:T(8,128)(2,1)S(1)}, bf16[2,2048,128]{2,1,0:T(8,128)(2,1)}, u32[]{:S(2)}, u32[]{:S(2)}) collective-permute-start(bf16[2,2048,128]{2,1,0:T(8,128)(2,1)S(1)} %pad_maximum_fusion.1.own_ref), channel_id=1, source_target_pairs={{0,48},{1,49},{2,50},{3,51},{4,52},{5,53},{6,54},{7,55},{8,56},{9,... | collective-permute-start | bytes 3145736 | tf_op jit(solution)/shard_map/ppermute | solution.py:30
  62.4 39.3 %collective-permute-start.15 = (bf16[128,4096]{1,0:T(8,128)(2,1)}, bf16[128,4096]{1,0:T(8,128)(2,1)}, u32[]{:S(2)}, u32[]{:S(2)}) collective-permute-start(bf16[128,4096]{1,0:T(8,128)(2,1)} %collective-permute-done.7.refs_3_), channel_id=1, source_target_pairs={{0,4},{1,5},{2,6},{3,7},{4,8},{5,9},{6,10},{7,11},{8,12},{9,13},{1... | collective-permute-start | bytes 3145736 | tf_op jit(solution)/shard_map/ppermute | solution.py:30
  71.4 35.6 %collective-permute-start.10 = (bf16[1024,512]{1,0:T(8,128)(2,1)}, bf16[1024,512]{1,0:T(8,128)(2,1)}, u32[]{:S(2)}, u32[]{:S(2)}) collective-permute-start(bf16[1024,512]{1,0:T(8,128)(2,1)} %get-tuple-element.91.refs_0_), channel_id=1, source_target_pairs={{0,66},{1,67},{2,64},{3,65},{4,70},{5,71},{6,68},{7,69},{8,74},{9,... | collective-permute-start | bytes 3145736 | tf_op jit(solution)/shard_map/ppermute | solution.py:30
  73.6 33.4 %collective-permute-start.9 = (bf16[1024,512]{1,0:T(8,128)(2,1)}, bf16[1024,512]{1,0:T(8,128)(2,1)S(1)}, u32[]{:S(2)}, u32[]{:S(2)}) collective-permute-start(bf16[1024,512]{1,0:T(8,128)(2,1)} %get-tuple-element.91.refs_0_), channel_id=1, source_target_pairs={{0,64},{1,65},{2,66},{3,67},{4,68},{5,69},{6,70},{7,71},{8,72},{9,... | collective-permute-start | bytes 3145736 | tf_op jit(solution)/shard_map/ppermute | solution.py:30
  83.8 15.5 %collective-permute-start.13 = (bf16[1,2048,128]{2,1,0:T(8,128)(2,1)}, bf16[1,2048,128]{2,1,0:T(8,128)(2,1)}, u32[]{:S(2)}, u32[]{:S(2)}) collective-permute-start(bf16[1,2048,128]{2,1,0:T(8,128)(2,1)} %slice.38), channel_id=1, source_target_pairs={{0,16},{1,17},{2,18},{3,19},{4,20},{5,21},{6,22},{7,23},{8,24},{9,... | collective-permute-start | bytes 1572872 | tf_op jit(solution)/shard_map/ppermute | solution.py:30
  86.0 13.2 %collective-permute-start.14 = (bf16[1,2048,128]{2,1,0:T(8,128)(2,1)}, bf16[1,2048,128]{2,1,0:T(8,128)(2,1)}, u32[]{:S(2)}, u32[]{:S(2)}) collective-permute-start(bf16[1,2048,128]{2,1,0:T(8,128)(2,1)} %slice.39), channel_id=1, source_target_pairs={{0,48},{1,49},{2,50},{3,51},{4,52},{5,53},{6,54},{7,55},{8,56},{9,... | collective-permute-start | bytes 1572872 | tf_op jit(solution)/shard_map/ppermute | solution.py:30
  107.0 4.4 %collective-permute-start.17 = (bf16[1024,512]{1,0:T(8,128)(2,1)}, bf16[1024,512]{1,0:T(8,128)(2,1)S(1)}, u32[]{:S(2)}, u32[]{:S(2)}) collective-permute-start(bf16[1024,512]{1,0:T(8,128)(2,1)} %collective-permute-done.10.refs_2_), channel_id=1, source_target_pairs={{0,1},{1,0},{2,3},{3,2},{4,5},{5,4},{6,7},{7,6},{8,9},{9,8},{10,11... | collective-permute-start | bytes 3145736 | tf_op jit(solution)/shard_map/ppermute | solution.py:30
  118.4 10.2 %collective-permute-start.18 = (bf16[512,4096]{1,0:T(8,128)(2,1)}, bf16[512,4096]{1,0:T(8,128)(2,1)}, u32[]{:S(2)}, u32[]{:S(2)}) collective-permute-start(bf16[512,4096]{1,0:T(8,128)(2,1)} %shard_map.86.hx_ref), channel_id=1, source_target_pairs={{0,1},{1,0},{2,3},{3,2},{4,5},{5,4},{6,7},{7,6},{8,9},{9,8},{10,11... | collective-permute-start | bytes 12582920 | tf_op jit(solution)/shard_map/ppermute | solution.py:30
  118.5 32.4 %all-to-all-start.2 = ((bf16[4,1024,256]{2,1,0:T(8,128)(2,1)}), bf16[4,1024,256]{2,1,0:T(8,128)(2,1)}, u32[]{:S(2)}, u32[]{:S(2)}) async-start(bf16[4,1024,256]{2,1,0:T(8,128)(2,1)} %shard_map.87), calls=%async_computation.2 | async-start | bytes 4194304 | tf_op jit(solution)/shard_map/all_to_all | solution.py:542
  124.7 16.4 %collective-permute-start.23 = (bf16[512,512]{1,0:T(8,128)(2,1)S(1)}, bf16[512,512]{1,0:T(8,128)(2,1)S(1)}, u32[]{:S(2)}, u32[]{:S(2)}) collective-permute-start(bf16[512,512]{1,0:T(8,128)(2,1)S(1)} %slice.42), channel_id=1, source_target_pairs={{0,64},{1,65},{2,66},{3,67},{4,68},{5,69},{6,70},{7,71},{8,72},{9,... | collective-permute-start | bytes 1572872 | tf_op jit(solution)/shard_map/ppermute | solution.py:30
  125.1 16.0 %collective-permute-start.24 = (bf16[512,512]{1,0:T(8,128)(2,1)S(1)}, bf16[512,512]{1,0:T(8,128)(2,1)S(1)}, u32[]{:S(2)}, u32[]{:S(2)}) collective-permute-start(bf16[512,512]{1,0:T(8,128)(2,1)S(1)} %slice.43), channel_id=1, source_target_pairs={{0,66},{1,67},{2,64},{3,65},{4,70},{5,71},{6,68},{7,69},{8,74},{9,... | collective-permute-start | bytes 1572872 | tf_op jit(solution)/shard_map/ppermute | solution.py:30
  128.6 16.5 %collective-permute-start.25 = (bf16[1024,512]{1,0:T(8,128)(2,1)S(1)}, bf16[1024,512]{1,0:T(8,128)(2,1)S(1)}, u32[]{:S(2)}, u32[]{:S(2)}) collective-permute-start(bf16[1024,512]{1,0:T(8,128)(2,1)S(1)} %copy-done.6), channel_id=1, source_target_pairs={{0,1},{1,0},{2,3},{3,2},{4,5},{5,4},{6,7},{7,6},{8,9},{9,8},{10,11... | collective-permute-start | bytes 3145736 | tf_op jit(solution)/shard_map/ppermute | solution.py:30
  141.7 26.6 %collective-permute-start.20 = (bf16[512,1024]{1,0:T(8,128)(2,1)}, bf16[512,1024]{1,0:T(8,128)(2,1)S(1)}, u32[]{:S(2)}, u32[]{:S(2)}) collective-permute-start(bf16[512,1024]{1,0:T(8,128)(2,1)} %get-tuple-element.88), channel_id=1, source_target_pairs={{0,48},{1,49},{2,50},{3,51},{4,52},{5,53},{6,54},{7,55},{8,56},{9,... | collective-permute-start | bytes 3145736 | tf_op jit(solution)/shard_map/ppermute | solution.py:30
  150.9 35.9 %all-to-all-start.3 = ((bf16[4,1024,256]{2,1,0:T(8,128)(2,1)}), bf16[4,1024,256]{2,1,0:T(8,128)(2,1)}, u32[]{:S(2)}, u32[]{:S(2)}) async-start(bf16[4,1024,256]{2,1,0:T(8,128)(2,1)} %shard_map.90), calls=%async_computation.3 | async-start | bytes 4194304 | tf_op jit(solution)/shard_map/all_to_all | solution.py:552
  155.7 26.4 %collective-permute-start.19 = (bf16[512,1024]{1,0:T(8,128)(2,1)}, bf16[512,1024]{1,0:T(8,128)(2,1)S(1)}, u32[]{:S(2)}, u32[]{:S(2)}) collective-permute-start(bf16[512,1024]{1,0:T(8,128)(2,1)} %get-tuple-element.87), channel_id=1, source_target_pairs={{0,16},{1,17},{2,18},{3,19},{4,20},{5,21},{6,22},{7,23},{8,24},{9,... | collective-permute-start | bytes 3145736 | tf_op jit(solution)/shard_map/ppermute | solution.py:30
  171.6 18.8 %collective-permute-start.22 = (bf16[256,1024]{1,0:T(8,128)(2,1)}, bf16[256,1024]{1,0:T(8,128)(2,1)S(1)}, u32[]{:S(2)}, u32[]{:S(2)}) collective-permute-start(bf16[256,1024]{1,0:T(8,128)(2,1)} %add_convert_fusion), channel_id=1, source_target_pairs={{0,48},{1,49},{2,50},{3,51},{4,52},{5,53},{6,54},{7,55},{8,56},{9,... | collective-permute-start | bytes 1572872 | tf_op jit(solution)/shard_map/ppermute | solution.py:30
  183.2 14.3 %collective-permute-start.21 = (bf16[256,1024]{1,0:T(8,128)(2,1)}, bf16[256,1024]{1,0:T(8,128)(2,1)S(1)}, u32[]{:S(2)}, u32[]{:S(2)}) collective-permute-start(bf16[256,1024]{1,0:T(8,128)(2,1)} %add_convert_fusion.1), channel_id=1, source_target_pairs={{0,16},{1,17},{2,18},{3,19},{4,20},{5,21},{6,22},{7,23},{8,24},{9,... | collective-permute-start | bytes 1572872 | tf_op jit(solution)/shard_map/ppermute | solution.py:30
  183.9 17.1 %collective-permute-start.28 = (bf16[1024,128]{1,0:T(8,128)(2,1)}, bf16[1024,128]{1,0:T(8,128)(2,1)S(1)}, u32[]{:S(2)}, u32[]{:S(2)}) collective-permute-start(bf16[1024,128]{1,0:T(8,128)(2,1)} %get-tuple-element.103), channel_id=1, source_target_pairs={{0,64},{1,65},{2,66},{3,67},{4,68},{5,69},{6,70},{7,71},{8,72},{9,... | collective-permute-start | bytes 786440 | tf_op jit(solution)/shard_map/ppermute | solution.py:30
  184.0 17.0 %collective-permute-start.30 = (bf16[1024,128]{1,0:T(8,128)(2,1)S(1)}, bf16[1024,128]{1,0:T(8,128)(2,1)S(1)}, u32[]{:S(2)}, u32[]{:S(2)}) collective-permute-start(bf16[1024,128]{1,0:T(8,128)(2,1)S(1)} %get-tuple-element.102), channel_id=1, source_target_pairs={{0,66},{1,67},{2,64},{3,65},{4,70},{5,71},{6,68},{7,69},{8,74},{9,... | collective-permute-start | bytes 786440 | tf_op jit(solution)/shard_map/ppermute | solution.py:30
  189.1 11.9 %collective-permute-start.29 = (bf16[1024,128]{1,0:T(8,128)(2,1)S(1)}, bf16[1024,128]{1,0:T(8,128)(2,1)S(1)}, u32[]{:S(2)}, u32[]{:S(2)}) collective-permute-start(bf16[1024,128]{1,0:T(8,128)(2,1)S(1)} %get-tuple-element.104), channel_id=1, source_target_pairs={{0,2},{1,3},{2,0},{3,1},{4,6},{5,7},{6,4},{7,5},{8,10},{9,11},{10,... | collective-permute-start | bytes 786440 | tf_op jit(solution)/shard_map/ppermute | solution.py:30
  (17 other events, 129.2 us)

commit v4 on v2

--- a/solution.py
+++ b/solution.py
@@ -506,10 +506,11 @@
     w_two = y_up(w_left[:1]), y_down(w_right[1:])
     w_all = in_order([w_own, w_right, *w_two, w_left], w_order)
     h_x = stacked([h0, h_right, h_two, h_left])
-    r_own, r_oth, w_here, w_all, h_x = tie(r_own, r_oth, w_here, w_all, h_x)
+    near = swap(r_own), swap(r_oth)
+    r_own, r_oth, w_here, w_all, h_x, *near = tie(r_own, r_oth, w_here, w_all, h_x, *near)
 
     far = z_flip[1](r_oth[:ht]), z_flip[3](r_own[ht:])
-    par = hidden_terms([r_own, swap(r_own), r_oth, swap(r_oth)], w_all)
+    par = hidden_terms([r_own, near[0], r_oth, near[1]], w_all)
     _, h_x = tie(par, h_x)
     h_k = swap(h_x)
     par_got = lax.all_to_all(par, "chan", 0, 0, axis_index_groups=x_groups)

time: 198 us -> 213 us (1.076)
  blocking collectives: 0 us -> 12.3 us
  waiting for transfers between devices: 44.7 us -> 52.9 us
  starting transfers between devices: 56.2 us -> 52.7 us
  other arithmetic: 16 us -> 13.3 us
    ppermute x31, waiting for transfers between devices: 31.4 us -> 46.3 us  [mover(): return lambda a: lax.ppermute(a, AXES, pairs)]
    all_to_all x0 -> x1, blocking collectives: none -> 12.3 us  [local(): lax.all_to_all(inner4, 'dp', 0, 0, axis_index_groups=groups).reshape(ch, ch)]
    all_to_all x1 -> x0, waiting for transfers between devices: 5.49 us -> none  [local(): lax.all_to_all(inner4, 'dp', 0, 0, axis_index_groups=groups).reshape(ch, ch)]
    all_to_all x1 -> x0, starting transfers between devices: 4.47 us -> none  [local(): lax.all_to_all(inner4, 'dp', 0, 0, axis_index_groups=groups).reshape(ch, ch)]
    unnamed x25 -> x29, local copies, waits for them, and re-layouts: 4.07 us -> 5.02 us
  transfers between devices with their start and end apart: 35 -> 34, of which waited for: 10 -> 11; matrix products, arithmetic and copies ran while one was open for 10% -> 8% of each run, Pallas kernels for 31% -> 25%
where the time goes in v4:
time: 213 us; the launch traced here: 212 us
  Pallas kernels  68.9 us (32%)
  waiting for transfers between devices  52.9 us (25%)
  starting transfers between devices  52.7 us (25%)
  other arithmetic  13.3 us (6%)
  blocking collectives  12.3 us (6%)
  local copies, waits for them, and re-layouts  10.5 us (5%)
    ppermute x31, waiting for transfers between devices, mover(): return lambda a: lax.ppermute(a, AXES, pairs)  46.3 us
    ppermute x31, starting transfers between devices, mover(): return lambda a: lax.ppermute(a, AXES, pairs)  36.9 us
    pallas_call x2, Pallas kernels, hidden_terms(): pl.pallas_call(hidden_kernel, out_shape=pltpu.HBM((4, rows, wide // 4), B...  13.6 us
    pallas_call x1, Pallas kernels, weight_terms(): pl.pallas_call(weight_kernel, out_shape=shapes, grid_spec=pltpu.PrefetchS...  12.5 us
    all_to_all x1, blocking collectives, local(): lax.all_to_all(inner4, 'dp', 0, 0, axis_index_groups=groups).reshape(ch, ch)  12.3 us
    pallas_call x1, Pallas kernels, weight_here(): pl.pallas_call(here_kernel, out_shape=pltpu.HBM((ch, 4 * feat), F32), gri...  10.3 us
    pallas_call x1, Pallas kernels, grad_z_of(): pl.pallas_call(functools.partial(grad_z_kernel, scale=2.0 / rows), out_sh...  7.24 us
    all_to_all x1, starting transfers between devices, local(): par_got = lax.all_to_all(par, 'chan', 0, 0, axis_index_groups=x_groups)  6.31 us
  transfers between devices with their start and end apart: 34, of which 11 were waited for; matrix products, arithmetic and copies ran while one was open for 8% of the time, Pallas kernels for 25%

profile of v4, /device:TPU:2, one launch (start us, length us, event | category | flops | bytes accessed | tf_op | source)
XLA Modules:
  0.0 211.7 jit_solution(11038922032006731136)
XLA Ops:
  2.6 6.0 %shard_map.77 = bf16[4,144,512]{2,1,0:T(8,128)(2,1)} custom-call(bf16[1024,512]{1,0:T(8,128)(2,1)} %z_ref.3, bf16[1024,512]{1,0:T(8,128)(2,1)} %g_ref.3, f32[512,512]{1,0:T(8,128)} %u_ref.7), custom_call_target="tpu_custom_call" | custom-call | flops 2147483648 | bytes 3670016 | tf_op jit(solution)/shard_map/pallas_call | solution.py:103
  12.3 2.2 %collective-permute-start.6 = (bf16[64,4096]{1,0:T(8,128)(2,1)S(1)}, bf16[64,4096]{1,0:T(8,128)(2,1)S(1)}, u32[]{:S(2)}, u32[]{:S(2)}) collective-permute-start(bf16[64,4096]{1,0:T(8,128)(2,1)S(1)} %get-tuple-element.112), channel_id=1, source_target_pairs={{0,66},{1,67},{2,64},{3,65},{4,70},{5,71},{6,68},{7,69},{8,74},{9,... | collective-permute-start | bytes 1572872 | tf_op jit(solution)/shard_map/ppermute | solution.py:30
  14.5 12.3 %collective-permute-done.5.refs_0_ = bf16[64,4096]{1,0:T(8,128)(2,1)S(1)} collective-permute-done((bf16[64,4096]{1,0:T(8,128)(2,1)S(1)}, bf16[64,4096]{1,0:T(8,128)(2,1)S(1)}, u32[]{:S(2)}, u32[]{:S(2)}) %collective-permute-start.5) | collective-permute-done | bytes 524320 | tf_op jit(solution)/shard_map/ppermute | solution.py:30
  29.9 4.5 %all-to-all-start = ((bf16[4,144,512]{2,1,0:T(8,128)(2,1)}), bf16[4,144,512]{2,1,0:T(8,128)(2,1)S(1)}, u32[]{:S(2)}, u32[]{:S(2)}) async-start(bf16[4,144,512]{2,1,0:T(8,128)(2,1)} %shard_map.77), calls=%async_computation | async-start | bytes 1179648 | tf_op jit(solution)/shard_map/all_to_all | solution.py:469
  35.6 3.2 %collective-permute-start.3 = (bf16[1024,128]{1,0:T(8,128)(2,1)S(1)}, bf16[1024,128]{1,0:T(8,128)(2,1)S(1)}, u32[]{:S(2)}, u32[]{:S(2)}) collective-permute-start(bf16[1024,128]{1,0:T(8,128)(2,1)S(1)} %get-tuple-element.61), channel_id=1, source_target_pairs={{0,2},{1,3},{2,0},{3,1},{4,6},{5,7},{6,4},{7,5},{8,10},{9,11},{10,... | collective-permute-start | bytes 786440 | tf_op jit(solution)/shard_map/ppermute | solution.py:30
  39.0 4.9 %all-to-all-done.got_ref = bf16[4,144,512]{2,1,0:T(8,128)(2,1)S(1)} async-done(((bf16[4,144,512]{2,1,0:T(8,128)(2,1)}), bf16[4,144,512]{2,1,0:T(8,128)(2,1)S(1)}, u32[]{:S(2)}, u32[]{:S(2)}) %all-to-all-start) | async-done | bytes 589856 | tf_op jit(solution)/shard_map/all_to_all | solution.py:469
  47.5 5.1 %shard_map.80 = (f32[512,512]{1,0:T(8,128)}, f32[1024,512]{1,0:T(8,128)}) custom-call(f32[512,512]{1,0:T(8,128)} %u_ref.7, f32[1,512]{1,0:T(1,128)S(1)} %bitcast.25, bf16[1024,512]{1,0:T(8,128)(2,1)} %g_ref.3), custom_call_target="tpu_custom_call" | custom-call | flops 1879048192 | bytes 5242880 | tf_op jit(solution)/shard_map/pallas_call | solution.py:190
  53.2 3.0 %shard_map.81 = (bf16[4,128,512]{2,1,0:T(8,128)(2,1)}, f32[8,512]{1,0:T(8,128)}) custom-call(s32[1]{0:T(128)} %bitcast.6.y_ref, f32[128,512]{1,0:T(8,128)} %get-tuple-element.54.quarter_ref, bf16[192,512]{1,0:T(8,128)(2,1)} %get-tuple-element.55.sent_ref, bf16[192,512]{1,0:T(8,128)(2,1)} %copy-done.12, f32[512,512]{1,0:T(8,128)} %u_ref.7, f32[512,512]{1,0:T(8,128)} %u_ref.7, ...), custom_call_target="tpu_custom_call" | custom-call | tf_op jit(solution)/shard_map/pallas_call | solution.py:158
  56.3 12.3 %all_to_all.20 = bf16[4,128,512]{2,1,0:T(8,128)(2,1)} all-to-all(bf16[4,128,512]{2,1,0:T(8,128)(2,1)} %get-tuple-element.64), channel_id=1, replica_groups={{0,16,32,48},{64,80,96,112},{1,17,33,49},{65,81,97,113},{2,18,34,50},{6..., dimensions={0} | all-to-all | bytes 1048576 | tf_op jit(solution)/shard_map/all_to_all | solution.py:487
  69.3 7.2 %shard_map.83 = (bf16[1024,512]{1,0:T(8,128)(2,1)}, bf16[512,1024]{1,0:T(8,128)(2,1)}) custom-call(f32[512,512]{1,0:T(8,128)} %u_ref.7, bf16[512,512]{1,0:T(8,128)(2,1)} %bitcast.27, bf16[1024,512]{1,0:T(8,128)(2,1)} %z_ref.3, f32[1024,512]{1,0:T(8,128)} %get-tuple-element.67.first_ref, f32[512,512]{1,0:T(8,128)} %get-tuple-element.68.wsum_ref, ...), custom_call_target="tpu_custom_call" | custom-call | flops 2415919104 | bytes 6815744 | tf_op jit(solution)/shard_map/pallas_call | solution.py:214
  78.0 2.7 %collective-permute-start.10 = (bf16[1024,512]{1,0:T(8,128)(2,1)}, bf16[1024,512]{1,0:T(8,128)(2,1)}, u32[]{:S(2)}, u32[]{:S(2)}) collective-permute-start(bf16[1024,512]{1,0:T(8,128)(2,1)} %get-tuple-element.95.refs_0_), channel_id=1, source_target_pairs={{0,66},{1,67},{2,64},{3,65},{4,70},{5,71},{6,68},{7,69},{8,74},{9,... | collective-permute-start | bytes 3145736 | tf_op jit(solution)/shard_map/ppermute | solution.py:30
  81.5 2.7 %collective-permute-start.12 = (bf16[2,2048,128]{2,1,0:T(8,128)(2,1)S(1)}, bf16[2,2048,128]{2,1,0:T(8,128)(2,1)S(1)}, u32[]{:S(2)}, u32[]{:S(2)}) collective-permute-start(bf16[2,2048,128]{2,1,0:T(8,128)(2,1)S(1)} %pad_maximum_fusion.1.own_ref), channel_id=1, source_target_pairs={{0,48},{1,49},{2,50},{3,51},{4,52},{5,53},{6,54},{7,55},{8,56},{9,... | collective-permute-start | bytes 3145736 | tf_op jit(solution)/shard_map/ppermute | solution.py:30
  85.6 12.8 %collective-permute-done.9.refs_0_.q_ref = bf16[1024,512]{1,0:T(8,128)(2,1)S(1)} collective-permute-done((bf16[1024,512]{1,0:T(8,128)(2,1)}, bf16[1024,512]{1,0:T(8,128)(2,1)S(1)}, u32[]{:S(2)}, u32[]{:S(2)}) %collective-permute-start.9) | collective-permute-done | bytes 1048608 | tf_op jit(solution)/shard_map/ppermute | solution.py:30
  98.4 2.2 %collective-permute-done.10.refs_2_ = bf16[1024,512]{1,0:T(8,128)(2,1)} collective-permute-done((bf16[1024,512]{1,0:T(8,128)(2,1)}, bf16[1024,512]{1,0:T(8,128)(2,1)}, u32[]{:S(2)}, u32[]{:S(2)}) %collective-permute-start.10) | collective-permute-done | bytes 1048608 | tf_op jit(solution)/shard_map/ppermute | solution.py:30
  100.6 2.0 collective-permute-done.11.left_ref
  104.7 3.0 %collective-permute-start.14 = (bf16[1,2048,128]{2,1,0:T(8,128)(2,1)}, bf16[1,2048,128]{2,1,0:T(8,128)(2,1)}, u32[]{:S(2)}, u32[]{:S(2)}) collective-permute-start(bf16[1,2048,128]{2,1,0:T(8,128)(2,1)} %slice.51), channel_id=1, source_target_pairs={{0,48},{1,49},{2,50},{3,51},{4,52},{5,53},{6,54},{7,55},{8,56},{9,... | collective-permute-start | bytes 1572872 | tf_op jit(solution)/shard_map/ppermute | solution.py:30
  107.8 10.3 %shard_map.84.own_ref = f32[512,4096]{1,0:T(8,128)} custom-call(s32[6]{0:T(128)S(1)} %stack.63.idx_ref, bf16[512,1024]{1,0:T(8,128)(2,1)} %get-tuple-element.76.p_ref, bf16[1024,8192]{1,0:T(8,128)(2,1)} %own_ref), custom_call_target="tpu_custom_call" | custom-call | flops 4294967296 | bytes 16777216 | tf_op jit(solution)/shard_map/pallas_call | solution.py:377
  118.1 2.6 %shard_map.85.refs_4_.refs_6_ = bf16[2048,1024]{1,0:T(8,128)(2,1)S(1)} custom-call(s32[8]{0:T(128)S(1)} %stack.75.idx_ref, bf16[2,2048,128]{2,1,0:T(8,128)(2,1)S(1)} %pad_maximum_fusion.1.own_ref, bf16[2,2048,128]{2,1,0:T(8,128)(2,1)S(1)} %copy-done.5, bf16[1,2048,128]{2,1,0:T(8,128)(2,1)} %collective-permute-done.13.two_a_ref, ...), custom_call_target="tpu_custom_call" | custom-call | tf_op jit(solution)/shard_map/pallas_call | solution.py:289
  120.8 5.2 %shard_map.86.hx_ref = bf16[512,4096]{1,0:T(8,128)(2,1)} custom-call(bf16[128,4096]{1,0:T(8,128)(2,1)S(1)} %copy-done.3, bf16[128,4096]{1,0:T(8,128)(2,1)S(1)} %copy-done.7, bf16[128,4096]{1,0:T(8,128)(2,1)} %collective-permute-done.15.refs_2_, bf16[128,4096]{1,0:T(8,128)(2,1)} %collective-permute-done.7.refs_3_), custom_call_target="tpu_custom_call" | custom-call | tf_op jit(solution)/shard_map/pallas_call | solution.py:309
  126.0 7.7 %shard_map.87 = bf16[4,1024,256]{2,1,0:T(8,128)(2,1)} custom-call(bf16[1024,512]{1,0:T(8,128)(2,1)S(1)} %collective-permute-done.9.refs_0_.q_ref, bf16[1024,512]{1,0:T(8,128)(2,1)} %collective-permute-done.16.refs_1_, bf16[1024,512]{1,0:T(8,128)(2,1)} %collective-permute-done.10.refs_2_, bf16[1024,512]{1,0:T(8,128)(2,1)} %collective-permute-done.17.refs_3_, ...), custom_call_target="tpu_custom_call" | custom-call | flops 4294967296 | bytes 10485760 | tf_op jit(solution)/shard_map/pallas_call | solution.py:362
  133.8 6.3 %all-to-all-start.2 = ((bf16[4,1024,256]{2,1,0:T(8,128)(2,1)}), bf16[4,1024,256]{2,1,0:T(8,128)(2,1)}, u32[]{:S(2)}, u32[]{:S(2)}) async-start(bf16[4,1024,256]{2,1,0:T(8,128)(2,1)} %shard_map.87), calls=%async_computation.2 | async-start | bytes 4194304 | tf_op jit(solution)/shard_map/all_to_all | solution.py:516
  143.3 12.5 %shard_map.88 = (bf16[512,1024]{1,0:T(8,128)(2,1)}, bf16[512,1024]{1,0:T(8,128)(2,1)}, f32[512,1024]{1,0:T(8,128)}, f32[256,1024]{1,0:T(8,128)}, f32[256,1024]{1,0:T(8,128)}) custom-call(s32[6]{0:T(128)S(1)} %stack.63.idx_ref, bf16[1024,512]{1,0:T(8,128)(2,1)S(1)} %collective-permute-done.9.refs_0_.q_ref, f32[512,4096]{1,0:T(8,128)} %shard_map.84.own_ref, ...), custom_call_target="tpu_custom_call" | custom-call | flops 4294967296 | bytes 23068672 | tf_op jit(solution)/shard_map/pallas_call | solution.py:418
  157.0 2.9 %collective-permute-start.19 = (bf16[512,1024]{1,0:T(8,128)(2,1)}, bf16[512,1024]{1,0:T(8,128)(2,1)}, u32[]{:S(2)}, u32[]{:S(2)}) collective-permute-start(bf16[512,1024]{1,0:T(8,128)(2,1)} %get-tuple-element.91), channel_id=1, source_target_pairs={{0,48},{1,49},{2,50},{3,51},{4,52},{5,53},{6,54},{7,55},{8,56},{9,... | collective-permute-start | bytes 3145736 | tf_op jit(solution)/shard_map/ppermute | solution.py:30
  159.9 5.9 %shard_map.89 = bf16[4,1024,256]{2,1,0:T(8,128)(2,1)} custom-call(bf16[1024,512]{1,0:T(8,128)(2,1)S(1)} %copy-done.8, bf16[1024,512]{1,0:T(8,128)(2,1)S(1)} %collective-permute-done.25.refs_1_, bf16[512,512]{1,0:T(8,128)(2,1)S(1)} %collective-permute-done.23.refs_2_, bf16[512,512]{1,0:T(8,128)(2,1)S(1)} %collective-permute-done.24.refs_3_, ...), custom_call_target="tpu_custom_call" | custom-call | flops 4294967296 | bytes 10485760 | tf_op jit(solution)/shard_map/pallas_call | solution.py:362
  165.9 5.0 %all-to-all-start.3 = ((bf16[4,1024,256]{2,1,0:T(8,128)(2,1)}), bf16[4,1024,256]{2,1,0:T(8,128)(2,1)S(1)}, u32[]{:S(2)}, u32[]{:S(2)}) async-start(bf16[4,1024,256]{2,1,0:T(8,128)(2,1)} %shard_map.89), calls=%async_computation.3 | async-start | bytes 4194304 | tf_op jit(solution)/shard_map/all_to_all | solution.py:526
  170.9 2.2 %reduce_sum.24 = bf16[1024,256]{1,0:T(8,128)(2,1)S(1)} reduce(bf16[4,1024,256]{2,1,0:T(8,128)(2,1)} %all-to-all-done.2, bf16[]{:T(256)} %constant.124.clone.1), dimensions={0}, to_apply=%region_0.1 | reduce | flops 786432 | bytes 2621442 | tf_op jit(solution)/shard_map/reduce_sum | solution.py:527
  173.1 9.9 %collective-permute-done.19 = bf16[512,1024]{1,0:T(8,128)(2,1)} collective-permute-done((bf16[512,1024]{1,0:T(8,128)(2,1)}, bf16[512,1024]{1,0:T(8,128)(2,1)}, u32[]{:S(2)}, u32[]{:S(2)}) %collective-permute-start.19) | collective-permute-done | bytes 1048608 | tf_op jit(solution)/shard_map/ppermute | solution.py:30
  183.0 2.3 %add_convert_fusion.1 = bf16[256,1024]{1,0:T(8,128)(2,1)} fusion(f32[256,1024]{1,0:T(8,128)} %get-tuple-element.94, bf16[512,1024]{1,0:T(8,128)(2,1)} %collective-permute-done.19), kind=kLoop, calls=%fused_computation.5 | loop fusion | flops 786432 | bytes 2097152 | tf_op jit(solution)/shard_map/convert_element_type | solution.py:44
  185.3 3.7 %collective-permute-start.22 = (bf16[256,1024]{1,0:T(8,128)(2,1)}, bf16[256,1024]{1,0:T(8,128)(2,1)S(1)}, u32[]{:S(2)}, u32[]{:S(2)}) collective-permute-start(bf16[256,1024]{1,0:T(8,128)(2,1)} %add_convert_fusion.1), channel_id=1, source_target_pairs={{0,48},{1,49},{2,50},{3,51},{4,52},{5,53},{6,54},{7,55},{8,56},{9,... | collective-permute-start | bytes 1572872 | tf_op jit(solution)/shard_map/ppermute | solution.py:30
  196.4 3.0 %collective-permute-done.30 = bf16[1024,128]{1,0:T(8,128)(2,1)} collective-permute-done((bf16[1024,128]{1,0:T(8,128)(2,1)}, bf16[1024,128]{1,0:T(8,128)(2,1)}, u32[]{:S(2)}, u32[]{:S(2)}) %collective-permute-start.30) | collective-permute-done | bytes 262176 | tf_op jit(solution)/shard_map/ppermute | solution.py:30
  202.1 3.3 %collective-permute-done.21 = bf16[256,1024]{1,0:T(8,128)(2,1)} collective-permute-done((bf16[256,1024]{1,0:T(8,128)(2,1)}, bf16[256,1024]{1,0:T(8,128)(2,1)}, u32[]{:S(2)}, u32[]{:S(2)}) %collective-permute-start.21) | collective-permute-done | bytes 524320 | tf_op jit(solution)/shard_map/ppermute | solution.py:30
  205.5 2.5 %add_convert_fusion.2 = (bf16[256,1024]{1,0:T(8,128)(2,1)S(1)}, bf16[256,1024]{1,0:T(8,128)(2,1)S(1)}) fusion(bf16[256,1024]{1,0:T(8,128)(2,1)} %collective-permute-done.21, f32[512,1024]{1,0:T(8,128)} %get-tuple-element.90, bf16[512,1024]{1,0:T(8,128)(2,1)} %collective-permute-done.19, bf16[256,1024]{1,0:T(8,128)(2,1)S(1)} %collective-permute-done.22, ...), kind=kLoop, calls=%fused_computation.6 | loop fusion | flops 2621440 | bytes 5242880 | tf_op jit(solution)/shard_map/convert.2
  (108 shorter events, 39.0 us)
Async XLA Ops:
  2.2 6.4 %collective-permute-start = (bf16[512,512]{1,0:T(8,128)(2,1)S(1)}, bf16[512,512]{1,0:T(8,128)(2,1)S(1)}, u32[]{:S(2)}, u32[]{:S(2)}) collective-permute-start(bf16[512,512]{1,0:T(8,128)(2,1)S(1)} %get-tuple-element.52), channel_id=1, source_target_pairs={{0,1},{1,0},{2,3},{3,2},{4,5},{5,4},{6,7},{7,6},{8,9},{9,8},{10,11... | collective-permute-start | bytes 1572872 | tf_op jit(solution)/shard_map/ppermute | solution.py:30
  10.3 16.5 %collective-permute-start.5 = (bf16[64,4096]{1,0:T(8,128)(2,1)S(1)}, bf16[64,4096]{1,0:T(8,128)(2,1)S(1)}, u32[]{:S(2)}, u32[]{:S(2)}) collective-permute-start(bf16[64,4096]{1,0:T(8,128)(2,1)S(1)} %get-tuple-element.113), channel_id=1, source_target_pairs={{0,64},{1,65},{2,66},{3,67},{4,68},{5,69},{6,70},{7,71},{8,72},{9,... | collective-permute-start | bytes 1572872 | tf_op jit(solution)/shard_map/ppermute | solution.py:30
  12.3 14.5 %collective-permute-start.6 = (bf16[64,4096]{1,0:T(8,128)(2,1)S(1)}, bf16[64,4096]{1,0:T(8,128)(2,1)S(1)}, u32[]{:S(2)}, u32[]{:S(2)}) collective-permute-start(bf16[64,4096]{1,0:T(8,128)(2,1)S(1)} %get-tuple-element.112), channel_id=1, source_target_pairs={{0,66},{1,67},{2,64},{3,65},{4,70},{5,71},{6,68},{7,69},{8,74},{9,... | collective-permute-start | bytes 1572872 | tf_op jit(solution)/shard_map/ppermute | solution.py:30
  27.8 40.7 %collective-permute-start.7 = (bf16[128,4096]{1,0:T(8,128)(2,1)}, bf16[128,4096]{1,0:T(8,128)(2,1)}, u32[]{:S(2)}, u32[]{:S(2)}) collective-permute-start(bf16[128,4096]{1,0:T(8,128)(2,1)} %shard_map.82.refs_0_), channel_id=1, source_target_pairs={{0,4},{1,5},{2,6},{3,7},{4,8},{5,9},{6,10},{7,11},{8,12},{9,13},{1... | collective-permute-start | bytes 3145736 | tf_op jit(solution)/shard_map/ppermute | solution.py:30
  29.3 39.2 %collective-permute-start.8 = (bf16[128,4096]{1,0:T(8,128)(2,1)}, bf16[128,4096]{1,0:T(8,128)(2,1)S(1)}, u32[]{:S(2)}, u32[]{:S(2)}) collective-permute-start(bf16[128,4096]{1,0:T(8,128)(2,1)} %shard_map.82.refs_0_), channel_id=1, source_target_pairs={{0,12},{1,13},{2,14},{3,15},{4,0},{5,1},{6,2},{7,3},{8,4},{9,5},{1... | collective-permute-start | bytes 3145736 | tf_op jit(solution)/shard_map/ppermute | solution.py:30
  29.9 14.1 %all-to-all-start = ((bf16[4,144,512]{2,1,0:T(8,128)(2,1)}), bf16[4,144,512]{2,1,0:T(8,128)(2,1)S(1)}, u32[]{:S(2)}, u32[]{:S(2)}) async-start(bf16[4,144,512]{2,1,0:T(8,128)(2,1)} %shard_map.77), calls=%async_computation | async-start | bytes 1179648 | tf_op jit(solution)/shard_map/all_to_all | solution.py:469
  34.3 12.3 %collective-permute-start.2 = (bf16[1024,128]{1,0:T(8,128)(2,1)S(1)}, bf16[1024,128]{1,0:T(8,128)(2,1)S(1)}, u32[]{:S(2)}, u32[]{:S(2)}) collective-permute-start(bf16[1024,128]{1,0:T(8,128)(2,1)S(1)} %get-tuple-element.60), channel_id=1, source_target_pairs={{0,64},{1,65},{2,66},{3,67},{4,68},{5,69},{6,70},{7,71},{8,72},{9,... | collective-permute-start | bytes 786440 | tf_op jit(solution)/shard_map/ppermute | solution.py:30
  35.6 17.0 %collective-permute-start.3 = (bf16[1024,128]{1,0:T(8,128)(2,1)S(1)}, bf16[1024,128]{1,0:T(8,128)(2,1)S(1)}, u32[]{:S(2)}, u32[]{:S(2)}) collective-permute-start(bf16[1024,128]{1,0:T(8,128)(2,1)S(1)} %get-tuple-element.61), channel_id=1, source_target_pairs={{0,2},{1,3},{2,0},{3,1},{4,6},{5,7},{6,4},{7,5},{8,10},{9,11},{10,... | collective-permute-start | bytes 786440 | tf_op jit(solution)/shard_map/ppermute | solution.py:30
  38.8 13.7 %collective-permute-start.4 = (bf16[1024,128]{1,0:T(8,128)(2,1)S(1)}, bf16[1024,128]{1,0:T(8,128)(2,1)S(1)}, u32[]{:S(2)}, u32[]{:S(2)}) collective-permute-start(bf16[1024,128]{1,0:T(8,128)(2,1)S(1)} %get-tuple-element.62), channel_id=1, source_target_pairs={{0,66},{1,67},{2,64},{3,65},{4,70},{5,71},{6,68},{7,69},{8,74},{9,... | collective-permute-start | bytes 786440 | tf_op jit(solution)/shard_map/ppermute | solution.py:30
  46.7 5.9 %collective-permute-start.1 = (bf16[192,512]{1,0:T(8,128)(2,1)}, bf16[192,512]{1,0:T(8,128)(2,1)S(1)}, u32[]{:S(2)}, u32[]{:S(2)}) collective-permute-start(bf16[192,512]{1,0:T(8,128)(2,1)} %get-tuple-element.55.sent_ref), channel_id=1, source_target_pairs={{0,64},{1,65},{2,66},{3,67},{4,68},{5,69},{6,70},{7,71},{8,72},{9,... | collective-permute-start | bytes 589832 | tf_op jit(solution)/shard_map/ppermute | solution.py:30
  76.5 21.9 %collective-permute-start.9 = (bf16[1024,512]{1,0:T(8,128)(2,1)}, bf16[1024,512]{1,0:T(8,128)(2,1)S(1)}, u32[]{:S(2)}, u32[]{:S(2)}) collective-permute-start(bf16[1024,512]{1,0:T(8,128)(2,1)} %get-tuple-element.95.refs_0_), channel_id=1, source_target_pairs={{0,64},{1,65},{2,66},{3,67},{4,68},{5,69},{6,70},{7,71},{8,72},{9,... | collective-permute-start | bytes 3145736 | tf_op jit(solution)/shard_map/ppermute | solution.py:30
  78.0 22.7 %collective-permute-start.10 = (bf16[1024,512]{1,0:T(8,128)(2,1)}, bf16[1024,512]{1,0:T(8,128)(2,1)}, u32[]{:S(2)}, u32[]{:S(2)}) collective-permute-start(bf16[1024,512]{1,0:T(8,128)(2,1)} %get-tuple-element.95.refs_0_), channel_id=1, source_target_pairs={{0,66},{1,67},{2,64},{3,65},{4,70},{5,71},{6,68},{7,69},{8,74},{9,... | collective-permute-start | bytes 3145736 | tf_op jit(solution)/shard_map/ppermute | solution.py:30
  80.9 21.8 %collective-permute-start.11 = (bf16[2,2048,128]{2,1,0:T(8,128)(2,1)S(1)}, bf16[2,2048,128]{2,1,0:T(8,128)(2,1)S(1)}, u32[]{:S(2)}, u32[]{:S(2)}) collective-permute-start(bf16[2,2048,128]{2,1,0:T(8,128)(2,1)S(1)} %pad_maximum_fusion.1.own_ref), channel_id=1, source_target_pairs={{0,16},{1,17},{2,18},{3,19},{4,20},{5,21},{6,22},{7,23},{8,24},{9,... | collective-permute-start | bytes 3145736 | tf_op jit(solution)/shard_map/ppermute | solution.py:30
  81.5 21.2 %collective-permute-start.12 = (bf16[2,2048,128]{2,1,0:T(8,128)(2,1)S(1)}, bf16[2,2048,128]{2,1,0:T(8,128)(2,1)S(1)}, u32[]{:S(2)}, u32[]{:S(2)}) collective-permute-start(bf16[2,2048,128]{2,1,0:T(8,128)(2,1)S(1)} %pad_maximum_fusion.1.own_ref), channel_id=1, source_target_pairs={{0,48},{1,49},{2,50},{3,51},{4,52},{5,53},{6,54},{7,55},{8,56},{9,... | collective-permute-start | bytes 3145736 | tf_op jit(solution)/shard_map/ppermute | solution.py:30
  84.2 36.6 %collective-permute-start.15 = (bf16[128,4096]{1,0:T(8,128)(2,1)}, bf16[128,4096]{1,0:T(8,128)(2,1)}, u32[]{:S(2)}, u32[]{:S(2)}) collective-permute-start(bf16[128,4096]{1,0:T(8,128)(2,1)} %collective-permute-done.7.refs_3_), channel_id=1, source_target_pairs={{0,4},{1,5},{2,6},{3,7},{4,8},{5,9},{6,10},{7,11},{8,12},{9,13},{1... | collective-permute-start | bytes 3145736 | tf_op jit(solution)/shard_map/ppermute | solution.py:30
  98.4 27.6 %collective-permute-start.16 = (bf16[1024,512]{1,0:T(8,128)(2,1)S(1)}, bf16[1024,512]{1,0:T(8,128)(2,1)}, u32[]{:S(2)}, u32[]{:S(2)}) collective-permute-start(bf16[1024,512]{1,0:T(8,128)(2,1)S(1)} %collective-permute-done.9.refs_0_.q_ref), channel_id=1, source_target_pairs={{0,1},{1,0},{2,3},{3,2},{4,5},{5,4},{6,7},{7,6},{8,9},{9,8},{10,11... | collective-permute-start | bytes 3145736 | tf_op jit(solution)/shard_map/ppermute | solution.py:30
  100.6 25.4 %collective-permute-start.17 = (bf16[1024,512]{1,0:T(8,128)(2,1)}, bf16[1024,512]{1,0:T(8,128)(2,1)}, u32[]{:S(2)}, u32[]{:S(2)}) collective-permute-start(bf16[1024,512]{1,0:T(8,128)(2,1)} %collective-permute-done.10.refs_2_), channel_id=1, source_target_pairs={{0,1},{1,0},{2,3},{3,2},{4,5},{5,4},{6,7},{7,6},{8,9},{9,8},{10,11... | collective-permute-start | bytes 3145736 | tf_op jit(solution)/shard_map/ppermute | solution.py:30
  103.6 14.6 %collective-permute-start.13 = (bf16[1,2048,128]{2,1,0:T(8,128)(2,1)}, bf16[1,2048,128]{2,1,0:T(8,128)(2,1)}, u32[]{:S(2)}, u32[]{:S(2)}) collective-permute-start(bf16[1,2048,128]{2,1,0:T(8,128)(2,1)} %slice.50), channel_id=1, source_target_pairs={{0,16},{1,17},{2,18},{3,19},{4,20},{5,21},{6,22},{7,23},{8,24},{9,... | collective-permute-start | bytes 1572872 | tf_op jit(solution)/shard_map/ppermute | solution.py:30
  104.7 13.4 %collective-permute-start.14 = (bf16[1,2048,128]{2,1,0:T(8,128)(2,1)}, bf16[1,2048,128]{2,1,0:T(8,128)(2,1)}, u32[]{:S(2)}, u32[]{:S(2)}) collective-permute-start(bf16[1,2048,128]{2,1,0:T(8,128)(2,1)} %slice.51), channel_id=1, source_target_pairs={{0,48},{1,49},{2,50},{3,51},{4,52},{5,53},{6,54},{7,55},{8,56},{9,... | collective-permute-start | bytes 1572872 | tf_op jit(solution)/shard_map/ppermute | solution.py:30
  133.8 9.5 %collective-permute-start.18 = (bf16[512,4096]{1,0:T(8,128)(2,1)}, bf16[512,4096]{1,0:T(8,128)(2,1)}, u32[]{:S(2)}, u32[]{:S(2)}) collective-permute-start(bf16[512,4096]{1,0:T(8,128)(2,1)} %shard_map.86.hx_ref), channel_id=1, source_target_pairs={{0,1},{1,0},{2,3},{3,2},{4,5},{5,4},{6,7},{7,6},{8,9},{9,8},{10,11... | collective-permute-start | bytes 12582920 | tf_op jit(solution)/shard_map/ppermute | solution.py:30
  133.8 32.1 %all-to-all-start.2 = ((bf16[4,1024,256]{2,1,0:T(8,128)(2,1)}), bf16[4,1024,256]{2,1,0:T(8,128)(2,1)}, u32[]{:S(2)}, u32[]{:S(2)}) async-start(bf16[4,1024,256]{2,1,0:T(8,128)(2,1)} %shard_map.87), calls=%async_computation.2 | async-start | bytes 4194304 | tf_op jit(solution)/shard_map/all_to_all | solution.py:516
  141.2 14.6 %collective-permute-start.23 = (bf16[512,512]{1,0:T(8,128)(2,1)S(1)}, bf16[512,512]{1,0:T(8,128)(2,1)S(1)}, u32[]{:S(2)}, u32[]{:S(2)}) collective-permute-start(bf16[512,512]{1,0:T(8,128)(2,1)S(1)} %slice.58), channel_id=1, source_target_pairs={{0,64},{1,65},{2,66},{3,67},{4,68},{5,69},{6,70},{7,71},{8,72},{9,... | collective-permute-start | bytes 1572872 | tf_op jit(solution)/shard_map/ppermute | solution.py:30
  141.3 15.2 %collective-permute-start.24 = (bf16[512,512]{1,0:T(8,128)(2,1)S(1)}, bf16[512,512]{1,0:T(8,128)(2,1)S(1)}, u32[]{:S(2)}, u32[]{:S(2)}) collective-permute-start(bf16[512,512]{1,0:T(8,128)(2,1)S(1)} %slice.59), channel_id=1, source_target_pairs={{0,66},{1,67},{2,64},{3,65},{4,70},{5,71},{6,68},{7,69},{8,74},{9,... | collective-permute-start | bytes 1572872 | tf_op jit(solution)/shard_map/ppermute | solution.py:30
  143.3 16.6 %collective-permute-start.25 = (bf16[1024,512]{1,0:T(8,128)(2,1)S(1)}, bf16[1024,512]{1,0:T(8,128)(2,1)S(1)}, u32[]{:S(2)}, u32[]{:S(2)}) collective-permute-start(bf16[1024,512]{1,0:T(8,128)(2,1)S(1)} %copy-done.8), channel_id=1, source_target_pairs={{0,1},{1,0},{2,3},{3,2},{4,5},{5,4},{6,7},{7,6},{8,9},{9,8},{10,11... | collective-permute-start | bytes 3145736 | tf_op jit(solution)/shard_map/ppermute | solution.py:30
  157.0 26.0 %collective-permute-start.19 = (bf16[512,1024]{1,0:T(8,128)(2,1)}, bf16[512,1024]{1,0:T(8,128)(2,1)}, u32[]{:S(2)}, u32[]{:S(2)}) collective-permute-start(bf16[512,1024]{1,0:T(8,128)(2,1)} %get-tuple-element.91), channel_id=1, source_target_pairs={{0,48},{1,49},{2,50},{3,51},{4,52},{5,53},{6,54},{7,55},{8,56},{9,... | collective-permute-start | bytes 3145736 | tf_op jit(solution)/shard_map/ppermute | solution.py:30
  159.9 29.1 %collective-permute-start.20 = (bf16[512,1024]{1,0:T(8,128)(2,1)}, bf16[512,1024]{1,0:T(8,128)(2,1)}, u32[]{:S(2)}, u32[]{:S(2)}) collective-permute-start(bf16[512,1024]{1,0:T(8,128)(2,1)} %get-tuple-element.93), channel_id=1, source_target_pairs={{0,16},{1,17},{2,18},{3,19},{4,20},{5,21},{6,22},{7,23},{8,24},{9,... | collective-permute-start | bytes 3145736 | tf_op jit(solution)/shard_map/ppermute | solution.py:30
  165.9 29.9 %all-to-all-start.3 = ((bf16[4,1024,256]{2,1,0:T(8,128)(2,1)}), bf16[4,1024,256]{2,1,0:T(8,128)(2,1)S(1)}, u32[]{:S(2)}, u32[]{:S(2)}) async-start(bf16[4,1024,256]{2,1,0:T(8,128)(2,1)} %shard_map.89), calls=%async_computation.3 | async-start | bytes 4194304 | tf_op jit(solution)/shard_map/all_to_all | solution.py:526
  185.3 16.8 %collective-permute-start.22 = (bf16[256,1024]{1,0:T(8,128)(2,1)}, bf16[256,1024]{1,0:T(8,128)(2,1)S(1)}, u32[]{:S(2)}, u32[]{:S(2)}) collective-permute-start(bf16[256,1024]{1,0:T(8,128)(2,1)} %add_convert_fusion.1), channel_id=1, source_target_pairs={{0,48},{1,49},{2,50},{3,51},{4,52},{5,53},{6,54},{7,55},{8,56},{9,... | collective-permute-start | bytes 1572872 | tf_op jit(solution)/shard_map/ppermute | solution.py:30
  191.0 14.5 %collective-permute-start.21 = (bf16[256,1024]{1,0:T(8,128)(2,1)}, bf16[256,1024]{1,0:T(8,128)(2,1)}, u32[]{:S(2)}, u32[]{:S(2)}) collective-permute-start(bf16[256,1024]{1,0:T(8,128)(2,1)} %add_convert_fusion.3), channel_id=1, source_target_pairs={{0,16},{1,17},{2,18},{3,19},{4,20},{5,21},{6,22},{7,23},{8,24},{9,... | collective-permute-start | bytes 1572872 | tf_op jit(solution)/shard_map/ppermute | solution.py:30
  191.8 7.7 %collective-permute-start.30 = (bf16[1024,128]{1,0:T(8,128)(2,1)}, bf16[1024,128]{1,0:T(8,128)(2,1)}, u32[]{:S(2)}, u32[]{:S(2)}) collective-permute-start(bf16[1024,128]{1,0:T(8,128)(2,1)} %get-tuple-element.119), channel_id=1, source_target_pairs={{0,64},{1,65},{2,66},{3,67},{4,68},{5,69},{6,70},{7,71},{8,72},{9,... | collective-permute-start | bytes 786440 | tf_op jit(solution)/shard_map/ppermute | solution.py:30
  193.1 16.3 %collective-permute-start.28 = (bf16[1024,128]{1,0:T(8,128)(2,1)S(1)}, bf16[1024,128]{1,0:T(8,128)(2,1)}, u32[]{:S(2)}, u32[]{:S(2)}) collective-permute-start(bf16[1024,128]{1,0:T(8,128)(2,1)S(1)} %get-tuple-element.118), channel_id=1, source_target_pairs={{0,66},{1,67},{2,64},{3,65},{4,70},{5,71},{6,68},{7,69},{8,74},{9,... | collective-permute-start | bytes 786440 | tf_op jit(solution)/shard_map/ppermute | solution.py:30
  200.4 9.0 %collective-permute-start.29 = (bf16[1024,128]{1,0:T(8,128)(2,1)S(1)}, bf16[1024,128]{1,0:T(8,128)(2,1)S(1)}, u32[]{:S(2)}, u32[]{:S(2)}) collective-permute-start(bf16[1024,128]{1,0:T(8,128)(2,1)S(1)} %get-tuple-element.120), channel_id=1, source_target_pairs={{0,2},{1,3},{2,0},{3,1},{4,6},{5,7},{6,4},{7,5},{8,10},{9,11},{10,... | collective-permute-start | bytes 786440 | tf_op jit(solution)/shard_map/ppermute | solution.py:30
  (16 other events, 121.4 us)

commit v5 on v2

--- a/solution.py
+++ b/solution.py
@@ -305,10 +305,14 @@
 
 
 def stacked(sources):
-    rows = sum(a.shape[0] for a in sources)
+    rows, wide = sum(a.shape[0] for a in sources), sources[0].shape[1]
+    block = lambda n: pl.BlockSpec((n, wide // 4), lambda c: (0, c))
     return pl.pallas_call(
         stack_kernel,
-        out_shape=pltpu.HBM((rows, sources[0].shape[1]), BF16),
+        out_shape=pltpu.HBM((rows, wide), BF16),
+        grid=(4,),
+        in_specs=[block(a.shape[0]) for a in sources],
+        out_specs=block(rows),
         compiler_params=params(12),
     )(*sources)
 

time: 198 us -> 197 us (level)
  no operation moved by 1% of the time
where the time goes in v5:
time: 197 us; the launch traced here: 196 us
  Pallas kernels  68.3 us (35%)
  starting transfers between devices  56.3 us (29%)
  waiting for transfers between devices  44 us (22%)
  other arithmetic  16 us (8%)
  local copies, waits for them, and re-layouts  10.6 us (5%)
    ppermute x31, starting transfers between devices, mover(): return lambda a: lax.ppermute(a, AXES, pairs)  37.6 us
    ppermute x31, waiting for transfers between devices, mover(): return lambda a: lax.ppermute(a, AXES, pairs)  30.8 us
    pallas_call x2, Pallas kernels, hidden_terms(): pl.pallas_call(hidden_kernel, out_shape=pltpu.HBM((4, rows, wide // 4), B...  13 us
    pallas_call x1, Pallas kernels, weight_terms(): pl.pallas_call(weight_kernel, out_shape=shapes, grid_spec=pltpu.PrefetchS...  12.5 us
    pallas_call x1, Pallas kernels, weight_here(): pl.pallas_call(here_kernel, out_shape=pltpu.HBM((ch, 4 * feat), F32), gri...  10.3 us
    pallas_call x1, Pallas kernels, grad_z_of(): pl.pallas_call(functools.partial(grad_z_kernel, scale=2.0 / rows), out_sh...  7.26 us
    pallas_call x2, Pallas kernels, stacked(): pl.pallas_call(stack_kernel, out_shape=pltpu.HBM((rows, wide), BF16), gri...  6.45 us
    pallas_call x1, Pallas kernels, moments(): pl.pallas_call(moments_kernel, out_shape=pltpu.HBM((4, ch // 4 + 16, ch),...  6.03 us
  transfers between devices with their start and end apart: 35, of which 10 were waited for; matrix products, arithmetic and copies ran while one was open for 10% of the time, Pallas kernels for 31%

profile of v5, /device:TPU:2, one launch (start us, length us, event | category | flops | bytes accessed | tf_op | source)
XLA Modules:
  0.0 196.3 jit_solution(2504089522027169247)
XLA Ops:
  2.6 6.0 %shard_map.77 = bf16[4,144,512]{2,1,0:T(8,128)(2,1)} custom-call(bf16[1024,512]{1,0:T(8,128)(2,1)} %z_ref.3, bf16[1024,512]{1,0:T(8,128)(2,1)} %g_ref.3, f32[512,512]{1,0:T(8,128)} %u_ref.7), custom_call_target="tpu_custom_call" | custom-call | flops 2147483648 | bytes 3670016 | tf_op jit(solution)/shard_map/pallas_call | solution.py:103
  13.0 2.2 %collective-permute-start.6 = (bf16[64,4096]{1,0:T(8,128)(2,1)S(1)}, bf16[64,4096]{1,0:T(8,128)(2,1)S(1)}, u32[]{:S(2)}, u32[]{:S(2)}) collective-permute-start(bf16[64,4096]{1,0:T(8,128)(2,1)S(1)} %get-tuple-element.108), channel_id=1, source_target_pairs={{0,66},{1,67},{2,64},{3,65},{4,70},{5,71},{6,68},{7,69},{8,74},{9,... | collective-permute-start | bytes 1572872 | tf_op jit(solution)/shard_map/ppermute | solution.py:30
  15.2 4.5 %all-to-all-start = ((bf16[4,144,512]{2,1,0:T(8,128)(2,1)}), bf16[4,144,512]{2,1,0:T(8,128)(2,1)S(1)}, u32[]{:S(2)}, u32[]{:S(2)}) async-start(bf16[4,144,512]{2,1,0:T(8,128)(2,1)} %shard_map.77), calls=%async_computation | async-start | bytes 1179648 | tf_op jit(solution)/shard_map/all_to_all | solution.py:473
  19.6 3.4 %collective-permute-start.3 = (bf16[1024,128]{1,0:T(8,128)(2,1)S(1)}, bf16[1024,128]{1,0:T(8,128)(2,1)}, u32[]{:S(2)}, u32[]{:S(2)}) collective-permute-start(bf16[1024,128]{1,0:T(8,128)(2,1)S(1)} %get-tuple-element.59), channel_id=1, source_target_pairs={{0,2},{1,3},{2,0},{3,1},{4,6},{5,7},{6,4},{7,5},{8,10},{9,11},{10,... | collective-permute-start | bytes 786440 | tf_op jit(solution)/shard_map/ppermute | solution.py:30
  24.3 5.7 %all-to-all-done.got_ref = bf16[4,144,512]{2,1,0:T(8,128)(2,1)S(1)} async-done(((bf16[4,144,512]{2,1,0:T(8,128)(2,1)}), bf16[4,144,512]{2,1,0:T(8,128)(2,1)S(1)}, u32[]{:S(2)}, u32[]{:S(2)}) %all-to-all-start) | async-done | bytes 589856 | tf_op jit(solution)/shard_map/all_to_all | solution.py:473
  36.5 5.1 %shard_map.80 = (f32[512,512]{1,0:T(8,128)}, f32[1024,512]{1,0:T(8,128)}) custom-call(f32[512,512]{1,0:T(8,128)} %u_ref.7, f32[1,512]{1,0:T(1,128)S(1)} %bitcast.24, bf16[1024,512]{1,0:T(8,128)(2,1)} %g_ref.3), custom_call_target="tpu_custom_call" | custom-call | flops 1879048192 | bytes 5242880 | tf_op jit(solution)/shard_map/pallas_call | solution.py:190
  43.2 3.0 %shard_map.81 = (bf16[4,128,512]{2,1,0:T(8,128)(2,1)}, f32[8,512]{1,0:T(8,128)}) custom-call(s32[1]{0:T(128)} %bitcast.6.y_ref, f32[128,512]{1,0:T(8,128)} %get-tuple-element.52.quarter_ref, bf16[192,512]{1,0:T(8,128)(2,1)} %get-tuple-element.53.sent_ref, bf16[192,512]{1,0:T(8,128)(2,1)} %copy-done.10, f32[512,512]{1,0:T(8,128)} %u_ref.7, f32[512,512]{1,0:T(8,128)} %u_ref.7, ...), custom_call_target="tpu_custom_call" | custom-call | tf_op jit(solution)/shard_map/pallas_call | solution.py:158
  46.2 4.5 %all-to-all-start.1 = ((bf16[4,128,512]{2,1,0:T(8,128)(2,1)}), bf16[4,128,512]{2,1,0:T(8,128)(2,1)}, u32[]{:S(2)}, u32[]{:S(2)}) async-start(bf16[4,128,512]{2,1,0:T(8,128)(2,1)} %get-tuple-element.62), calls=%async_computation.1 | async-start | bytes 1048576 | tf_op jit(solution)/shard_map/all_to_all | solution.py:491
  52.8 2.1 %collective-permute-start.11 = (bf16[2,2048,128]{2,1,0:T(8,128)(2,1)S(1)}, bf16[2,2048,128]{2,1,0:T(8,128)(2,1)S(1)}, u32[]{:S(2)}, u32[]{:S(2)}) collective-permute-start(bf16[2,2048,128]{2,1,0:T(8,128)(2,1)S(1)} %pad_maximum_fusion.1.own_ref), channel_id=1, source_target_pairs={{0,16},{1,17},{2,18},{3,19},{4,20},{5,21},{6,22},{7,23},{8,24},{9,... | collective-permute-start | bytes 3145736 | tf_op jit(solution)/shard_map/ppermute | solution.py:30
  56.2 5.5 %all-to-all-done.1 = bf16[4,128,512]{2,1,0:T(8,128)(2,1)} async-done(((bf16[4,128,512]{2,1,0:T(8,128)(2,1)}), bf16[4,128,512]{2,1,0:T(8,128)(2,1)}, u32[]{:S(2)}, u32[]{:S(2)}) %all-to-all-start.1) | async-done | bytes 524320 | tf_op jit(solution)/shard_map/all_to_all | solution.py:491
  63.5 7.3 %shard_map.83 = (bf16[1024,512]{1,0:T(8,128)(2,1)}, bf16[512,1024]{1,0:T(8,128)(2,1)}) custom-call(f32[512,512]{1,0:T(8,128)} %u_ref.7, bf16[512,512]{1,0:T(8,128)(2,1)} %bitcast.9.inner_ref, bf16[1024,512]{1,0:T(8,128)(2,1)} %z_ref.3, f32[1024,512]{1,0:T(8,128)} %get-tuple-element.65.first_ref, f32[512,512]{1,0:T(8,128)} %get-tuple-element.66.wsum_ref, ...), custom_call_target="tpu_custom_call" | custom-call | flops 2415919104 | bytes 6815744 | tf_op jit(solution)/shard_map/pallas_call | solution.py:214
  70.7 2.2 %collective-permute-start.10 = (bf16[1024,512]{1,0:T(8,128)(2,1)}, bf16[1024,512]{1,0:T(8,128)(2,1)}, u32[]{:S(2)}, u32[]{:S(2)}) collective-permute-start(bf16[1024,512]{1,0:T(8,128)(2,1)} %get-tuple-element.91.refs_0_), channel_id=1, source_target_pairs={{0,66},{1,67},{2,64},{3,65},{4,70},{5,71},{6,68},{7,69},{8,74},{9,... | collective-permute-start | bytes 3145736 | tf_op jit(solution)/shard_map/ppermute | solution.py:30
  74.0 8.2 %collective-permute-done.11.left_ref = bf16[2,2048,128]{2,1,0:T(8,128)(2,1)S(1)} collective-permute-done((bf16[2,2048,128]{2,1,0:T(8,128)(2,1)S(1)}, bf16[2,2048,128]{2,1,0:T(8,128)(2,1)S(1)}, u32[]{:S(2)}, u32[]{:S(2)}) %collective-permute-start.11) | collective-permute-done | bytes 1048608 | tf_op jit(solution)/shard_map/ppermute | solution.py:30
  85.4 2.8 %collective-permute-start.14 = (bf16[1,2048,128]{2,1,0:T(8,128)(2,1)}, bf16[1,2048,128]{2,1,0:T(8,128)(2,1)}, u32[]{:S(2)}, u32[]{:S(2)}) collective-permute-start(bf16[1,2048,128]{2,1,0:T(8,128)(2,1)} %slice.51), channel_id=1, source_target_pairs={{0,48},{1,49},{2,50},{3,51},{4,52},{5,53},{6,54},{7,55},{8,56},{9,... | collective-permute-start | bytes 1572872 | tf_op jit(solution)/shard_map/ppermute | solution.py:30
  88.4 10.3 %shard_map.84.own_ref = f32[512,4096]{1,0:T(8,128)} custom-call(s32[6]{0:T(128)S(1)} %stack.63.idx_ref, bf16[512,1024]{1,0:T(8,128)(2,1)} %get-tuple-element.74.p_ref, bf16[1024,8192]{1,0:T(8,128)(2,1)} %own_ref), custom_call_target="tpu_custom_call" | custom-call | flops 4294967296 | bytes 16777216 | tf_op jit(solution)/shard_map/pallas_call | solution.py:381
  98.7 2.4 %shard_map.85.refs_4_.refs_6_ = bf16[2048,1024]{1,0:T(8,128)(2,1)S(1)} custom-call(s32[8]{0:T(128)S(1)} %stack.75.idx_ref, bf16[2,2048,128]{2,1,0:T(8,128)(2,1)S(1)} %pad_maximum_fusion.1.own_ref, bf16[2,2048,128]{2,1,0:T(8,128)(2,1)} %collective-permute-done.12.right_ref, bf16[1,2048,128]{2,1,0:T(8,128)(2,1)} %collective-permute-done.13.two_a_ref, ...), custom_call_target="tpu_custom_call" | custom-call | tf_op jit(solution)/shard_map/pallas_call | solution.py:289
  101.1 4.8 %shard_map.86.hx_ref = bf16[512,4096]{1,0:T(8,128)(2,1)} custom-call(bf16[128,4096]{1,0:T(8,128)(2,1)S(1)} %copy-done.3, bf16[128,4096]{1,0:T(8,128)(2,1)S(1)} %copy-done.5, bf16[128,4096]{1,0:T(8,128)(2,1)} %collective-permute-done.15.refs_2_, bf16[128,4096]{1,0:T(8,128)(2,1)} %collective-permute-done.7.refs_3_), custom_call_target="tpu_custom_call" | custom-call | tf_op jit(solution)/shard_map/pallas_call | solution.py:310
  106.5 2.7 %collective-permute-done.16.refs_1_ = bf16[1024,512]{1,0:T(8,128)(2,1)S(1)} collective-permute-done((bf16[1024,512]{1,0:T(8,128)(2,1)S(1)}, bf16[1024,512]{1,0:T(8,128)(2,1)S(1)}, u32[]{:S(2)}, u32[]{:S(2)}) %collective-permute-start.16) | collective-permute-done | bytes 1048608 | tf_op jit(solution)/shard_map/ppermute | solution.py:30
  110.4 7.1 %shard_map.87 = bf16[4,1024,256]{2,1,0:T(8,128)(2,1)} custom-call(bf16[1024,512]{1,0:T(8,128)(2,1)S(1)} %collective-permute-done.9.refs_0_.q_ref, bf16[1024,512]{1,0:T(8,128)(2,1)S(1)} %collective-permute-done.16.refs_1_, bf16[1024,512]{1,0:T(8,128)(2,1)} %collective-permute-done.10.refs_2_, bf16[1024,512]{1,0:T(8,128)(2,1)S(1)} %collective-permute-done.17.refs_3_, ...), custom_call_target="tpu_custom_call" | custom-call | flops 4294967296 | bytes 10485760 | tf_op jit(solution)/shard_map/pallas_call | solution.py:366
  117.6 5.0 %all-to-all-start.2 = ((bf16[4,1024,256]{2,1,0:T(8,128)(2,1)}), bf16[4,1024,256]{2,1,0:T(8,128)(2,1)}, u32[]{:S(2)}, u32[]{:S(2)}) async-start(bf16[4,1024,256]{2,1,0:T(8,128)(2,1)} %shard_map.87), calls=%async_computation.2 | async-start | bytes 4194304 | tf_op jit(solution)/shard_map/all_to_all | solution.py:519
  124.8 2.8 %collective-permute-start.24 = (bf16[512,512]{1,0:T(8,128)(2,1)S(1)}, bf16[512,512]{1,0:T(8,128)(2,1)S(1)}, u32[]{:S(2)}, u32[]{:S(2)}) collective-permute-start(bf16[512,512]{1,0:T(8,128)(2,1)S(1)} %slice.59), channel_id=1, source_target_pairs={{0,66},{1,67},{2,64},{3,65},{4,70},{5,71},{6,68},{7,69},{8,74},{9,... | collective-permute-start | bytes 1572872 | tf_op jit(solution)/shard_map/ppermute | solution.py:30
  127.7 12.5 %shard_map.88 = (bf16[512,1024]{1,0:T(8,128)(2,1)}, bf16[512,1024]{1,0:T(8,128)(2,1)}, f32[512,1024]{1,0:T(8,128)}, f32[256,1024]{1,0:T(8,128)}, f32[256,1024]{1,0:T(8,128)}) custom-call(s32[6]{0:T(128)S(1)} %stack.63.idx_ref, bf16[1024,512]{1,0:T(8,128)(2,1)S(1)} %collective-permute-done.9.refs_0_.q_ref, f32[512,4096]{1,0:T(8,128)} %shard_map.84.own_ref, ...), custom_call_target="tpu_custom_call" | custom-call | flops 4294967296 | bytes 23068672 | tf_op jit(solution)/shard_map/pallas_call | solution.py:422
  140.9 3.2 %collective-permute-start.19 = (bf16[512,1024]{1,0:T(8,128)(2,1)}, bf16[512,1024]{1,0:T(8,128)(2,1)}, u32[]{:S(2)}, u32[]{:S(2)}) collective-permute-start(bf16[512,1024]{1,0:T(8,128)(2,1)} %get-tuple-element.87), channel_id=1, source_target_pairs={{0,48},{1,49},{2,50},{3,51},{4,52},{5,53},{6,54},{7,55},{8,56},{9,... | collective-permute-start | bytes 3145736 | tf_op jit(solution)/shard_map/ppermute | solution.py:30
  144.1 5.9 %shard_map.89 = bf16[4,1024,256]{2,1,0:T(8,128)(2,1)} custom-call(bf16[1024,512]{1,0:T(8,128)(2,1)S(1)} %copy-done.6, bf16[1024,512]{1,0:T(8,128)(2,1)S(1)} %collective-permute-done.25.refs_1_, bf16[512,512]{1,0:T(8,128)(2,1)S(1)} %collective-permute-done.23.refs_2_, bf16[512,512]{1,0:T(8,128)(2,1)S(1)} %collective-permute-done.24.refs_3_, ...), custom_call_target="tpu_custom_call" | custom-call | flops 4294967296 | bytes 10485760 | tf_op jit(solution)/shard_map/pallas_call | solution.py:366
  150.0 4.8 %all-to-all-start.3 = ((bf16[4,1024,256]{2,1,0:T(8,128)(2,1)}), bf16[4,1024,256]{2,1,0:T(8,128)(2,1)S(1)}, u32[]{:S(2)}, u32[]{:S(2)}) async-start(bf16[4,1024,256]{2,1,0:T(8,128)(2,1)} %shard_map.89), calls=%async_computation.3 | async-start | bytes 4194304 | tf_op jit(solution)/shard_map/all_to_all | solution.py:529
  154.8 2.2 %reduce_sum.24 = bf16[1024,256]{1,0:T(8,128)(2,1)S(1)} reduce(bf16[4,1024,256]{2,1,0:T(8,128)(2,1)} %all-to-all-done.2, bf16[]{:T(256)} %constant.124.clone.1), dimensions={0}, to_apply=%region_0.1 | reduce | flops 786432 | bytes 2621442 | tf_op jit(solution)/shard_map/reduce_sum | solution.py:530
  156.9 10.4 %collective-permute-done.19 = bf16[512,1024]{1,0:T(8,128)(2,1)} collective-permute-done((bf16[512,1024]{1,0:T(8,128)(2,1)}, bf16[512,1024]{1,0:T(8,128)(2,1)}, u32[]{:S(2)}, u32[]{:S(2)}) %collective-permute-start.19) | collective-permute-done | bytes 1048608 | tf_op jit(solution)/shard_map/ppermute | solution.py:30
  167.4 2.3 %add_convert_fusion.1 = bf16[256,1024]{1,0:T(8,128)(2,1)} fusion(f32[256,1024]{1,0:T(8,128)} %get-tuple-element.90, bf16[512,1024]{1,0:T(8,128)(2,1)} %collective-permute-done.19), kind=kLoop, calls=%fused_computation.5 | loop fusion | flops 786432 | bytes 2097152 | tf_op jit(solution)/shard_map/convert_element_type | solution.py:44
  169.7 3.7 %collective-permute-start.22 = (bf16[256,1024]{1,0:T(8,128)(2,1)}, bf16[256,1024]{1,0:T(8,128)(2,1)S(1)}, u32[]{:S(2)}, u32[]{:S(2)}) collective-permute-start(bf16[256,1024]{1,0:T(8,128)(2,1)} %add_convert_fusion.1), channel_id=1, source_target_pairs={{0,48},{1,49},{2,50},{3,51},{4,52},{5,53},{6,54},{7,55},{8,56},{9,... | collective-permute-start | bytes 1572872 | tf_op jit(solution)/shard_map/ppermute | solution.py:30
  180.6 3.4 %collective-permute-done.30 = bf16[1024,128]{1,0:T(8,128)(2,1)} collective-permute-done((bf16[1024,128]{1,0:T(8,128)(2,1)}, bf16[1024,128]{1,0:T(8,128)(2,1)}, u32[]{:S(2)}, u32[]{:S(2)}) %collective-permute-start.30) | collective-permute-done | bytes 262176 | tf_op jit(solution)/shard_map/ppermute | solution.py:30
  186.1 4.0 %collective-permute-done.21 = bf16[256,1024]{1,0:T(8,128)(2,1)} collective-permute-done((bf16[256,1024]{1,0:T(8,128)(2,1)}, bf16[256,1024]{1,0:T(8,128)(2,1)}, u32[]{:S(2)}, u32[]{:S(2)}) %collective-permute-start.21) | collective-permute-done | bytes 524320 | tf_op jit(solution)/shard_map/ppermute | solution.py:30
  190.1 2.5 %add_convert_fusion.2 = (bf16[256,1024]{1,0:T(8,128)(2,1)S(1)}, bf16[256,1024]{1,0:T(8,128)(2,1)S(1)}) fusion(bf16[256,1024]{1,0:T(8,128)(2,1)} %collective-permute-done.21, f32[512,1024]{1,0:T(8,128)} %get-tuple-element.86, bf16[512,1024]{1,0:T(8,128)(2,1)} %collective-permute-done.19, bf16[256,1024]{1,0:T(8,128)(2,1)S(1)} %collective-permute-done.22, ...), kind=kLoop, calls=%fused_computation.6 | loop fusion | flops 2621440 | bytes 5242880 | tf_op jit(solution)/shard_map/convert.2
  (105 shorter events, 42.8 us)
Async XLA Ops:
  2.2 6.4 %collective-permute-start = (bf16[512,512]{1,0:T(8,128)(2,1)S(1)}, bf16[512,512]{1,0:T(8,128)(2,1)S(1)}, u32[]{:S(2)}, u32[]{:S(2)}) collective-permute-start(bf16[512,512]{1,0:T(8,128)(2,1)S(1)} %get-tuple-element.50), channel_id=1, source_target_pairs={{0,1},{1,0},{2,3},{3,2},{4,5},{5,4},{6,7},{7,6},{8,9},{9,8},{10,11... | collective-permute-start | bytes 1572872 | tf_op jit(solution)/shard_map/ppermute | solution.py:30
  11.0 21.8 %collective-permute-start.5 = (bf16[64,4096]{1,0:T(8,128)(2,1)S(1)}, bf16[64,4096]{1,0:T(8,128)(2,1)S(1)}, u32[]{:S(2)}, u32[]{:S(2)}) collective-permute-start(bf16[64,4096]{1,0:T(8,128)(2,1)S(1)} %get-tuple-element.109), channel_id=1, source_target_pairs={{0,64},{1,65},{2,66},{3,67},{4,68},{5,69},{6,70},{7,71},{8,72},{9,... | collective-permute-start | bytes 1572872 | tf_op jit(solution)/shard_map/ppermute | solution.py:30
  13.0 19.8 %collective-permute-start.6 = (bf16[64,4096]{1,0:T(8,128)(2,1)S(1)}, bf16[64,4096]{1,0:T(8,128)(2,1)S(1)}, u32[]{:S(2)}, u32[]{:S(2)}) collective-permute-start(bf16[64,4096]{1,0:T(8,128)(2,1)S(1)} %get-tuple-element.108), channel_id=1, source_target_pairs={{0,66},{1,67},{2,64},{3,65},{4,70},{5,71},{6,68},{7,69},{8,74},{9,... | collective-permute-start | bytes 1572872 | tf_op jit(solution)/shard_map/ppermute | solution.py:30
  15.2 14.8 %all-to-all-start = ((bf16[4,144,512]{2,1,0:T(8,128)(2,1)}), bf16[4,144,512]{2,1,0:T(8,128)(2,1)S(1)}, u32[]{:S(2)}, u32[]{:S(2)}) async-start(bf16[4,144,512]{2,1,0:T(8,128)(2,1)} %shard_map.77), calls=%async_computation | async-start | bytes 1179648 | tf_op jit(solution)/shard_map/all_to_all | solution.py:473
  19.6 16.3 %collective-permute-start.2 = (bf16[1024,128]{1,0:T(8,128)(2,1)}, bf16[1024,128]{1,0:T(8,128)(2,1)}, u32[]{:S(2)}, u32[]{:S(2)}) collective-permute-start(bf16[1024,128]{1,0:T(8,128)(2,1)} %get-tuple-element.58), channel_id=1, source_target_pairs={{0,64},{1,65},{2,66},{3,67},{4,68},{5,69},{6,70},{7,71},{8,72},{9,... | collective-permute-start | bytes 786440 | tf_op jit(solution)/shard_map/ppermute | solution.py:30
  19.6 22.1 %collective-permute-start.3 = (bf16[1024,128]{1,0:T(8,128)(2,1)S(1)}, bf16[1024,128]{1,0:T(8,128)(2,1)}, u32[]{:S(2)}, u32[]{:S(2)}) collective-permute-start(bf16[1024,128]{1,0:T(8,128)(2,1)S(1)} %get-tuple-element.59), channel_id=1, source_target_pairs={{0,2},{1,3},{2,0},{3,1},{4,6},{5,7},{6,4},{7,5},{8,10},{9,11},{10,... | collective-permute-start | bytes 786440 | tf_op jit(solution)/shard_map/ppermute | solution.py:30
  23.0 18.7 %collective-permute-start.4 = (bf16[1024,128]{1,0:T(8,128)(2,1)S(1)}, bf16[1024,128]{1,0:T(8,128)(2,1)}, u32[]{:S(2)}, u32[]{:S(2)}) collective-permute-start(bf16[1024,128]{1,0:T(8,128)(2,1)S(1)} %get-tuple-element.60), channel_id=1, source_target_pairs={{0,66},{1,67},{2,64},{3,65},{4,70},{5,71},{6,68},{7,69},{8,74},{9,... | collective-permute-start | bytes 786440 | tf_op jit(solution)/shard_map/ppermute | solution.py:30
  32.7 9.8 %collective-permute-start.1 = (bf16[192,512]{1,0:T(8,128)(2,1)}, bf16[192,512]{1,0:T(8,128)(2,1)S(1)}, u32[]{:S(2)}, u32[]{:S(2)}) collective-permute-start(bf16[192,512]{1,0:T(8,128)(2,1)} %get-tuple-element.53.sent_ref), channel_id=1, source_target_pairs={{0,64},{1,65},{2,66},{3,67},{4,68},{5,69},{6,70},{7,71},{8,72},{9,... | collective-permute-start | bytes 589832 | tf_op jit(solution)/shard_map/ppermute | solution.py:30
  34.4 27.3 %collective-permute-start.7 = (bf16[128,4096]{1,0:T(8,128)(2,1)}, bf16[128,4096]{1,0:T(8,128)(2,1)}, u32[]{:S(2)}, u32[]{:S(2)}) collective-permute-start(bf16[128,4096]{1,0:T(8,128)(2,1)} %shard_map.82.refs_0_), channel_id=1, source_target_pairs={{0,4},{1,5},{2,6},{3,7},{4,8},{5,9},{6,10},{7,11},{8,12},{9,13},{1... | collective-permute-start | bytes 3145736 | tf_op jit(solution)/shard_map/ppermute | solution.py:30
  35.9 25.8 %collective-permute-start.8 = (bf16[128,4096]{1,0:T(8,128)(2,1)}, bf16[128,4096]{1,0:T(8,128)(2,1)S(1)}, u32[]{:S(2)}, u32[]{:S(2)}) collective-permute-start(bf16[128,4096]{1,0:T(8,128)(2,1)} %shard_map.82.refs_0_), channel_id=1, source_target_pairs={{0,12},{1,13},{2,14},{3,15},{4,0},{5,1},{6,2},{7,3},{8,4},{9,5},{1... | collective-permute-start | bytes 3145736 | tf_op jit(solution)/shard_map/ppermute | solution.py:30
  46.2 15.5 %all-to-all-start.1 = ((bf16[4,128,512]{2,1,0:T(8,128)(2,1)}), bf16[4,128,512]{2,1,0:T(8,128)(2,1)}, u32[]{:S(2)}, u32[]{:S(2)}) async-start(bf16[4,128,512]{2,1,0:T(8,128)(2,1)} %get-tuple-element.62), calls=%async_computation.1 | async-start | bytes 1048576 | tf_op jit(solution)/shard_map/all_to_all | solution.py:491
  52.8 29.4 %collective-permute-start.11 = (bf16[2,2048,128]{2,1,0:T(8,128)(2,1)S(1)}, bf16[2,2048,128]{2,1,0:T(8,128)(2,1)S(1)}, u32[]{:S(2)}, u32[]{:S(2)}) collective-permute-start(bf16[2,2048,128]{2,1,0:T(8,128)(2,1)S(1)} %pad_maximum_fusion.1.own_ref), channel_id=1, source_target_pairs={{0,16},{1,17},{2,18},{3,19},{4,20},{5,21},{6,22},{7,23},{8,24},{9,... | collective-permute-start | bytes 3145736 | tf_op jit(solution)/shard_map/ppermute | solution.py:30
  54.9 27.3 %collective-permute-start.12 = (bf16[2,2048,128]{2,1,0:T(8,128)(2,1)S(1)}, bf16[2,2048,128]{2,1,0:T(8,128)(2,1)}, u32[]{:S(2)}, u32[]{:S(2)}) collective-permute-start(bf16[2,2048,128]{2,1,0:T(8,128)(2,1)S(1)} %pad_maximum_fusion.1.own_ref), channel_id=1, source_target_pairs={{0,48},{1,49},{2,50},{3,51},{4,52},{5,53},{6,54},{7,55},{8,56},{9,... | collective-permute-start | bytes 3145736 | tf_op jit(solution)/shard_map/ppermute | solution.py:30
  61.7 39.4 %collective-permute-start.15 = (bf16[128,4096]{1,0:T(8,128)(2,1)}, bf16[128,4096]{1,0:T(8,128)(2,1)}, u32[]{:S(2)}, u32[]{:S(2)}) collective-permute-start(bf16[128,4096]{1,0:T(8,128)(2,1)} %collective-permute-done.7.refs_3_), channel_id=1, source_target_pairs={{0,4},{1,5},{2,6},{3,7},{4,8},{5,9},{6,10},{7,11},{8,12},{9,13},{1... | collective-permute-start | bytes 3145736 | tf_op jit(solution)/shard_map/ppermute | solution.py:30
  70.7 35.2 %collective-permute-start.10 = (bf16[1024,512]{1,0:T(8,128)(2,1)}, bf16[1024,512]{1,0:T(8,128)(2,1)}, u32[]{:S(2)}, u32[]{:S(2)}) collective-permute-start(bf16[1024,512]{1,0:T(8,128)(2,1)} %get-tuple-element.91.refs_0_), channel_id=1, source_target_pairs={{0,66},{1,67},{2,64},{3,65},{4,70},{5,71},{6,68},{7,69},{8,74},{9,... | collective-permute-start | bytes 3145736 | tf_op jit(solution)/shard_map/ppermute | solution.py:30
  72.9 33.0 %collective-permute-start.9 = (bf16[1024,512]{1,0:T(8,128)(2,1)}, bf16[1024,512]{1,0:T(8,128)(2,1)S(1)}, u32[]{:S(2)}, u32[]{:S(2)}) collective-permute-start(bf16[1024,512]{1,0:T(8,128)(2,1)} %get-tuple-element.91.refs_0_), channel_id=1, source_target_pairs={{0,64},{1,65},{2,66},{3,67},{4,68},{5,69},{6,70},{7,71},{8,72},{9,... | collective-permute-start | bytes 3145736 | tf_op jit(solution)/shard_map/ppermute | solution.py:30
  83.1 15.6 %collective-permute-start.13 = (bf16[1,2048,128]{2,1,0:T(8,128)(2,1)}, bf16[1,2048,128]{2,1,0:T(8,128)(2,1)}, u32[]{:S(2)}, u32[]{:S(2)}) collective-permute-start(bf16[1,2048,128]{2,1,0:T(8,128)(2,1)} %slice.50), channel_id=1, source_target_pairs={{0,16},{1,17},{2,18},{3,19},{4,20},{5,21},{6,22},{7,23},{8,24},{9,... | collective-permute-start | bytes 1572872 | tf_op jit(solution)/shard_map/ppermute | solution.py:30
  85.4 13.3 %collective-permute-start.14 = (bf16[1,2048,128]{2,1,0:T(8,128)(2,1)}, bf16[1,2048,128]{2,1,0:T(8,128)(2,1)}, u32[]{:S(2)}, u32[]{:S(2)}) collective-permute-start(bf16[1,2048,128]{2,1,0:T(8,128)(2,1)} %slice.51), channel_id=1, source_target_pairs={{0,48},{1,49},{2,50},{3,51},{4,52},{5,53},{6,54},{7,55},{8,56},{9,... | collective-permute-start | bytes 1572872 | tf_op jit(solution)/shard_map/ppermute | solution.py:30
  106.0 4.4 %collective-permute-start.17 = (bf16[1024,512]{1,0:T(8,128)(2,1)}, bf16[1024,512]{1,0:T(8,128)(2,1)S(1)}, u32[]{:S(2)}, u32[]{:S(2)}) collective-permute-start(bf16[1024,512]{1,0:T(8,128)(2,1)} %collective-permute-done.10.refs_2_), channel_id=1, source_target_pairs={{0,1},{1,0},{2,3},{3,2},{4,5},{5,4},{6,7},{7,6},{8,9},{9,8},{10,11... | collective-permute-start | bytes 3145736 | tf_op jit(solution)/shard_map/ppermute | solution.py:30
  117.5 10.2 %collective-permute-start.18 = (bf16[512,4096]{1,0:T(8,128)(2,1)}, bf16[512,4096]{1,0:T(8,128)(2,1)}, u32[]{:S(2)}, u32[]{:S(2)}) collective-permute-start(bf16[512,4096]{1,0:T(8,128)(2,1)} %shard_map.86.hx_ref), channel_id=1, source_target_pairs={{0,1},{1,0},{2,3},{3,2},{4,5},{5,4},{6,7},{7,6},{8,9},{9,8},{10,11... | collective-permute-start | bytes 12582920 | tf_op jit(solution)/shard_map/ppermute | solution.py:30
  117.6 32.4 %all-to-all-start.2 = ((bf16[4,1024,256]{2,1,0:T(8,128)(2,1)}), bf16[4,1024,256]{2,1,0:T(8,128)(2,1)}, u32[]{:S(2)}, u32[]{:S(2)}) async-start(bf16[4,1024,256]{2,1,0:T(8,128)(2,1)} %shard_map.87), calls=%async_computation.2 | async-start | bytes 4194304 | tf_op jit(solution)/shard_map/all_to_all | solution.py:519
  123.8 16.4 %collective-permute-start.23 = (bf16[512,512]{1,0:T(8,128)(2,1)S(1)}, bf16[512,512]{1,0:T(8,128)(2,1)S(1)}, u32[]{:S(2)}, u32[]{:S(2)}) collective-permute-start(bf16[512,512]{1,0:T(8,128)(2,1)S(1)} %slice.58), channel_id=1, source_target_pairs={{0,64},{1,65},{2,66},{3,67},{4,68},{5,69},{6,70},{7,71},{8,72},{9,... | collective-permute-start | bytes 1572872 | tf_op jit(solution)/shard_map/ppermute | solution.py:30
  124.8 15.4 %collective-permute-start.24 = (bf16[512,512]{1,0:T(8,128)(2,1)S(1)}, bf16[512,512]{1,0:T(8,128)(2,1)S(1)}, u32[]{:S(2)}, u32[]{:S(2)}) collective-permute-start(bf16[512,512]{1,0:T(8,128)(2,1)S(1)} %slice.59), channel_id=1, source_target_pairs={{0,66},{1,67},{2,64},{3,65},{4,70},{5,71},{6,68},{7,69},{8,74},{9,... | collective-permute-start | bytes 1572872 | tf_op jit(solution)/shard_map/ppermute | solution.py:30
  127.7 16.4 %collective-permute-start.25 = (bf16[1024,512]{1,0:T(8,128)(2,1)S(1)}, bf16[1024,512]{1,0:T(8,128)(2,1)S(1)}, u32[]{:S(2)}, u32[]{:S(2)}) collective-permute-start(bf16[1024,512]{1,0:T(8,128)(2,1)S(1)} %copy-done.6), channel_id=1, source_target_pairs={{0,1},{1,0},{2,3},{3,2},{4,5},{5,4},{6,7},{7,6},{8,9},{9,8},{10,11... | collective-permute-start | bytes 3145736 | tf_op jit(solution)/shard_map/ppermute | solution.py:30
  140.9 26.5 %collective-permute-start.19 = (bf16[512,1024]{1,0:T(8,128)(2,1)}, bf16[512,1024]{1,0:T(8,128)(2,1)}, u32[]{:S(2)}, u32[]{:S(2)}) collective-permute-start(bf16[512,1024]{1,0:T(8,128)(2,1)} %get-tuple-element.87), channel_id=1, source_target_pairs={{0,48},{1,49},{2,50},{3,51},{4,52},{5,53},{6,54},{7,55},{8,56},{9,... | collective-permute-start | bytes 3145736 | tf_op jit(solution)/shard_map/ppermute | solution.py:30
  144.1 29.3 %collective-permute-start.20 = (bf16[512,1024]{1,0:T(8,128)(2,1)}, bf16[512,1024]{1,0:T(8,128)(2,1)}, u32[]{:S(2)}, u32[]{:S(2)}) collective-permute-start(bf16[512,1024]{1,0:T(8,128)(2,1)} %get-tuple-element.89), channel_id=1, source_target_pairs={{0,16},{1,17},{2,18},{3,19},{4,20},{5,21},{6,22},{7,23},{8,24},{9,... | collective-permute-start | bytes 3145736 | tf_op jit(solution)/shard_map/ppermute | solution.py:30
  150.0 30.0 %all-to-all-start.3 = ((bf16[4,1024,256]{2,1,0:T(8,128)(2,1)}), bf16[4,1024,256]{2,1,0:T(8,128)(2,1)S(1)}, u32[]{:S(2)}, u32[]{:S(2)}) async-start(bf16[4,1024,256]{2,1,0:T(8,128)(2,1)} %shard_map.89), calls=%async_computation.3 | async-start | bytes 4194304 | tf_op jit(solution)/shard_map/all_to_all | solution.py:529
  169.7 16.4 %collective-permute-start.22 = (bf16[256,1024]{1,0:T(8,128)(2,1)}, bf16[256,1024]{1,0:T(8,128)(2,1)S(1)}, u32[]{:S(2)}, u32[]{:S(2)}) collective-permute-start(bf16[256,1024]{1,0:T(8,128)(2,1)} %add_convert_fusion.1), channel_id=1, source_target_pairs={{0,48},{1,49},{2,50},{3,51},{4,52},{5,53},{6,54},{7,55},{8,56},{9,... | collective-permute-start | bytes 1572872 | tf_op jit(solution)/shard_map/ppermute | solution.py:30
  175.4 14.7 %collective-permute-start.21 = (bf16[256,1024]{1,0:T(8,128)(2,1)}, bf16[256,1024]{1,0:T(8,128)(2,1)}, u32[]{:S(2)}, u32[]{:S(2)}) collective-permute-start(bf16[256,1024]{1,0:T(8,128)(2,1)} %add_convert_fusion.3), channel_id=1, source_target_pairs={{0,16},{1,17},{2,18},{3,19},{4,20},{5,21},{6,22},{7,23},{8,24},{9,... | collective-permute-start | bytes 1572872 | tf_op jit(solution)/shard_map/ppermute | solution.py:30
  176.1 7.9 %collective-permute-start.30 = (bf16[1024,128]{1,0:T(8,128)(2,1)}, bf16[1024,128]{1,0:T(8,128)(2,1)}, u32[]{:S(2)}, u32[]{:S(2)}) collective-permute-start(bf16[1024,128]{1,0:T(8,128)(2,1)} %get-tuple-element.115), channel_id=1, source_target_pairs={{0,64},{1,65},{2,66},{3,67},{4,68},{5,69},{6,70},{7,71},{8,72},{9,... | collective-permute-start | bytes 786440 | tf_op jit(solution)/shard_map/ppermute | solution.py:30
  176.2 17.8 %collective-permute-start.28 = (bf16[1024,128]{1,0:T(8,128)(2,1)S(1)}, bf16[1024,128]{1,0:T(8,128)(2,1)}, u32[]{:S(2)}, u32[]{:S(2)}) collective-permute-start(bf16[1024,128]{1,0:T(8,128)(2,1)S(1)} %get-tuple-element.114), channel_id=1, source_target_pairs={{0,66},{1,67},{2,64},{3,65},{4,70},{5,71},{6,68},{7,69},{8,74},{9,... | collective-permute-start | bytes 786440 | tf_op jit(solution)/shard_map/ppermute | solution.py:30
  185.0 9.0 %collective-permute-start.29 = (bf16[1024,128]{1,0:T(8,128)(2,1)S(1)}, bf16[1024,128]{1,0:T(8,128)(2,1)S(1)}, u32[]{:S(2)}, u32[]{:S(2)}) collective-permute-start(bf16[1024,128]{1,0:T(8,128)(2,1)S(1)} %get-tuple-element.116), channel_id=1, source_target_pairs={{0,2},{1,3},{2,0},{3,1},{4,6},{5,7},{6,4},{7,5},{8,10},{9,11},{10,... | collective-permute-start | bytes 786440 | tf_op jit(solution)/shard_map/ppermute | solution.py:30
  (15 other events, 113.0 us)
